TPU v7x, 32 devices: a whole 2x2x4 slice. The times are simulated.
32 devices in a mesh: dp: 16 (over z, x, core), ctx: 2 (over y).
Axes of the slice: x: 2, y: 2, z: 4, core: 2. Of those that a mesh axis runs over, the one named last changes fastest.
Arguments:
- projections: bfloat16 [8192, 6144], P(('dp', 'ctx')), may hold values from -6 to 6
- block_source: int32 [16, 2, 2], P('dp', 'ctx'), may hold values from 0 to 63, as said below
- clip_ids: int32 [16, 4], P('dp'), may hold values from 0 to 2, as said below
- out_weight: bfloat16 [2048, 1536], P('dp'), may hold values from -1 to 1
Outputs:
- mixed: bfloat16 [8192, 1536], P(('dp', 'ctx'))
Inputs may be any that keep to these rules, and one draw needn't show every extreme that they name: `block_source`: arrival block a lies on the device numbered a // 2 in dp-major order (dp index a // (2 * 2), ctx index (a // 2) % 2). The block that fills pack block (o, j, l) lies on the device with the same ctx index j and dp index o or o XOR 1. Every arrival block fills exactly one pack block. `clip_ids`: in each pack the clip numbers start at 0, never fall and rise by at most one from block to block; every clip spans 1 to 2 blocks, and in every pack some clip spans exactly 2 blocks.
All inputs are finite; a program needn't handle non-finite values.
Results may differ from a plain program's by a relative error of at most 0.0057.
Values may be sent and summed in bfloat16 or wider, within the bound.
No kernel may reach another device: no remote copies, remote signals or barrier semaphores. Data moves between devices by JAX's collectives and lax.ppermute only.
A program may use at most 64 MiB of HBM per device.

v0:
```python
import functools
import math

import jax
import jax.numpy as jnp
from jax import lax
from jax.experimental import pallas as pl
from jax.experimental.pallas import tpu as pltpu
from jax.sharding import PartitionSpec as P

HEAD = 128


big_negative = -1e30
MIB = 1 << 20


def partner(value, axis, bit):
    mask = 2**bit
    pairs = [(source, source ^ mask) for source in range(lax.axis_size(axis))]
    return lax.ppermute(value, axis, pairs)


def soft_weights(scores, allowed):
    masked = jnp.where(allowed, scores, big_negative)
    row_max = jnp.max(masked, axis=-1, keepdims=True)
    exponent = jnp.exp(masked - row_max)
    return (exponent / jnp.sum(exponent, axis=-1, keepdims=True)).astype(jnp.bfloat16)


def attend_dense(queries, key_rows, value_rows, token_clip, scaling):
    token_count, head_count, head_size = queries.shape
    step_size = min(token_count, 512)
    step_count = token_count // step_size
    query_steps = queries.reshape(step_count, step_size, head_count, head_size)
    clip_steps = token_clip.reshape(step_count, step_size)

    def one_step(arguments):
        query_block, clip_block = arguments
        scores = (
            jnp.einsum("qhe,khe->hqk", query_block, key_rows, preferred_element_type=jnp.float32)
            * scaling
        )
        allowed = (clip_block[:, None] == token_clip[None, :])[None]
        weights = soft_weights(scores, allowed)
        return jnp.einsum(
            "hqk,khe->qhe", weights, value_rows, preferred_element_type=jnp.float32
        ).astype(jnp.bfloat16)

    outputs = lax.map(one_step, (query_steps, clip_steps))
    return outputs.reshape(token_count, head_count, head_size)


def body_general(projections, block_source, clip_ids, out_weight):
    ctx_count = lax.axis_size("ctx")
    local_rows, row_width = projections.shape
    local_blocks = block_source.shape[2]
    block_rows = local_rows // local_blocks
    own_blocks = projections.reshape(local_blocks, block_rows, row_width)
    partner_blocks = partner(own_blocks, "dp", 0)
    source_ids = block_source.reshape(local_blocks)
    from_partner = source_ids // (local_blocks * ctx_count) != lax.axis_index("dp")
    chosen_slot = source_ids % local_blocks + local_blocks * from_partner.astype(jnp.int32)
    candidates = jnp.concatenate([own_blocks, partner_blocks], axis=0)
    packed = jnp.take(candidates, chosen_slot, axis=0)
    local_heads = row_width // (3 * HEAD) // ctx_count
    grouped = packed.reshape(local_rows, ctx_count, local_heads, 3 * HEAD)
    block_clip = clip_ids.reshape(-1)
    token_clip = jnp.repeat(block_clip, block_rows)
    scaling = 1.0 / math.sqrt(HEAD)
    regrouped = lax.all_to_all(grouped, "ctx", split_axis=1, concat_axis=0, tiled=True)
    token_count = regrouped.shape[0]
    item_count = regrouped.shape[2]
    features = regrouped.reshape(token_count, item_count, 3 * HEAD)
    queries = features[:, :, :HEAD]
    key_rows = features[:, :, HEAD : 2 * HEAD]
    value_rows = features[:, :, 2 * HEAD :]
    attended = attend_dense(queries, key_rows, value_rows, token_clip, scaling)
    merged = attended.reshape(local_rows * ctx_count, local_heads * HEAD)
    attention_rows = lax.all_to_all(merged, "ctx", split_axis=0, concat_axis=1, tiled=True)
    result = jnp.dot(
        attention_rows,
        lax.all_gather(out_weight, "dp", axis=0, tiled=True),
        preferred_element_type=jnp.float32,
    )
    return result.astype(jnp.bfloat16)


EDGE_AWAY, EDGE_SLOT, INNER_AWAY, INNER_SLOT, INNER_JOINS, EDGE_JOINS, CROSSES = range(7)


def stage_kernel(sources, clips, own_ref, out_ref, facts_ref, source_ref, clip_ref, few_sems, sems):
    parts = sems.shape[1]
    slots = own_ref.shape[0]
    rows = own_ref.shape[1] // parts
    copies = []
    for block in range(slots):
        for part in range(parts):
            here = (block, pl.ds(part * rows, rows))
            copies.append(
                pltpu.make_async_copy(own_ref.at[here], out_ref.at[here], sems.at[block, part])
            )
    few = [
        pltpu.make_async_copy(sources, source_ref, few_sems.at[0]),
        pltpu.make_async_copy(clips, clip_ref, few_sems.at[1]),
    ]
    for copy in few + copies:
        copy.start()
    for copy in few:
        copy.wait()
    ctx, dp = lax.axis_index("ctx"), lax.axis_index("dp")
    facts = {}
    for block, away, at in ((1 - ctx, EDGE_AWAY, EDGE_SLOT), (ctx, INNER_AWAY, INNER_SLOT)):
        source = source_ref[0, 0, block]
        facts[away] = (source // (2 * slots) != dp).astype(jnp.int32)
        facts[at] = lax.rem(source, slots)
    edge_clip = clip_ref[0, 1 + ctx]
    crosses = edge_clip == clip_ref[0, 2 - ctx]
    facts[CROSSES] = crosses.astype(jnp.int32)
    facts[EDGE_JOINS] = jnp.logical_or(crosses, edge_clip == clip_ref[0, 3 * ctx]).astype(jnp.int32)
    facts[INNER_JOINS] = (clip_ref[0, 2 * ctx] == clip_ref[0, 2 * ctx + 1]).astype(jnp.int32)
    for which, fact in facts.items():
        facts_ref[which] = jnp.full(facts_ref.shape[1:], fact, jnp.int32)
    for copy in copies:
        copy.wait()


def fact(facts_ref, which):
    return jnp.max(facts_ref[which])


def pack_first_kernel(facts_ref, own_ref, partner_ref, halo_ref):
    away, slot = fact(facts_ref, EDGE_AWAY) > 0, fact(facts_ref, EDGE_SLOT)

    def fill(ref):
        for head in range(halo_ref.shape[1] // (2 * HEAD)):
            columns = slice(head * 3 * HEAD + HEAD, (head + 1) * 3 * HEAD)
            halo_ref[:, head * 2 * HEAD : (head + 1) * 2 * HEAD] = ref[slot, :, columns]

    @pl.when(away)
    def _():
        fill(partner_ref)

    @pl.when(jnp.logical_not(away))
    def _():
        fill(own_ref)


def pack_kernel(facts_ref, own_ref, partner_ref, rows_ref, halo_ref, sems):
    for which, away, at in ((1, EDGE_AWAY, EDGE_SLOT), (0, INNER_AWAY, INNER_SLOT)):
        away, slot = fact(facts_ref, away) > 0, fact(facts_ref, at)

        @pl.when(jnp.logical_not(away))
        def _():
            pltpu.make_async_copy(own_ref.at[slot], rows_ref.at[which], sems.at[which]).start()

        @pl.when(away)
        def _():
            pltpu.make_async_copy(partner_ref.at[slot], rows_ref.at[which], sems.at[which]).start()

    pltpu.make_async_copy(own_ref.at[0], rows_ref.at[1], sems.at[1]).wait()
    heads = halo_ref.shape[1] // (2 * HEAD)
    skipped = rows_ref.shape[2] // (3 * HEAD) - heads
    for head in range(heads):
        first = (skipped + head) * 3 * HEAD + HEAD
        halo_ref[:, head * 2 * HEAD : (head + 1) * 2 * HEAD] = rows_ref[
            1, :, first : first + 2 * HEAD
        ]
    pltpu.make_async_copy(own_ref.at[0], rows_ref.at[0], sems.at[0]).wait()


def attend(heads, load_queries, load_own, load_more, allowed, out_ref, other_ref):
    scaling = math.log2(math.e) / math.sqrt(HEAD)
    contract_last = (((1,), (1,)), ((), ()))
    ones = jnp.ones((2 * out_ref.shape[0], HEAD), jnp.bfloat16)
    odd_core = lax.rem(lax.axis_index("dp"), 2) == 1
    for start in range(0, heads, 4):
        group = min(4, heads - start)
        scores = []
        for head in range(start, start + group):
            queries = load_queries(head)
            pair = []
            for loader in (load_own, load_more):
                pair.append(
                    lax.dot_general(
                        queries, loader(head, 0), contract_last, preferred_element_type=jnp.float32
                    )
                    * scaling
                )
            scores.append(pair)
        weights = []
        for own, more in scores:
            more = jnp.where(allowed, more, big_negative)
            row_max = jnp.max(jnp.maximum(own, more), axis=-1, keepdims=True)
            weights.append(
                jnp.concatenate(
                    [
                        jnp.exp2(own - row_max).astype(jnp.bfloat16),
                        jnp.exp2(more - row_max).astype(jnp.bfloat16),
                    ],
                    axis=1,
                )
            )
        outs = []
        for head in range(start, start + group):
            values = jnp.concatenate([load_own(head, 1), load_more(head, 1)], axis=0)
            sums = jnp.dot(
                weights[head - start],
                jnp.concatenate([values, ones], axis=1),
                preferred_element_type=jnp.float32,
            )
            outs.append(sums[:, :HEAD] / sums[:, HEAD:])
            out_ref[:, head * HEAD : (head + 1) * HEAD] = outs[-1].astype(jnp.bfloat16)
        for pair in range(group // 2):
            at = (start // 2 + pair) * HEAD
            other = jnp.where(odd_core, outs[2 * pair], outs[2 * pair + 1])
            other_ref[:, at : at + HEAD] = other.astype(jnp.bfloat16)


def inner_kernel(facts_ref, rows_ref, out_ref, other_ref):
    allowed = fact(facts_ref, INNER_JOINS) > 0

    def loader(block):
        def get(head, which):
            first = (head * 3 + 1 + which) * HEAD
            return rows_ref[block, :, first : first + HEAD]

        return get

    attend(
        out_ref.shape[1] // HEAD,
        lambda head: loader(0)(head, -1),
        loader(0),
        loader(1),
        allowed,
        out_ref,
        other_ref,
    )


def edge_kernel(first_head, facts_ref, rows_ref, halo_ref, out_ref, other_ref):
    crosses, allowed = fact(facts_ref, CROSSES) > 0, fact(facts_ref, EDGE_JOINS) > 0

    def load_own(head, which):
        first = ((first_head + head) * 3 + 1 + which) * HEAD
        return rows_ref[1, :, first : first + HEAD]

    def load_more(head, which):
        first = ((first_head + head) * 3 + 1 + which) * HEAD
        at = (2 * head + which) * HEAD
        return jnp.where(crosses, halo_ref[:, at : at + HEAD], rows_ref[0, :, first : first + HEAD])

    attend(
        out_ref.shape[1] // HEAD,
        lambda head: load_own(head, -1),
        load_own,
        load_more,
        allowed,
        out_ref,
        other_ref,
    )


def ring_order(lines):
    return list(range(0, lines, 2)) + list(range(1, lines, 2))[::-1]


def shard_places(origins, depth):
    index = lax.axis_index("dp")
    core, side, line = lax.rem(index, 2), lax.rem(index // 2, 2), index // 4
    places = ring_order(lax.axis_size("dp") // 4)
    found = []
    for steps, other_side in origins:
        from_line = line
        for at, place in enumerate(places):
            from_line = jnp.where(line == place, places[at - steps], from_line)
        pair = from_line * 2 + (1 - side if other_side else side)
        here = pl.ds(pl.multiple_of((pair * 2 + core) * depth, depth), depth)
        there = pl.ds(pl.multiple_of(pair * depth, depth), depth)
        found.append((here, there))
    return found


def inner_project_kernel(origins, early, inner_ref, their_ref, *rest):
    shard_refs, (total_ref, left_ref, features) = rest[:-3], rest[-3:]
    block = inner_ref.shape[0]
    depth = left_ref.shape[1] // (len(origins) - early)
    for number, (here, there) in enumerate(shard_places(origins, depth)):
        ref, at = (features, number) if number < early else (left_ref, number - early)
        ref[:block, at * depth : (at + 1) * depth] = inner_ref[:, here]
        ref[block:, at * depth : (at + 1) * depth] = their_ref[:, there]
    tile = 2 * HEAD
    for first in range(0, total_ref.shape[1], tile):
        columns = slice(first, first + tile)
        weight = jnp.concatenate([ref[:, columns] for ref in shard_refs], axis=0)
        total_ref[:, columns] = jnp.dot(
            features[...], weight, preferred_element_type=jnp.float32
        )


def add_products_kernel(left_ref, inner_total_ref, *rest):
    shard_refs, total_ref = rest[:-1], rest[-1]
    depths = sum(ref.shape[0] for ref in shard_refs)
    tile = 2 * HEAD
    for first in range(0, total_ref.shape[1], tile):
        columns = slice(first, first + tile)
        weight = jnp.concatenate([ref[:, columns] for ref in shard_refs], axis=0)
        total_ref[:, columns] = inner_total_ref[:, columns] + jnp.dot(
            left_ref[:, :depths], weight, preferred_element_type=jnp.float32
        )


def edge_project_kernel(origins, parts, *refs):
    edge_refs, their_refs, shard_refs = refs[:parts], refs[parts : 2 * parts], refs[2 * parts : -5]
    total_ref, left_ref, edge_rows, their_rows, features = refs[-5:]
    for refs, held in ((edge_refs, edge_rows), (their_refs, their_rows)):
        first = 0
        for ref in refs:
            held[:, first : first + ref.shape[1]] = ref[...]
            first += ref.shape[1]
    block, depth = left_ref.shape[0] // 2, left_ref.shape[1]
    for number, (here, there) in enumerate(shard_places(origins, depth)):
        last = number == len(origins) - 1
        ref, at = (left_ref, 0) if last else (features, number * depth)
        ref[:block, at : at + depth] = edge_rows[:, here]
        ref[block:, at : at + depth] = their_rows[:, there]
    tile = 2 * HEAD
    for first in range(0, total_ref.shape[1], tile):
        columns = slice(first, first + tile)
        weight = jnp.concatenate([ref[:, columns] for ref in shard_refs], axis=0)
        total_ref[:, columns] = jnp.dot(
            features[...], weight, preferred_element_type=jnp.float32
        )


def last_project_kernel(first, edge_ref, left_ref, inner_total_ref, edge_total_ref, *rest):
    shard_refs, (own_total_ref, their_total_ref) = rest[:-2], rest[-2:]
    block = own_total_ref.shape[0] // 2
    depth = sum(ref.shape[0] for ref in shard_refs)
    features = jnp.concatenate([left_ref[:, -depth:], edge_ref[...]], axis=0)
    tile = 2 * HEAD
    for at in range(0, own_total_ref.shape[1], tile):
        here = slice(at, at + tile)
        columns = slice(first + at, first + at + tile)
        weight = jnp.concatenate([ref[:, columns] for ref in shard_refs], axis=0)
        total = jnp.dot(features, weight, preferred_element_type=jnp.float32)
        inner = inner_total_ref[:, columns] + total[: 2 * block]
        edge = edge_total_ref[:, columns] + total[2 * block :]
        own_total_ref[:block, here] = inner[:block]
        own_total_ref[block:, here] = edge[:block]
        their_total_ref[:block, here] = inner[block:].astype(jnp.bfloat16)
        their_total_ref[block:, here] = edge[block:].astype(jnp.bfloat16)


def add_kernel(total_ref, more_ref, out_ref):
    out_ref[...] = (total_ref[...] + more_ref[...]).astype(jnp.bfloat16)


def finish_kernel(total_ref, more_ref, ready_ref, out_ref, held, sems):
    block = out_ref.shape[0] // 2
    ctx = lax.axis_index("ctx")
    ready = ready_ref.shape[1]
    blocks = [(slice(0, block), ctx), (slice(block, 2 * block), 1 - ctx)]

    def copy(source_ref, which, first, sem):
        rows, place = blocks[which]
        there = pl.ds(pl.multiple_of(place * block, block), block)
        columns = pl.ds(first, source_ref.shape[1])
        return pltpu.make_async_copy(source_ref.at[rows], out_ref.at[there, columns], sem)

    copies = [copy(ready_ref, which, 0, sems.at[which]) for which in range(2)]
    for one in copies:
        one.start()
    for which, (rows, _) in enumerate(blocks):
        held[rows] = (total_ref[rows] + more_ref[rows]).astype(jnp.bfloat16)
        copies.append(copy(held, which, ready, sems.at[2 + which]))
        copies[-1].start()
    for one in copies:
        one.wait()


SMEM = functools.partial(pl.BlockSpec, memory_space=pltpu.SMEM)
VMEM = functools.partial(pl.BlockSpec, memory_space=pltpu.VMEM)
HBM = functools.partial(pl.BlockSpec, memory_space=pltpu.HBM)


def after(value, *others):
    return lax.optimization_barrier((value, *others))[0]


def body_edge(projections, block_source, clip_ids, out_weight):
    local_rows, row_width = projections.shape
    block_rows = local_rows // 2
    heads = row_width // (3 * HEAD)
    features = heads * HEAD
    depth, width = out_weight.shape
    count = lax.axis_size("dp")
    bf16 = jnp.bfloat16

    def call(kernel, name, shape, in_specs, dtypes=None, scratch=(), out_spec=VMEM()):
        many = isinstance(shape, list)
        shapes = shape if many else [shape]
        dtypes = dtypes or [bf16] * len(shapes)
        shapes = [jax.ShapeDtypeStruct(*one) for one in zip(shapes, dtypes, strict=True)]
        return pl.pallas_call(
            kernel,
            out_shape=shapes if many else shapes[0],
            in_specs=in_specs,
            out_specs=[out_spec] * len(shapes) if many else out_spec,
            scratch_shapes=scratch,
            cost_estimate=pl.CostEstimate(flops=0, bytes_accessed=0, transcendentals=0),
            compiler_params=pltpu.CompilerParams(vmem_limit_bytes=8 * MIB),
            name=name,
        )

    def around(value, step):
        places = ring_order(count // 4)
        moves = [(here, places[(at + step) % len(places)]) for at, here in enumerate(places)]
        return lax.ppermute(
            value, "dp", [(4 * here + rest, 4 * there + rest) for here, there in moves for rest in range(4)]
        )

    def to_side(value):
        return partner(value, "dp", 1)

    def to_core(value):
        return partner(value, "dp", 0)

    def in_hbm(value):
        return pltpu.with_memory_space_constraint(value, pltpu.HBM)

    own = in_hbm(projections.reshape(2, block_rows, row_width))
    shards = {(0, False): [out_weight]}
    from_partner = pltpu.with_memory_space_constraint(to_core(own), pltpu.VMEM)
    ahead = around(out_weight, 1)
    across = to_side(out_weight)
    staged, facts = call(
        stage_kernel,
        "stage",
        [own.shape, (7, 8, 128)],
        [HBM()] * 3,
        dtypes=[bf16, jnp.int32],
        scratch=[
            pltpu.SMEM(block_source.shape, jnp.int32),
            pltpu.SMEM(clip_ids.shape, jnp.int32),
            pltpu.SemaphoreType.DMA((2,)),
            pltpu.SemaphoreType.DMA((2, 4)),
        ],
    )(in_hbm(block_source), in_hbm(clip_ids), own)
    part_heads = [heads * 8 // 16, heads * 8 // 16]
    packed_first = call(
        pack_first_kernel,
        "pack_first",
        (block_rows, 2 * HEAD * part_heads[0]),
        [VMEM()] * 3,
    )(facts, staged, from_partner)
    rows, packed_last = call(
        pack_kernel,
        "pack",
        [(2, block_rows, row_width), (block_rows, 2 * HEAD * part_heads[1])],
        [VMEM()] * 3,
        scratch=[pltpu.SemaphoreType.DMA((2,))],
    )(facts, staged, after(from_partner, packed_first))
    packed = [packed_first, packed_last]
    halos = [lax.ppermute(part, "ctx", [(0, 1), (1, 0)]) for part in packed]

    def edge_rows(part, *before):
        some = part_heads[part]
        return call(
            functools.partial(edge_kernel, sum(part_heads[:part])),
            "edge_rows",
            [(block_rows, some * HEAD), (block_rows, some // 2 * HEAD)],
            [VMEM()] * 3,
        )(after(facts, *before), rows, halos[part])

    back = around(after(out_weight, staged), -1)
    ahead = after(ahead, *packed)
    shards[1, False], shards[0, True] = [ahead], [across]
    second = around(after(ahead, across), 1)
    across = to_side(ahead)
    inner, inner_other = call(
        inner_kernel,
        "inner_rows",
        [(block_rows, features), (block_rows, features // 2)],
        [VMEM()] * 2,
    )(after(facts, ahead), rows)
    theirs = [to_core(inner_other)]

    back = after(back, inner)
    shards[3, False] = [back]
    back_across = to_side(back)
    shards[1, True] = [across]
    early = list(shards)
    origins = [*early, (2, False), (3, True), (2, True)]
    inner_total, inner_left = call(
        functools.partial(inner_project_kernel, origins, len(early)),
        "inner_project",
        [(local_rows, width), (local_rows, (len(origins) - len(early)) * depth)],
        [VMEM()] * (2 + len(early)),
        dtypes=[jnp.float32, bf16],
        scratch=[pltpu.VMEM((local_rows, len(early) * depth), bf16)],
    )(inner, *theirs, *[shards[origin][0] for origin in early])
    edges, edge_others = zip(*[edge_rows(part) for part in range(len(part_heads))], strict=True)
    second = after(second, inner_total, edges[0])
    cut = depth // 8 * 5
    shards[2, False] = [second]
    shards[3, True] = [back_across]
    shards[2, True] = [around(after(across, edges[0])[:cut], 1), to_side(second[cut:])]
    theirs = [to_core(part) for part in edge_others]

    more = [shards[origin][0] for origin in origins[len(early) : -1]]
    inner_total = call(
        add_products_kernel,
        "add_products",
        inner_total.shape,
        [VMEM()] * (2 + len(more)),
        dtypes=[jnp.float32],
    )(inner_left, inner_total, *more)
    theirs[-1] = after(theirs[-1], inner_total)
    pieces = [piece for origin in origins[:-1] for piece in shards[origin]]
    edge_total, edge_left = call(
        functools.partial(edge_project_kernel, origins, len(edges)),
        "edge_project",
        [(local_rows, width), (local_rows, depth)],
        [VMEM()] * (len(edges) + len(theirs) + len(pieces)),
        dtypes=[jnp.float32, bf16],
        scratch=[
            pltpu.VMEM((block_rows, features), bf16),
            pltpu.VMEM((block_rows, features // 2), bf16),
            pltpu.VMEM((local_rows, (len(origins) - 1) * depth), bf16),
        ],
    )(*edges, *theirs, *pieces)
    sums = []
    first = 0
    for columns in (width // 3 * 2, width // 3):
        own_total, their_total = call(
            functools.partial(last_project_kernel, first),
            "last_project",
            [(local_rows, columns)] * 2,
            [VMEM()] * (4 + len(shards[origins[-1]])),
            dtypes=[jnp.float32, bf16],
        )(edge_left, inner_left, inner_total, edge_total, *shards[origins[-1]])
        sums.append((own_total, to_core(their_total)))
        first += columns
    ready = call(add_kernel, "add", sums[0][0].shape, [VMEM()] * 2)(*sums[0])
    return call(
        finish_kernel,
        "finish",
        (local_rows, width),
        [VMEM()] * 3,
        scratch=[pltpu.VMEM(sums[1][0].shape, bf16), pltpu.SemaphoreType.DMA((4,))],
        out_spec=HBM(),
    )(*sums[1], ready)


def body(projections, block_source, clip_ids, out_weight):
    heads = projections.shape[1] // (3 * HEAD)
    two_and_two = lax.axis_size("ctx") == 2 and block_source.shape[2] == 2
    whole_tiles = out_weight.shape[0] % HEAD == 0 and heads % 16 == 0
    if two_and_two and whole_tiles and lax.axis_size("dp") == 16:
        return body_edge(projections, block_source, clip_ids, out_weight)
    return body_general(projections, block_source, clip_ids, out_weight)


def solution(mesh):
    return jax.shard_map(
        body,
        mesh=mesh,
        in_specs=(P(("dp", "ctx"), None), P("dp", "ctx", None), P("dp", None), P("dp", None)),
        out_specs=P(("dp", "ctx"), None),
        check_vma=False,
    )
```

profile of v0, /device:TPU:0, one launch (start us, length us, event | category | flops | bytes accessed | tf_op | source)
XLA Modules:
  0.0 42.3 jit_solution(2488028752259141088)
XLA Ops:
  0.0 0.5 %collective-permute-start = (bf16[2,128,6144]{2,1,0:T(8,128)(2,1)}, bf16[2,128,6144]{2,1,0:T(8,128)(2,1)S(1)}, u32[]{:S(2)}, u32[]{:S(2)}) collective-permute-start(bf16[2,128,6144]{2,1,0:T(8,128)(2,1)} %bitcast.1), channel_id=1, source_target_pairs={{0,2},{2,0},{4,6},{6,4},{8,10},{10,8},{12,14},{14,12},{16,18},{18,... | collective-permute-start | bytes 9437192 | tf_op jit(solution)/shard_map/ppermute | solution.py:21
  0.5 3.6 %collective-permute-start.5 = (bf16[128,1536]{1,0:T(8,128)(2,1)}, bf16[128,1536]{1,0:T(8,128)(2,1)S(1)}, u32[]{:S(2)}, u32[]{:S(2)}) collective-permute-start(bf16[128,1536]{1,0:T(8,128)(2,1)} %refs_4_.1), channel_id=1, source_target_pairs={{0,16},{2,18},{4,20},{6,22},{16,24},{18,26},{20,28},{22,30},{24,8}... | collective-permute-start | bytes 1179656 | tf_op jit(solution)/shard_map/ppermute | solution.py:419
  4.0 1.5 %collective-permute-start.7 = (bf16[128,1536]{1,0:T(8,128)(2,1)}, bf16[128,1536]{1,0:T(8,128)(2,1)S(1)}, u32[]{:S(2)}, u32[]{:S(2)}) collective-permute-start(bf16[128,1536]{1,0:T(8,128)(2,1)} %refs_4_.1), channel_id=1, source_target_pairs={{0,4},{2,6},{4,0},{6,2},{8,12},{10,14},{12,8},{14,10},{16,20},{18,... | collective-permute-start | bytes 1179656 | tf_op jit(solution)/shard_map/ppermute | solution.py:21
  5.5 1.9 %stage.1 = (bf16[2,128,6144]{2,1,0:T(8,128)(2,1)S(1)}, s32[7,8,128]{2,1,0:T(8,128)S(1)}) custom-call(s32[1,1,2]{2,1,0:T(1,128)} %sources.1, s32[1,4]{1,0:T(1,128)} %clips.1, bf16[2,128,6144]{2,1,0:T(8,128)(2,1)} %bitcast.2), custom_call_target="tpu_custom_call" | custom-call | tf_op jit(solution)/shard_map/stage/pallas_call | solution.py:437
  7.5 0.0 collective-permute-done.partner_ref
  7.5 0.0 copy-start
  7.5 0.2 pack_first.1
  7.7 1.6 %collective-permute-start.1 = (bf16[128,2048]{1,0:T(8,128)(2,1)S(1)}, bf16[128,2048]{1,0:T(8,128)(2,1)S(1)}, u32[]{:S(2)}, u32[]{:S(2)}) collective-permute-start(bf16[128,2048]{1,0:T(8,128)(2,1)S(1)} %pack_first.1), channel_id=1, source_target_pairs={{0,1},{1,0},{2,3},{3,2},{4,5},{5,4},{6,7},{7,6},{8,9},{9,8},{10,11... | collective-permute-start | bytes 1572872 | tf_op jit(solution)/shard_map/ppermute | solution.py:465
  9.3 0.0 copy-done
  9.3 1.4 %collective-permute-start.8 = (bf16[128,1536]{1,0:T(8,128)(2,1)S(1)}, bf16[128,1536]{1,0:T(8,128)(2,1)S(1)}, u32[]{:S(2)}, u32[]{:S(2)}) collective-permute-start(bf16[128,1536]{1,0:T(8,128)(2,1)S(1)} %copy-done), channel_id=1, source_target_pairs={{0,8},{2,10},{4,12},{6,14},{16,0},{18,2},{20,4},{22,6},{24,16},{26... | collective-permute-start | bytes 1179656 | tf_op jit(solution)/shard_map/ppermute | solution.py:419
  10.7 0.7 %pack.1 = (bf16[2,128,6144]{2,1,0:T(8,128)(2,1)S(1)}, bf16[128,2048]{1,0:T(8,128)(2,1)S(1)}) custom-call(s32[7,8,128]{2,1,0:T(8,128)S(1)} %get-tuple-element.42.facts_ref, bf16[2,128,6144]{2,1,0:T(8,128)(2,1)S(1)} %get-tuple-element.33.own_ref, bf16[2,128,6144]{2,1,0:T(8,128)(2,1)S(1)} %collective-permute-done.partner_ref), custom_call_target="tpu_custom_call" | custom-call | tf_op jit(solution)/shard_map/pack/pallas_call | solution.py:457
  11.4 0.7 %collective-permute-start.2 = (bf16[128,2048]{1,0:T(8,128)(2,1)S(1)}, bf16[128,2048]{1,0:T(8,128)(2,1)S(1)}, u32[]{:S(2)}, u32[]{:S(2)}) collective-permute-start(bf16[128,2048]{1,0:T(8,128)(2,1)S(1)} %get-tuple-element.37), channel_id=1, source_target_pairs={{0,1},{1,0},{2,3},{3,2},{4,5},{5,4},{6,7},{7,6},{8,9},{9,8},{10,11... | collective-permute-start | bytes 1572872 | tf_op jit(solution)/shard_map/ppermute | solution.py:465
  12.2 1.6 %collective-permute-done.5.rest_1_.refs_5_ = bf16[128,1536]{1,0:T(8,128)(2,1)S(1)} collective-permute-done((bf16[128,1536]{1,0:T(8,128)(2,1)}, bf16[128,1536]{1,0:T(8,128)(2,1)S(1)}, u32[]{:S(2)}, u32[]{:S(2)}) %collective-permute-start.5) | collective-permute-done | bytes 393248 | tf_op jit(solution)/shard_map/ppermute | solution.py:419
  13.8 1.5 %collective-permute-start.9 = (bf16[128,1536]{1,0:T(8,128)(2,1)S(1)}, bf16[128,1536]{1,0:T(8,128)(2,1)S(1)}, u32[]{:S(2)}, u32[]{:S(2)}) collective-permute-start(bf16[128,1536]{1,0:T(8,128)(2,1)S(1)} %collective-permute-done.5.rest_1_.refs_5_), channel_id=1, source_target_pairs={{0,4},{2,6},{4,0},{6,2},{8,12},{10,14},{12,8},{14,10},{16,20},{18,... | collective-permute-start | bytes 1179656 | tf_op jit(solution)/shard_map/ppermute | solution.py:21
  15.3 0.2 collective-permute-done.7.rest_2_.refs_6_
  15.5 3.1 %collective-permute-start.10 = (bf16[128,1536]{1,0:T(8,128)(2,1)S(1)}, bf16[128,1536]{1,0:T(8,128)(2,1)S(1)}, u32[]{:S(2)}, u32[]{:S(2)}) collective-permute-start(bf16[128,1536]{1,0:T(8,128)(2,1)S(1)} %collective-permute-done.5.rest_1_.refs_5_), channel_id=1, source_target_pairs={{0,16},{2,18},{4,20},{6,22},{16,24},{18,26},{20,28},{22,30},{24,8}... | collective-permute-start | bytes 1179656 | tf_op jit(solution)/shard_map/ppermute | solution.py:419
  18.6 1.7 %inner_rows.1 = (bf16[128,2048]{1,0:T(8,128)(2,1)S(1)}, bf16[128,1024]{1,0:T(8,128)(2,1)S(1)}) custom-call(s32[7,8,128]{2,1,0:T(8,128)S(1)} %get-tuple-element.42.facts_ref, bf16[2,128,6144]{2,1,0:T(8,128)(2,1)S(1)} %get-tuple-element.35.rows_ref), custom_call_target="tpu_custom_call" | custom-call | tf_op jit(solution)/shard_map/inner_rows/pallas_call | solution.py:481
  20.3 3.7 %collective-permute-done.8.rest_3_.refs_7_ = bf16[128,1536]{1,0:T(8,128)(2,1)S(1)} collective-permute-done((bf16[128,1536]{1,0:T(8,128)(2,1)S(1)}, bf16[128,1536]{1,0:T(8,128)(2,1)S(1)}, u32[]{:S(2)}, u32[]{:S(2)}) %collective-permute-start.8) | collective-permute-done | bytes 393248 | tf_op jit(solution)/shard_map/ppermute | solution.py:419
  24.0 0.0 collective-permute-start.6
  24.0 0.0 collective-permute-done.1.halo_ref
  24.0 1.5 %collective-permute-start.11 = (bf16[128,1536]{1,0:T(8,128)(2,1)S(1)}, bf16[128,1536]{1,0:T(8,128)(2,1)S(1)}, u32[]{:S(2)}, u32[]{:S(2)}) collective-permute-start(bf16[128,1536]{1,0:T(8,128)(2,1)S(1)} %collective-permute-done.8.rest_3_.refs_7_), channel_id=1, source_target_pairs={{0,4},{2,6},{4,0},{6,2},{8,12},{10,14},{12,8},{14,10},{16,20},{18,... | collective-permute-start | bytes 1179656 | tf_op jit(solution)/shard_map/ppermute | solution.py:21
  25.5 1.1 %edge_rows.2 = (bf16[128,1024]{1,0:T(8,128)(2,1)S(1)}, bf16[128,512]{1,0:T(8,128)(2,1)S(1)}) custom-call(s32[7,8,128]{2,1,0:T(8,128)S(1)} %get-tuple-element.42.facts_ref, bf16[2,128,6144]{2,1,0:T(8,128)(2,1)S(1)} %get-tuple-element.35.rows_ref, bf16[128,2048]{1,0:T(8,128)(2,1)S(1)} %collective-permute-done.1.halo_ref), custom_call_target="tpu_custom_call" | custom-call | tf_op jit(solution)/shard_map/edge_rows/pallas_call | solution.py:469
  26.6 0.0 collective-permute-done.9.rest_4_.refs_8_
  26.6 1.1 %collective-permute-start.12 = (bf16[80,1536]{1,0:T(8,128)(2,1)S(1)}, bf16[80,1536]{1,0:T(8,128)(2,1)S(1)}, u32[]{:S(2)}, u32[]{:S(2)}) collective-permute-start(bf16[80,1536]{1,0:T(8,128)(2,1)S(1)} %slice.6), channel_id=1, source_target_pairs={{0,16},{2,18},{4,20},{6,22},{16,24},{18,26},{20,28},{22,30},{24,8}... | collective-permute-start | bytes 737288 | tf_op jit(solution)/shard_map/ppermute | solution.py:419
  27.7 0.0 collective-permute-done.6.their_ref
  27.7 0.9 %inner_project.1 = (f32[256,1536]{1,0:T(8,128)S(1)}, bf16[256,384]{1,0:T(8,128)(2,1)S(1)}) custom-call(bf16[128,2048]{1,0:T(8,128)(2,1)S(1)} %get-tuple-element.43.inner_ref, bf16[128,1024]{1,0:T(8,128)(2,1)S(1)} %collective-permute-done.6.their_ref, bf16[128,1536]{1,0:T(8,128)(2,1)S(1)} %copy-done, ...), custom_call_target="tpu_custom_call" | custom-call | tf_op jit(solution)/shard_map/inner_project/pallas_call | solution.py:495
  28.6 3.5 %collective-permute-done.10.rest_0_.refs_9_ = bf16[128,1536]{1,0:T(8,128)(2,1)S(1)} collective-permute-done((bf16[128,1536]{1,0:T(8,128)(2,1)S(1)}, bf16[128,1536]{1,0:T(8,128)(2,1)S(1)}, u32[]{:S(2)}, u32[]{:S(2)}) %collective-permute-start.10) | collective-permute-done | bytes 393248 | tf_op jit(solution)/shard_map/ppermute | solution.py:419
  32.1 1.6 %collective-permute-start.13 = (bf16[48,1536]{1,0:T(8,128)(2,1)S(1)}, bf16[48,1536]{1,0:T(8,128)(2,1)S(1)}, u32[]{:S(2)}, u32[]{:S(2)}) collective-permute-start(bf16[48,1536]{1,0:T(8,128)(2,1)S(1)} %slice.7), channel_id=1, source_target_pairs={{0,4},{2,6},{4,0},{6,2},{8,12},{10,14},{12,8},{14,10},{16,20},{18,... | collective-permute-start | bytes 442376 | tf_op jit(solution)/shard_map/ppermute | solution.py:21
  33.6 0.0 collective-permute-done.2.halo_ref
  33.6 1.1 %edge_rows.3 = (bf16[128,1024]{1,0:T(8,128)(2,1)S(1)}, bf16[128,512]{1,0:T(8,128)(2,1)S(1)}) custom-call(s32[7,8,128]{2,1,0:T(8,128)S(1)} %get-tuple-element.42.facts_ref, bf16[2,128,6144]{2,1,0:T(8,128)(2,1)S(1)} %get-tuple-element.35.rows_ref, bf16[128,2048]{1,0:T(8,128)(2,1)S(1)} %collective-permute-done.2.halo_ref), custom_call_target="tpu_custom_call" | custom-call | tf_op jit(solution)/shard_map/edge_rows/pallas_call | solution.py:469
  34.7 0.1 collective-permute-start.4
  34.8 0.5 %collective-permute-start.3 = (bf16[128,512]{1,0:T(8,128)(2,1)S(1)}, bf16[128,512]{1,0:T(8,128)(2,1)S(1)}, u32[]{:S(2)}, u32[]{:S(2)}) collective-permute-start(bf16[128,512]{1,0:T(8,128)(2,1)S(1)} %get-tuple-element.39), channel_id=1, source_target_pairs={{0,2},{2,0},{4,6},{6,4},{8,10},{10,8},{12,14},{14,12},{16,18},{18,... | collective-permute-start | bytes 393224 | tf_op jit(solution)/shard_map/ppermute | solution.py:21
  35.3 0.6 %collective-permute-done.11.rest_1_.refs_10_ = bf16[128,1536]{1,0:T(8,128)(2,1)S(1)} collective-permute-done((bf16[128,1536]{1,0:T(8,128)(2,1)S(1)}, bf16[128,1536]{1,0:T(8,128)(2,1)S(1)}, u32[]{:S(2)}, u32[]{:S(2)}) %collective-permute-start.11) | collective-permute-done | bytes 393248 | tf_op jit(solution)/shard_map/ppermute | solution.py:21
  35.9 0.4 add_products.1.inner_total_ref
  36.2 0.0 collective-permute-done.4.refs_3_
  36.3 0.1 collective-permute-done.3.refs_2_
  36.3 1.1 %edge_project.1 = (f32[256,1536]{1,0:T(8,128)S(1)}, bf16[256,128]{1,0:T(8,128)(2,1)S(1)}) custom-call(bf16[128,1024]{1,0:T(8,128)(2,1)S(1)} %get-tuple-element.36.refs_0_, bf16[128,1024]{1,0:T(8,128)(2,1)S(1)} %get-tuple-element.38.refs_1_, bf16[128,512]{1,0:T(8,128)(2,1)S(1)} %collective-permute-done.3.refs_2_, ...), custom_call_target="tpu_custom_call" | custom-call | tf_op jit(solution)/shard_map/edge_project/pallas_call | solution.py:521
  37.4 1.2 %collective-permute-done.13.rest_1_ = bf16[48,1536]{1,0:T(8,128)(2,1)S(1)} collective-permute-done((bf16[48,1536]{1,0:T(8,128)(2,1)S(1)}, bf16[48,1536]{1,0:T(8,128)(2,1)S(1)}, u32[]{:S(2)}, u32[]{:S(2)}) %collective-permute-start.13) | collective-permute-done | bytes 147488 | tf_op jit(solution)/shard_map/ppermute | solution.py:21
  38.6 0.0 collective-permute-done.12.rest_0_
  38.7 0.4 last_project.3
  39.1 0.1 collective-permute-start.15
  39.2 0.3 last_project.2
  39.4 0.6 %collective-permute-start.14 = (bf16[256,512]{1,0:T(8,128)(2,1)S(1)}, bf16[256,512]{1,0:T(8,128)(2,1)S(1)}, u32[]{:S(2)}, u32[]{:S(2)}) collective-permute-start(bf16[256,512]{1,0:T(8,128)(2,1)S(1)} %get-tuple-element.56), channel_id=1, source_target_pairs={{0,2},{2,0},{4,6},{6,4},{8,10},{10,8},{12,14},{14,12},{16,18},{18,... | collective-permute-start | bytes 786440 | tf_op jit(solution)/shard_map/ppermute | solution.py:21
  40.0 1.1 %collective-permute-done.15.more_ref = bf16[256,1024]{1,0:T(8,128)(2,1)S(1)} collective-permute-done((bf16[256,1024]{1,0:T(8,128)(2,1)S(1)}, bf16[256,1024]{1,0:T(8,128)(2,1)S(1)}, u32[]{:S(2)}, u32[]{:S(2)}) %collective-permute-start.15) | collective-permute-done | bytes 524320 | tf_op jit(solution)/shard_map/ppermute | solution.py:21
  41.1 0.1 add.1.ready_ref
  41.1 0.3 collective-permute-done.14.more_ref
  41.4 0.9 %finish.1 = bf16[256,1536]{1,0:T(8,128)(2,1)} custom-call(f32[256,512]{1,0:T(8,128)S(1)} %get-tuple-element.55.total_ref, bf16[256,512]{1,0:T(8,128)(2,1)S(1)} %collective-permute-done.14.more_ref, bf16[256,1024]{1,0:T(8,128)(2,1)S(1)} %add.1.ready_ref), custom_call_target="tpu_custom_call" | custom-call | tf_op jit(solution)/shard_map/finish/pallas_call | solution.py:546
  (2 shorter events, 0.0 us)
Async XLA Ops:
  0.0 7.5 %collective-permute-start = (bf16[2,128,6144]{2,1,0:T(8,128)(2,1)}, bf16[2,128,6144]{2,1,0:T(8,128)(2,1)S(1)}, u32[]{:S(2)}, u32[]{:S(2)}) collective-permute-start(bf16[2,128,6144]{2,1,0:T(8,128)(2,1)} %bitcast.1), channel_id=1, source_target_pairs={{0,2},{2,0},{4,6},{6,4},{8,10},{10,8},{12,14},{14,12},{16,18},{18,... | collective-permute-start | bytes 9437192 | tf_op jit(solution)/shard_map/ppermute | solution.py:21
  0.5 13.3 %collective-permute-start.5 = (bf16[128,1536]{1,0:T(8,128)(2,1)}, bf16[128,1536]{1,0:T(8,128)(2,1)S(1)}, u32[]{:S(2)}, u32[]{:S(2)}) collective-permute-start(bf16[128,1536]{1,0:T(8,128)(2,1)} %refs_4_.1), channel_id=1, source_target_pairs={{0,16},{2,18},{4,20},{6,22},{16,24},{18,26},{20,28},{22,30},{24,8}... | collective-permute-start | bytes 1179656 | tf_op jit(solution)/shard_map/ppermute | solution.py:419
  4.0 11.5 %collective-permute-start.7 = (bf16[128,1536]{1,0:T(8,128)(2,1)}, bf16[128,1536]{1,0:T(8,128)(2,1)S(1)}, u32[]{:S(2)}, u32[]{:S(2)}) collective-permute-start(bf16[128,1536]{1,0:T(8,128)(2,1)} %refs_4_.1), channel_id=1, source_target_pairs={{0,4},{2,6},{4,0},{6,2},{8,12},{10,14},{12,8},{14,10},{16,20},{18,... | collective-permute-start | bytes 1179656 | tf_op jit(solution)/shard_map/ppermute | solution.py:21
  7.5 1.9 %copy-start = (bf16[128,1536]{1,0:T(8,128)(2,1)S(1)}, bf16[128,1536]{1,0:T(8,128)(2,1)}, u32[]{:S(2)}) copy-start(bf16[128,1536]{1,0:T(8,128)(2,1)} %refs_4_.1) | copy-start | bytes 1179652
  7.7 16.2 %collective-permute-start.1 = (bf16[128,2048]{1,0:T(8,128)(2,1)S(1)}, bf16[128,2048]{1,0:T(8,128)(2,1)S(1)}, u32[]{:S(2)}, u32[]{:S(2)}) collective-permute-start(bf16[128,2048]{1,0:T(8,128)(2,1)S(1)} %pack_first.1), channel_id=1, source_target_pairs={{0,1},{1,0},{2,3},{3,2},{4,5},{5,4},{6,7},{7,6},{8,9},{9,8},{10,11... | collective-permute-start | bytes 1572872 | tf_op jit(solution)/shard_map/ppermute | solution.py:465
  9.3 14.6 %collective-permute-start.8 = (bf16[128,1536]{1,0:T(8,128)(2,1)S(1)}, bf16[128,1536]{1,0:T(8,128)(2,1)S(1)}, u32[]{:S(2)}, u32[]{:S(2)}) collective-permute-start(bf16[128,1536]{1,0:T(8,128)(2,1)S(1)} %copy-done), channel_id=1, source_target_pairs={{0,8},{2,10},{4,12},{6,14},{16,0},{18,2},{20,4},{22,6},{24,16},{26... | collective-permute-start | bytes 1179656 | tf_op jit(solution)/shard_map/ppermute | solution.py:419
  11.4 22.2 %collective-permute-start.2 = (bf16[128,2048]{1,0:T(8,128)(2,1)S(1)}, bf16[128,2048]{1,0:T(8,128)(2,1)S(1)}, u32[]{:S(2)}, u32[]{:S(2)}) collective-permute-start(bf16[128,2048]{1,0:T(8,128)(2,1)S(1)} %get-tuple-element.37), channel_id=1, source_target_pairs={{0,1},{1,0},{2,3},{3,2},{4,5},{5,4},{6,7},{7,6},{8,9},{9,8},{10,11... | collective-permute-start | bytes 1572872 | tf_op jit(solution)/shard_map/ppermute | solution.py:465
  13.8 12.8 %collective-permute-start.9 = (bf16[128,1536]{1,0:T(8,128)(2,1)S(1)}, bf16[128,1536]{1,0:T(8,128)(2,1)S(1)}, u32[]{:S(2)}, u32[]{:S(2)}) collective-permute-start(bf16[128,1536]{1,0:T(8,128)(2,1)S(1)} %collective-permute-done.5.rest_1_.refs_5_), channel_id=1, source_target_pairs={{0,4},{2,6},{4,0},{6,2},{8,12},{10,14},{12,8},{14,10},{16,20},{18,... | collective-permute-start | bytes 1179656 | tf_op jit(solution)/shard_map/ppermute | solution.py:21
  15.5 16.5 %collective-permute-start.10 = (bf16[128,1536]{1,0:T(8,128)(2,1)S(1)}, bf16[128,1536]{1,0:T(8,128)(2,1)S(1)}, u32[]{:S(2)}, u32[]{:S(2)}) collective-permute-start(bf16[128,1536]{1,0:T(8,128)(2,1)S(1)} %collective-permute-done.5.rest_1_.refs_5_), channel_id=1, source_target_pairs={{0,16},{2,18},{4,20},{6,22},{16,24},{18,26},{20,28},{22,30},{24,8}... | collective-permute-start | bytes 1179656 | tf_op jit(solution)/shard_map/ppermute | solution.py:419
  24.0 3.7 %collective-permute-start.6 = (bf16[128,1024]{1,0:T(8,128)(2,1)S(1)}, bf16[128,1024]{1,0:T(8,128)(2,1)S(1)}, u32[]{:S(2)}, u32[]{:S(2)}) collective-permute-start(bf16[128,1024]{1,0:T(8,128)(2,1)S(1)} %get-tuple-element.44), channel_id=1, source_target_pairs={{0,2},{2,0},{4,6},{6,4},{8,10},{10,8},{12,14},{14,12},{16,18},{18,... | collective-permute-start | bytes 786440 | tf_op jit(solution)/shard_map/ppermute | solution.py:21
  24.0 11.9 %collective-permute-start.11 = (bf16[128,1536]{1,0:T(8,128)(2,1)S(1)}, bf16[128,1536]{1,0:T(8,128)(2,1)S(1)}, u32[]{:S(2)}, u32[]{:S(2)}) collective-permute-start(bf16[128,1536]{1,0:T(8,128)(2,1)S(1)} %collective-permute-done.8.rest_3_.refs_7_), channel_id=1, source_target_pairs={{0,4},{2,6},{4,0},{6,2},{8,12},{10,14},{12,8},{14,10},{16,20},{18,... | collective-permute-start | bytes 1179656 | tf_op jit(solution)/shard_map/ppermute | solution.py:21
  26.6 12.0 %collective-permute-start.12 = (bf16[80,1536]{1,0:T(8,128)(2,1)S(1)}, bf16[80,1536]{1,0:T(8,128)(2,1)S(1)}, u32[]{:S(2)}, u32[]{:S(2)}) collective-permute-start(bf16[80,1536]{1,0:T(8,128)(2,1)S(1)} %slice.6), channel_id=1, source_target_pairs={{0,16},{2,18},{4,20},{6,22},{16,24},{18,26},{20,28},{22,30},{24,8}... | collective-permute-start | bytes 737288 | tf_op jit(solution)/shard_map/ppermute | solution.py:419
  32.1 6.6 %collective-permute-start.13 = (bf16[48,1536]{1,0:T(8,128)(2,1)S(1)}, bf16[48,1536]{1,0:T(8,128)(2,1)S(1)}, u32[]{:S(2)}, u32[]{:S(2)}) collective-permute-start(bf16[48,1536]{1,0:T(8,128)(2,1)S(1)} %slice.7), channel_id=1, source_target_pairs={{0,4},{2,6},{4,0},{6,2},{8,12},{10,14},{12,8},{14,10},{16,20},{18,... | collective-permute-start | bytes 442376 | tf_op jit(solution)/shard_map/ppermute | solution.py:21
  34.7 1.5 %collective-permute-start.4 = (bf16[128,512]{1,0:T(8,128)(2,1)S(1)}, bf16[128,512]{1,0:T(8,128)(2,1)S(1)}, u32[]{:S(2)}, u32[]{:S(2)}) collective-permute-start(bf16[128,512]{1,0:T(8,128)(2,1)S(1)} %get-tuple-element.40), channel_id=1, source_target_pairs={{0,2},{2,0},{4,6},{6,4},{8,10},{10,8},{12,14},{14,12},{16,18},{18,... | collective-permute-start | bytes 393224 | tf_op jit(solution)/shard_map/ppermute | solution.py:21
  34.8 1.5 %collective-permute-start.3 = (bf16[128,512]{1,0:T(8,128)(2,1)S(1)}, bf16[128,512]{1,0:T(8,128)(2,1)S(1)}, u32[]{:S(2)}, u32[]{:S(2)}) collective-permute-start(bf16[128,512]{1,0:T(8,128)(2,1)S(1)} %get-tuple-element.39), channel_id=1, source_target_pairs={{0,2},{2,0},{4,6},{6,4},{8,10},{10,8},{12,14},{14,12},{16,18},{18,... | collective-permute-start | bytes 393224 | tf_op jit(solution)/shard_map/ppermute | solution.py:21
  39.1 2.0 %collective-permute-start.15 = (bf16[256,1024]{1,0:T(8,128)(2,1)S(1)}, bf16[256,1024]{1,0:T(8,128)(2,1)S(1)}, u32[]{:S(2)}, u32[]{:S(2)}) collective-permute-start(bf16[256,1024]{1,0:T(8,128)(2,1)S(1)} %get-tuple-element.58), channel_id=1, source_target_pairs={{0,2},{2,0},{4,6},{6,4},{8,10},{10,8},{12,14},{14,12},{16,18},{18,... | collective-permute-start | bytes 1572872 | tf_op jit(solution)/shard_map/ppermute | solution.py:21
  39.4 2.0 %collective-permute-start.14 = (bf16[256,512]{1,0:T(8,128)(2,1)S(1)}, bf16[256,512]{1,0:T(8,128)(2,1)S(1)}, u32[]{:S(2)}, u32[]{:S(2)}) collective-permute-start(bf16[256,512]{1,0:T(8,128)(2,1)S(1)} %get-tuple-element.56), channel_id=1, source_target_pairs={{0,2},{2,0},{4,6},{6,4},{8,10},{10,8},{12,14},{14,12},{16,18},{18,... | collective-permute-start | bytes 786440 | tf_op jit(solution)/shard_map/ppermute | solution.py:21
where the time goes:
time: 42.5 us; the launch traced here: 42.3 us
  starting transfers between devices  19.2 us (45%)
  waiting for transfers between devices  12.2 us (29%)
  Pallas kernels  10.8 us (25%)
    ppermute x4, starting transfers between devices, around(): lax.ppermute(value, 'dp', [(4 * here + rest, 4 * there + rest) for here,...  9.15 us
    ppermute x4, waiting for transfers between devices, around(): lax.ppermute(value, 'dp', [(4 * here + rest, 4 * there + rest) for here,...  8.75 us
    ppermute x10, starting transfers between devices, partner(): return lax.ppermute(value, axis, pairs)  7.69 us
    ppermute x10, waiting for transfers between devices, partner(): return lax.ppermute(value, axis, pairs)  3.43 us
    ppermute x2, starting transfers between devices, body_edge(): halos = [lax.ppermute(part, 'ctx', [(0, 1), (1, 0)]) for part in packed]  2.33 us
    pallas_call x2, Pallas kernels, edge_rows(): call(functools.partial(edge_kernel, sum(part_heads[:part])), 'edge_rows',...  2.24 us
    pallas_call x1, Pallas kernels, body_edge(): call(stage_kernel, 'stage', [own.shape, (7, 8, 128)], [HBM()] * 3, dtypes...  1.91 us
    pallas_call x1, Pallas kernels, body_edge(): call(inner_kernel, 'inner_rows', [(block_rows, features), (block_rows, fe...  1.73 us
  transfers between devices with their start and end apart: 16, of which 9 were waited for; matrix products, arithmetic and copies ran while one was open for 0% of the time, Pallas kernels for 22%

commit v1 on v0

--- a/solution.py
+++ b/solution.py
@@ -275,9 +275,8 @@
         for at, place in enumerate(places):
             from_line = jnp.where(line == place, places[at - steps], from_line)
         pair = from_line * 2 + (1 - side if other_side else side)
-        here = pl.ds(pl.multiple_of((pair * 2 + core) * depth, depth), depth)
-        there = pl.ds(pl.multiple_of(pair * depth, depth), depth)
-        found.append((here, there))
+        columns = [pair * 2 + core, pair * 2 + 1 - core, pair]
+        found.append([pl.ds(pl.multiple_of(column * depth, depth), depth) for column in columns])
     return found
 
 
@@ -285,7 +284,7 @@
     shard_refs, (total_ref, left_ref, features) = rest[:-3], rest[-3:]
     block = inner_ref.shape[0]
     depth = left_ref.shape[1] // (len(origins) - early)
-    for number, (here, there) in enumerate(shard_places(origins, depth)):
+    for number, (here, _, there) in enumerate(shard_places(origins, depth)):
         ref, at = (features, number) if number < early else (left_ref, number - early)
         ref[:block, at * depth : (at + 1) * depth] = inner_ref[:, here]
         ref[block:, at * depth : (at + 1) * depth] = their_ref[:, there]
@@ -300,83 +299,79 @@
 
 def add_products_kernel(left_ref, inner_total_ref, *rest):
     shard_refs, total_ref = rest[:-1], rest[-1]
-    depths = sum(ref.shape[0] for ref in shard_refs)
     tile = 2 * HEAD
     for first in range(0, total_ref.shape[1], tile):
         columns = slice(first, first + tile)
         weight = jnp.concatenate([ref[:, columns] for ref in shard_refs], axis=0)
         total_ref[:, columns] = inner_total_ref[:, columns] + jnp.dot(
-            left_ref[:, :depths], weight, preferred_element_type=jnp.float32
+            left_ref[...], weight, preferred_element_type=jnp.float32
         )
 
 
-def edge_project_kernel(origins, parts, *refs):
-    edge_refs, their_refs, shard_refs = refs[:parts], refs[parts : 2 * parts], refs[2 * parts : -5]
-    total_ref, left_ref, edge_rows, their_rows, features = refs[-5:]
-    for refs, held in ((edge_refs, edge_rows), (their_refs, their_rows)):
+def arrange_kernel(origins, parts, inner_ref, *refs):
+    edge_refs, their_refs = refs[:parts], refs[parts : 2 * parts]
+    out_ref, last_ref, edge_rows, their_rows = refs[2 * parts :]
+    for some_refs, held in ((edge_refs, edge_rows), (their_refs, their_rows)):
         first = 0
-        for ref in refs:
+        for ref in some_refs:
             held[:, first : first + ref.shape[1]] = ref[...]
             first += ref.shape[1]
-    block, depth = left_ref.shape[0] // 2, left_ref.shape[1]
-    for number, (here, there) in enumerate(shard_places(origins, depth)):
-        last = number == len(origins) - 1
-        ref, at = (left_ref, 0) if last else (features, number * depth)
-        ref[:block, at : at + depth] = edge_rows[:, here]
-        ref[block:, at : at + depth] = their_rows[:, there]
-    tile = 2 * HEAD
-    for first in range(0, total_ref.shape[1], tile):
-        columns = slice(first, first + tile)
-        weight = jnp.concatenate([ref[:, columns] for ref in shard_refs], axis=0)
-        total_ref[:, columns] = jnp.dot(
-            features[...], weight, preferred_element_type=jnp.float32
-        )
-
-
-def last_project_kernel(first, edge_ref, left_ref, inner_total_ref, edge_total_ref, *rest):
+    block, depth = last_ref.shape[0] // 2, last_ref.shape[1] // 2
+    places = shard_places(origins, depth)
+    for number, (here, _, there) in enumerate(places[:-1]):
+        at = slice(number * depth, (number + 1) * depth)
+        out_ref[:block, at] = edge_rows[:, here]
+        out_ref[block:, at] = their_rows[:, there]
+    for number, here in enumerate(places[-1][:2]):
+        at = slice(number * depth, (number + 1) * depth)
+        last_ref[:block, at] = inner_ref[:, here]
+        last_ref[block:, at] = edge_rows[:, here]
+
+
+def project_kernel(first, edge_ref, inner_total_ref, *rest):
     shard_refs, (own_total_ref, their_total_ref) = rest[:-2], rest[-2:]
     block = own_total_ref.shape[0] // 2
-    depth = sum(ref.shape[0] for ref in shard_refs)
-    features = jnp.concatenate([left_ref[:, -depth:], edge_ref[...]], axis=0)
     tile = 2 * HEAD
     for at in range(0, own_total_ref.shape[1], tile):
         here = slice(at, at + tile)
         columns = slice(first + at, first + at + tile)
         weight = jnp.concatenate([ref[:, columns] for ref in shard_refs], axis=0)
-        total = jnp.dot(features, weight, preferred_element_type=jnp.float32)
-        inner = inner_total_ref[:, columns] + total[: 2 * block]
-        edge = edge_total_ref[:, columns] + total[2 * block :]
-        own_total_ref[:block, here] = inner[:block]
+        edge = jnp.dot(edge_ref[...], weight, preferred_element_type=jnp.float32)
+        own_total_ref[:block, here] = inner_total_ref[:block, columns]
         own_total_ref[block:, here] = edge[:block]
-        their_total_ref[:block, here] = inner[block:].astype(jnp.bfloat16)
+        their_total_ref[:block, here] = inner_total_ref[block:, columns].astype(jnp.bfloat16)
         their_total_ref[block:, here] = edge[block:].astype(jnp.bfloat16)
 
 
-def add_kernel(total_ref, more_ref, out_ref):
-    out_ref[...] = (total_ref[...] + more_ref[...]).astype(jnp.bfloat16)
-
-
-def finish_kernel(total_ref, more_ref, ready_ref, out_ref, held, sems):
+def last_project_kernel(features_ref, *rest):
+    shard_refs, total_refs, out_ref = rest[:4], rest[4:-1], rest[-1]
+    first = 0
+    for total_ref in total_refs:
+        columns = slice(first, first + total_ref.shape[1])
+        weight = jnp.concatenate([ref[:, columns] for ref in shard_refs], axis=0)
+        out_ref[:, columns] = total_ref[...] + jnp.dot(
+            features_ref[...], weight, preferred_element_type=jnp.float32
+        )
+        first += total_ref.shape[1]
+
+
+def finish_kernel(total_ref, *rest):
+    more_refs, (out_ref, held, sems) = rest[:-3], rest[-3:]
     block = out_ref.shape[0] // 2
     ctx = lax.axis_index("ctx")
-    ready = ready_ref.shape[1]
-    blocks = [(slice(0, block), ctx), (slice(block, 2 * block), 1 - ctx)]
-
-    def copy(source_ref, which, first, sem):
-        rows, place = blocks[which]
-        there = pl.ds(pl.multiple_of(place * block, block), block)
-        columns = pl.ds(first, source_ref.shape[1])
-        return pltpu.make_async_copy(source_ref.at[rows], out_ref.at[there, columns], sem)
-
-    copies = [copy(ready_ref, which, 0, sems.at[which]) for which in range(2)]
-    for one in copies:
-        one.start()
-    for which, (rows, _) in enumerate(blocks):
-        held[rows] = (total_ref[rows] + more_ref[rows]).astype(jnp.bfloat16)
-        copies.append(copy(held, which, ready, sems.at[2 + which]))
+    copies = []
+    for which, place in ((0, ctx), (1, 1 - ctx)):
+        rows = slice(which * block, (which + 1) * block)
+        first = 0
+        for more_ref in more_refs:
+            columns = slice(first, first + more_ref.shape[1])
+            held[rows, columns] = (total_ref[rows, columns] + more_ref[rows]).astype(jnp.bfloat16)
+            first += more_ref.shape[1]
+        target = out_ref.at[pl.ds(pl.multiple_of(place * block, block), block)]
+        copies.append(pltpu.make_async_copy(held.at[rows], target, sems.at[which]))
         copies[-1].start()
-    for one in copies:
-        one.wait()
+    for copy in copies:
+        copy.wait()
 
 
 SMEM = functools.partial(pl.BlockSpec, memory_space=pltpu.SMEM)
@@ -493,9 +488,9 @@
     early = list(shards)
     origins = [*early, (2, False), (3, True), (2, True)]
     inner_total, inner_left = call(
-        functools.partial(inner_project_kernel, origins, len(early)),
+        functools.partial(inner_project_kernel, origins[:-1], len(early)),
         "inner_project",
-        [(local_rows, width), (local_rows, (len(origins) - len(early)) * depth)],
+        [(local_rows, width), (local_rows, (len(origins) - 1 - len(early)) * depth)],
         [VMEM()] * (2 + len(early)),
         dtypes=[jnp.float32, bf16],
         scratch=[pltpu.VMEM((local_rows, len(early) * depth), bf16)],
@@ -517,40 +512,49 @@
         dtypes=[jnp.float32],
     )(inner_left, inner_total, *more)
     theirs[-1] = after(theirs[-1], inner_total)
-    pieces = [piece for origin in origins[:-1] for piece in shards[origin]]
-    edge_total, edge_left = call(
-        functools.partial(edge_project_kernel, origins, len(edges)),
-        "edge_project",
-        [(local_rows, width), (local_rows, depth)],
-        [VMEM()] * (len(edges) + len(theirs) + len(pieces)),
-        dtypes=[jnp.float32, bf16],
+    arranged, last_features = call(
+        functools.partial(arrange_kernel, origins, len(edges)),
+        "arrange",
+        [(local_rows, (len(origins) - 1) * depth), (local_rows, 2 * depth)],
+        [VMEM()] * (1 + len(edges) + len(theirs)),
         scratch=[
             pltpu.VMEM((block_rows, features), bf16),
             pltpu.VMEM((block_rows, features // 2), bf16),
-            pltpu.VMEM((local_rows, (len(origins) - 1) * depth), bf16),
         ],
-    )(*edges, *theirs, *pieces)
-    sums = []
-    first = 0
-    for columns in (width // 3 * 2, width // 3):
+    )(inner, *edges, *theirs)
+    last = shards[origins[-1]]
+    last_swapped = [to_core(piece) for piece in last]
+    pieces = [piece for origin in origins[:-1] for piece in shards[origin]]
+    own_totals, mores = [], []
+    parts = 3
+    for part in range(parts):
+        columns = width // parts
         own_total, their_total = call(
-            functools.partial(last_project_kernel, first),
-            "last_project",
+            functools.partial(project_kernel, part * columns),
+            "project",
             [(local_rows, columns)] * 2,
-            [VMEM()] * (4 + len(shards[origins[-1]])),
+            [VMEM()] * (2 + len(pieces)),
             dtypes=[jnp.float32, bf16],
-        )(edge_left, inner_left, inner_total, edge_total, *shards[origins[-1]])
-        sums.append((own_total, to_core(their_total)))
-        first += columns
-    ready = call(add_kernel, "add", sums[0][0].shape, [VMEM()] * 2)(*sums[0])
+        )(arranged, inner_total, *pieces)
+        own_totals.append(own_total)
+        if part == parts - 1:
+            their_total = after(their_total, *last)
+        mores.append(to_core(their_total))
+    total = call(
+        last_project_kernel,
+        "last_project",
+        (local_rows, width),
+        [VMEM()] * (1 + 2 * len(last) + parts),
+        dtypes=[jnp.float32],
+    )(last_features, *last, *last_swapped, *own_totals)
     return call(
         finish_kernel,
         "finish",
         (local_rows, width),
-        [VMEM()] * 3,
-        scratch=[pltpu.VMEM(sums[1][0].shape, bf16), pltpu.SemaphoreType.DMA((4,))],
+        [VMEM()] * (1 + parts),
+        scratch=[pltpu.VMEM((local_rows, width), bf16), pltpu.SemaphoreType.DMA((2,))],
         out_spec=HBM(),
-    )(*sums[1], ready)
+    )(total, *mores)
 
 
 def body(projections, block_source, clip_ids, out_weight):

time: 42.5 us -> 42.3 us (level)
  waiting for transfers between devices: 12.2 us -> 11 us
  starting transfers between devices: 19.2 us -> 20 us
    ppermute x10 -> x13, waiting for transfers between devices: 3.43 us -> 2.3 us  [partner(): return lax.ppermute(value, axis, pairs)]
    ppermute x10 -> x13, starting transfers between devices: 7.69 us -> 8.49 us  [partner(): return lax.ppermute(value, axis, pairs)]
    pallas_call x6 -> x7, Pallas kernels: 3.64 us -> 3.72 us  [the longest x3 1.31 us: body_edge(): call(functools.partial(project_kernel, part * columns), 'project', [(loca...]
  transfers between devices with their start and end apart: 16 -> 19, of which waited for: 9 -> 8; matrix products, arithmetic and copies ran while one was open for 0% -> 0% of each run, Pallas kernels for 22% -> 24%
where the time goes in v1:
time: 42.3 us; the launch traced here: 42.1 us
  starting transfers between devices  20 us (47%)
  waiting for transfers between devices  11 us (26%)
  Pallas kernels  10.9 us (26%)
    ppermute x4, starting transfers between devices, around(): lax.ppermute(value, 'dp', [(4 * here + rest, 4 * there + rest) for here,...  9.14 us
    ppermute x4, waiting for transfers between devices, around(): lax.ppermute(value, 'dp', [(4 * here + rest, 4 * there + rest) for here,...  8.74 us
    ppermute x13, starting transfers between devices, partner(): return lax.ppermute(value, axis, pairs)  8.49 us
    ppermute x2, starting transfers between devices, body_edge(): halos = [lax.ppermute(part, 'ctx', [(0, 1), (1, 0)]) for part in packed]  2.33 us
    ppermute x13, waiting for transfers between devices, partner(): return lax.ppermute(value, axis, pairs)  2.3 us
    pallas_call x2, Pallas kernels, edge_rows(): call(functools.partial(edge_kernel, sum(part_heads[:part])), 'edge_rows',...  2.24 us
    pallas_call x1, Pallas kernels, body_edge(): call(stage_kernel, 'stage', [own.shape, (7, 8, 128)], [HBM()] * 3, dtypes...  1.91 us
    pallas_call x1, Pallas kernels, body_edge(): call(inner_kernel, 'inner_rows', [(block_rows, features), (block_rows, fe...  1.73 us
  transfers between devices with their start and end apart: 19, of which 8 were waited for; matrix products, arithmetic and copies ran while one was open for 0% of the time, Pallas kernels for 24%

profile of v1, /device:TPU:0, one launch (start us, length us, event | category | flops | bytes accessed | tf_op | source)
XLA Modules:
  0.0 42.1 jit_solution(13603650523912104475)
XLA Ops:
  0.0 0.5 %collective-permute-start.1 = (bf16[2,128,6144]{2,1,0:T(8,128)(2,1)}, bf16[2,128,6144]{2,1,0:T(8,128)(2,1)S(1)}, u32[]{:S(2)}, u32[]{:S(2)}) collective-permute-start(bf16[2,128,6144]{2,1,0:T(8,128)(2,1)} %bitcast.1), channel_id=1, source_target_pairs={{0,2},{2,0},{4,6},{6,4},{8,10},{10,8},{12,14},{14,12},{16,18},{18,... | collective-permute-start | bytes 9437192 | tf_op jit(solution)/shard_map/ppermute | solution.py:21
  0.5 3.6 %collective-permute-start = (bf16[128,1536]{1,0:T(8,128)(2,1)}, bf16[128,1536]{1,0:T(8,128)(2,1)S(1)}, u32[]{:S(2)}, u32[]{:S(2)}) collective-permute-start(bf16[128,1536]{1,0:T(8,128)(2,1)} %rest_0_.7), channel_id=1, source_target_pairs={{0,16},{2,18},{4,20},{6,22},{16,24},{18,26},{20,28},{22,30},{24,8}... | collective-permute-start | bytes 1179656 | tf_op jit(solution)/shard_map/ppermute | solution.py:414
  4.0 1.5 %collective-permute-start.7 = (bf16[128,1536]{1,0:T(8,128)(2,1)}, bf16[128,1536]{1,0:T(8,128)(2,1)S(1)}, u32[]{:S(2)}, u32[]{:S(2)}) collective-permute-start(bf16[128,1536]{1,0:T(8,128)(2,1)} %rest_0_.7), channel_id=1, source_target_pairs={{0,4},{2,6},{4,0},{6,2},{8,12},{10,14},{12,8},{14,10},{16,20},{18,... | collective-permute-start | bytes 1179656 | tf_op jit(solution)/shard_map/ppermute | solution.py:21
  5.5 1.9 %stage.1 = (bf16[2,128,6144]{2,1,0:T(8,128)(2,1)S(1)}, s32[7,8,128]{2,1,0:T(8,128)S(1)}) custom-call(s32[1,1,2]{2,1,0:T(1,128)} %sources.1, s32[1,4]{1,0:T(1,128)} %clips.1, bf16[2,128,6144]{2,1,0:T(8,128)(2,1)} %bitcast.2), custom_call_target="tpu_custom_call" | custom-call | tf_op jit(solution)/shard_map/stage/pallas_call | solution.py:432
  7.5 0.0 collective-permute-done.1.partner_ref
  7.5 0.0 copy-start
  7.5 0.2 pack_first.1
  7.7 1.6 %collective-permute-start.2 = (bf16[128,2048]{1,0:T(8,128)(2,1)S(1)}, bf16[128,2048]{1,0:T(8,128)(2,1)S(1)}, u32[]{:S(2)}, u32[]{:S(2)}) collective-permute-start(bf16[128,2048]{1,0:T(8,128)(2,1)S(1)} %pack_first.1), channel_id=1, source_target_pairs={{0,1},{1,0},{2,3},{3,2},{4,5},{5,4},{6,7},{7,6},{8,9},{9,8},{10,11... | collective-permute-start | bytes 1572872 | tf_op jit(solution)/shard_map/ppermute | solution.py:460
  9.3 1.4 %collective-permute-start.8 = (bf16[128,1536]{1,0:T(8,128)(2,1)S(1)}, bf16[128,1536]{1,0:T(8,128)(2,1)S(1)}, u32[]{:S(2)}, u32[]{:S(2)}) collective-permute-start(bf16[128,1536]{1,0:T(8,128)(2,1)S(1)} %copy-done), channel_id=1, source_target_pairs={{0,8},{2,10},{4,12},{6,14},{16,0},{18,2},{20,4},{22,6},{24,16},{26... | collective-permute-start | bytes 1179656 | tf_op jit(solution)/shard_map/ppermute | solution.py:414
  10.7 0.7 %pack.1 = (bf16[2,128,6144]{2,1,0:T(8,128)(2,1)S(1)}, bf16[128,2048]{1,0:T(8,128)(2,1)S(1)}) custom-call(s32[7,8,128]{2,1,0:T(8,128)S(1)} %get-tuple-element.40.facts_ref, bf16[2,128,6144]{2,1,0:T(8,128)(2,1)S(1)} %get-tuple-element.36.own_ref, bf16[2,128,6144]{2,1,0:T(8,128)(2,1)S(1)} %collective-permute-done.1.partner_ref), custom_call_target="tpu_custom_call" | custom-call | tf_op jit(solution)/shard_map/pack/pallas_call | solution.py:452
  11.4 0.7 %collective-permute-start.3 = (bf16[128,2048]{1,0:T(8,128)(2,1)S(1)}, bf16[128,2048]{1,0:T(8,128)(2,1)S(1)}, u32[]{:S(2)}, u32[]{:S(2)}) collective-permute-start(bf16[128,2048]{1,0:T(8,128)(2,1)S(1)} %get-tuple-element.38), channel_id=1, source_target_pairs={{0,1},{1,0},{2,3},{3,2},{4,5},{5,4},{6,7},{7,6},{8,9},{9,8},{10,11... | collective-permute-start | bytes 1572872 | tf_op jit(solution)/shard_map/ppermute | solution.py:460
  12.2 1.6 %collective-permute-done.rest_1_ = bf16[128,1536]{1,0:T(8,128)(2,1)S(1)} collective-permute-done((bf16[128,1536]{1,0:T(8,128)(2,1)}, bf16[128,1536]{1,0:T(8,128)(2,1)S(1)}, u32[]{:S(2)}, u32[]{:S(2)}) %collective-permute-start) | collective-permute-done | bytes 393248 | tf_op jit(solution)/shard_map/ppermute | solution.py:414
  13.8 1.5 %collective-permute-start.9 = (bf16[128,1536]{1,0:T(8,128)(2,1)S(1)}, bf16[128,1536]{1,0:T(8,128)(2,1)S(1)}, u32[]{:S(2)}, u32[]{:S(2)}) collective-permute-start(bf16[128,1536]{1,0:T(8,128)(2,1)S(1)} %collective-permute-done.rest_1_), channel_id=1, source_target_pairs={{0,4},{2,6},{4,0},{6,2},{8,12},{10,14},{12,8},{14,10},{16,20},{18,... | collective-permute-start | bytes 1179656 | tf_op jit(solution)/shard_map/ppermute | solution.py:21
  15.3 0.2 collective-permute-done.7.rest_2_
  15.5 3.1 %collective-permute-start.10 = (bf16[128,1536]{1,0:T(8,128)(2,1)S(1)}, bf16[128,1536]{1,0:T(8,128)(2,1)S(1)}, u32[]{:S(2)}, u32[]{:S(2)}) collective-permute-start(bf16[128,1536]{1,0:T(8,128)(2,1)S(1)} %collective-permute-done.rest_1_), channel_id=1, source_target_pairs={{0,16},{2,18},{4,20},{6,22},{16,24},{18,26},{20,28},{22,30},{24,8}... | collective-permute-start | bytes 1179656 | tf_op jit(solution)/shard_map/ppermute | solution.py:414
  18.6 1.7 %inner_rows.1 = (bf16[128,2048]{1,0:T(8,128)(2,1)S(1)}, bf16[128,1024]{1,0:T(8,128)(2,1)S(1)}) custom-call(s32[7,8,128]{2,1,0:T(8,128)S(1)} %get-tuple-element.40.facts_ref, bf16[2,128,6144]{2,1,0:T(8,128)(2,1)S(1)} %get-tuple-element.41.rows_ref), custom_call_target="tpu_custom_call" | custom-call | tf_op jit(solution)/shard_map/inner_rows/pallas_call | solution.py:476
  20.3 3.7 %collective-permute-done.8.rest_3_ = bf16[128,1536]{1,0:T(8,128)(2,1)S(1)} collective-permute-done((bf16[128,1536]{1,0:T(8,128)(2,1)S(1)}, bf16[128,1536]{1,0:T(8,128)(2,1)S(1)}, u32[]{:S(2)}, u32[]{:S(2)}) %collective-permute-start.8) | collective-permute-done | bytes 393248 | tf_op jit(solution)/shard_map/ppermute | solution.py:414
  24.0 0.0 collective-permute-done.2.halo_ref
  24.0 1.5 %collective-permute-start.11 = (bf16[128,1536]{1,0:T(8,128)(2,1)S(1)}, bf16[128,1536]{1,0:T(8,128)(2,1)S(1)}, u32[]{:S(2)}, u32[]{:S(2)}) collective-permute-start(bf16[128,1536]{1,0:T(8,128)(2,1)S(1)} %collective-permute-done.8.rest_3_), channel_id=1, source_target_pairs={{0,4},{2,6},{4,0},{6,2},{8,12},{10,14},{12,8},{14,10},{16,20},{18,... | collective-permute-start | bytes 1179656 | tf_op jit(solution)/shard_map/ppermute | solution.py:21
  25.5 1.1 %edge_rows.2 = (bf16[128,1024]{1,0:T(8,128)(2,1)S(1)}, bf16[128,512]{1,0:T(8,128)(2,1)S(1)}) custom-call(s32[7,8,128]{2,1,0:T(8,128)S(1)} %get-tuple-element.40.facts_ref, bf16[2,128,6144]{2,1,0:T(8,128)(2,1)S(1)} %get-tuple-element.41.rows_ref, bf16[128,2048]{1,0:T(8,128)(2,1)S(1)} %collective-permute-done.2.halo_ref), custom_call_target="tpu_custom_call" | custom-call | tf_op jit(solution)/shard_map/edge_rows/pallas_call | solution.py:464
  26.6 0.0 collective-permute-done.9.rest_4_
  26.6 1.1 %collective-permute-start.12 = (bf16[80,1536]{1,0:T(8,128)(2,1)S(1)}, bf16[80,1536]{1,0:T(8,128)(2,1)S(1)}, u32[]{:S(2)}, u32[]{:S(2)}) collective-permute-start(bf16[80,1536]{1,0:T(8,128)(2,1)S(1)} %slice.6), channel_id=1, source_target_pairs={{0,16},{2,18},{4,20},{6,22},{16,24},{18,26},{20,28},{22,30},{24,8}... | collective-permute-start | bytes 737288 | tf_op jit(solution)/shard_map/ppermute | solution.py:414
  27.7 0.9 %inner_project.1 = (f32[256,1536]{1,0:T(8,128)S(1)}, bf16[256,256]{1,0:T(8,128)(2,1)S(1)}) custom-call(bf16[128,2048]{1,0:T(8,128)(2,1)S(1)} %get-tuple-element.42.inner_ref, bf16[128,1024]{1,0:T(8,128)(2,1)S(1)} %collective-permute-done.6.their_ref, bf16[128,1536]{1,0:T(8,128)(2,1)S(1)} %copy-done, bf16[128,1536]{1,0:T(8,128)(2,1)S(1)} %collective-permute-done.rest_1_, ...), custom_call_target="tpu_custom_call" | custom-call | tf_op jit(solution)/shard_map/inner_project/pallas_call | solution.py:490
  28.6 3.5 %collective-permute-done.10.rest_0_.rest_5_ = bf16[128,1536]{1,0:T(8,128)(2,1)S(1)} collective-permute-done((bf16[128,1536]{1,0:T(8,128)(2,1)S(1)}, bf16[128,1536]{1,0:T(8,128)(2,1)S(1)}, u32[]{:S(2)}, u32[]{:S(2)}) %collective-permute-start.10) | collective-permute-done | bytes 393248 | tf_op jit(solution)/shard_map/ppermute | solution.py:414
  32.1 1.6 %collective-permute-start.13 = (bf16[48,1536]{1,0:T(8,128)(2,1)S(1)}, bf16[48,1536]{1,0:T(8,128)(2,1)S(1)}, u32[]{:S(2)}, u32[]{:S(2)}) collective-permute-start(bf16[48,1536]{1,0:T(8,128)(2,1)S(1)} %slice.7), channel_id=1, source_target_pairs={{0,4},{2,6},{4,0},{6,2},{8,12},{10,14},{12,8},{14,10},{16,20},{18,... | collective-permute-start | bytes 442376 | tf_op jit(solution)/shard_map/ppermute | solution.py:21
  33.6 0.0 collective-permute-done.3.halo_ref
  33.6 1.1 %edge_rows.3 = (bf16[128,1024]{1,0:T(8,128)(2,1)S(1)}, bf16[128,512]{1,0:T(8,128)(2,1)S(1)}) custom-call(s32[7,8,128]{2,1,0:T(8,128)S(1)} %get-tuple-element.40.facts_ref, bf16[2,128,6144]{2,1,0:T(8,128)(2,1)S(1)} %get-tuple-element.41.rows_ref, bf16[128,2048]{1,0:T(8,128)(2,1)S(1)} %collective-permute-done.3.halo_ref), custom_call_target="tpu_custom_call" | custom-call | tf_op jit(solution)/shard_map/edge_rows/pallas_call | solution.py:464
  34.7 0.1 collective-permute-start.5
  34.8 0.5 %collective-permute-start.4 = (bf16[128,512]{1,0:T(8,128)(2,1)S(1)}, bf16[128,512]{1,0:T(8,128)(2,1)S(1)}, u32[]{:S(2)}, u32[]{:S(2)}) collective-permute-start(bf16[128,512]{1,0:T(8,128)(2,1)S(1)} %get-tuple-element.45), channel_id=1, source_target_pairs={{0,2},{2,0},{4,6},{6,4},{8,10},{10,8},{12,14},{14,12},{16,18},{18,... | collective-permute-start | bytes 393224 | tf_op jit(solution)/shard_map/ppermute | solution.py:21
  35.3 0.6 %collective-permute-done.11.rest_1_.rest_6_ = bf16[128,1536]{1,0:T(8,128)(2,1)S(1)} collective-permute-done((bf16[128,1536]{1,0:T(8,128)(2,1)S(1)}, bf16[128,1536]{1,0:T(8,128)(2,1)S(1)}, u32[]{:S(2)}, u32[]{:S(2)}) %collective-permute-start.11) | collective-permute-done | bytes 393248 | tf_op jit(solution)/shard_map/ppermute | solution.py:21
  35.9 0.4 add_products.1.inner_total_ref
  36.2 0.0 collective-permute-done.5.refs_3_
  36.3 0.1 collective-permute-done.4.refs_2_
  36.3 0.2 arrange.1
  36.6 0.4 %project.4 = (f32[256,512]{1,0:T(8,128)S(1)}, bf16[256,512]{1,0:T(8,128)(2,1)S(1)}) custom-call(bf16[256,896]{1,0:T(8,128)(2,1)S(1)} %get-tuple-element.57.edge_ref, f32[256,1536]{1,0:T(8,128)S(1)} %add_products.1.inner_total_ref, bf16[128,1536]{1,0:T(8,128)(2,1)S(1)} %copy-done, bf16[128,1536]{1,0:T(8,128)(2,1)S(1)} %collective-permute-done.rest_1_, ...), custom_call_target="tpu_custom_call" | custom-call | tf_op jit(solution)/shard_map/project/pallas_call | solution.py:532
  37.0 0.4 collective-permute-start.17
  37.4 0.4 %project.3 = (f32[256,512]{1,0:T(8,128)S(1)}, bf16[256,512]{1,0:T(8,128)(2,1)S(1)}) custom-call(bf16[256,896]{1,0:T(8,128)(2,1)S(1)} %get-tuple-element.57.edge_ref, f32[256,1536]{1,0:T(8,128)S(1)} %add_products.1.inner_total_ref, bf16[128,1536]{1,0:T(8,128)(2,1)S(1)} %copy-done, bf16[128,1536]{1,0:T(8,128)(2,1)S(1)} %collective-permute-done.rest_1_, ...), custom_call_target="tpu_custom_call" | custom-call | tf_op jit(solution)/shard_map/project/pallas_call | solution.py:532
  37.8 0.3 collective-permute-start.16
  38.1 0.4 %project.5 = (f32[256,512]{1,0:T(8,128)S(1)}, bf16[256,512]{1,0:T(8,128)(2,1)S(1)}) custom-call(bf16[256,896]{1,0:T(8,128)(2,1)S(1)} %get-tuple-element.57.edge_ref, f32[256,1536]{1,0:T(8,128)S(1)} %add_products.1.inner_total_ref, bf16[128,1536]{1,0:T(8,128)(2,1)S(1)} %copy-done, bf16[128,1536]{1,0:T(8,128)(2,1)S(1)} %collective-permute-done.rest_1_, ...), custom_call_target="tpu_custom_call" | custom-call | tf_op jit(solution)/shard_map/project/pallas_call | solution.py:532
  38.5 0.1 collective-permute-done.13.rest_1_
  38.6 0.0 collective-permute-done.12.rest_0_
  38.7 0.3 collective-permute-start.18
  38.9 0.2 collective-permute-start.14
  39.2 0.3 collective-permute-start.15
  39.5 1.3 %collective-permute-done.15.rest_3_ = bf16[48,1536]{1,0:T(8,128)(2,1)S(1)} collective-permute-done((bf16[48,1536]{1,0:T(8,128)(2,1)S(1)}, bf16[48,1536]{1,0:T(8,128)(2,1)S(1)}, u32[]{:S(2)}, u32[]{:S(2)}) %collective-permute-start.15) | collective-permute-done | bytes 147488 | tf_op jit(solution)/shard_map/ppermute | solution.py:21
  40.8 0.0 collective-permute-done.14.rest_2_
  40.8 0.4 last_project.1.total_ref
  41.2 1.0 %finish.1 = bf16[256,1536]{1,0:T(8,128)(2,1)} custom-call(f32[256,1536]{1,0:T(8,128)S(1)} %last_project.1.total_ref, bf16[256,512]{1,0:T(8,128)(2,1)S(1)} %collective-permute-done.16.rest_0_, bf16[256,512]{1,0:T(8,128)(2,1)S(1)} %collective-permute-done.17.rest_1_, bf16[256,512]{1,0:T(8,128)(2,1)S(1)} %collective-permute-done.18.rest_2_), custom_call_target="tpu_custom_call" | custom-call | tf_op jit(solution)/shard_map/finish/pallas_call | solution.py:550
  (8 shorter events, 0.0 us)
Async XLA Ops:
  0.0 7.5 %collective-permute-start.1 = (bf16[2,128,6144]{2,1,0:T(8,128)(2,1)}, bf16[2,128,6144]{2,1,0:T(8,128)(2,1)S(1)}, u32[]{:S(2)}, u32[]{:S(2)}) collective-permute-start(bf16[2,128,6144]{2,1,0:T(8,128)(2,1)} %bitcast.1), channel_id=1, source_target_pairs={{0,2},{2,0},{4,6},{6,4},{8,10},{10,8},{12,14},{14,12},{16,18},{18,... | collective-permute-start | bytes 9437192 | tf_op jit(solution)/shard_map/ppermute | solution.py:21
  0.5 13.3 %collective-permute-start = (bf16[128,1536]{1,0:T(8,128)(2,1)}, bf16[128,1536]{1,0:T(8,128)(2,1)S(1)}, u32[]{:S(2)}, u32[]{:S(2)}) collective-permute-start(bf16[128,1536]{1,0:T(8,128)(2,1)} %rest_0_.7), channel_id=1, source_target_pairs={{0,16},{2,18},{4,20},{6,22},{16,24},{18,26},{20,28},{22,30},{24,8}... | collective-permute-start | bytes 1179656 | tf_op jit(solution)/shard_map/ppermute | solution.py:414
  4.0 11.5 %collective-permute-start.7 = (bf16[128,1536]{1,0:T(8,128)(2,1)}, bf16[128,1536]{1,0:T(8,128)(2,1)S(1)}, u32[]{:S(2)}, u32[]{:S(2)}) collective-permute-start(bf16[128,1536]{1,0:T(8,128)(2,1)} %rest_0_.7), channel_id=1, source_target_pairs={{0,4},{2,6},{4,0},{6,2},{8,12},{10,14},{12,8},{14,10},{16,20},{18,... | collective-permute-start | bytes 1179656 | tf_op jit(solution)/shard_map/ppermute | solution.py:21
  7.5 1.9 %copy-start = (bf16[128,1536]{1,0:T(8,128)(2,1)S(1)}, bf16[128,1536]{1,0:T(8,128)(2,1)}, u32[]{:S(2)}) copy-start(bf16[128,1536]{1,0:T(8,128)(2,1)} %rest_0_.7) | copy-start | bytes 1179652
  7.7 16.2 %collective-permute-start.2 = (bf16[128,2048]{1,0:T(8,128)(2,1)S(1)}, bf16[128,2048]{1,0:T(8,128)(2,1)S(1)}, u32[]{:S(2)}, u32[]{:S(2)}) collective-permute-start(bf16[128,2048]{1,0:T(8,128)(2,1)S(1)} %pack_first.1), channel_id=1, source_target_pairs={{0,1},{1,0},{2,3},{3,2},{4,5},{5,4},{6,7},{7,6},{8,9},{9,8},{10,11... | collective-permute-start | bytes 1572872 | tf_op jit(solution)/shard_map/ppermute | solution.py:460
  9.3 14.6 %collective-permute-start.8 = (bf16[128,1536]{1,0:T(8,128)(2,1)S(1)}, bf16[128,1536]{1,0:T(8,128)(2,1)S(1)}, u32[]{:S(2)}, u32[]{:S(2)}) collective-permute-start(bf16[128,1536]{1,0:T(8,128)(2,1)S(1)} %copy-done), channel_id=1, source_target_pairs={{0,8},{2,10},{4,12},{6,14},{16,0},{18,2},{20,4},{22,6},{24,16},{26... | collective-permute-start | bytes 1179656 | tf_op jit(solution)/shard_map/ppermute | solution.py:414
  11.4 22.2 %collective-permute-start.3 = (bf16[128,2048]{1,0:T(8,128)(2,1)S(1)}, bf16[128,2048]{1,0:T(8,128)(2,1)S(1)}, u32[]{:S(2)}, u32[]{:S(2)}) collective-permute-start(bf16[128,2048]{1,0:T(8,128)(2,1)S(1)} %get-tuple-element.38), channel_id=1, source_target_pairs={{0,1},{1,0},{2,3},{3,2},{4,5},{5,4},{6,7},{7,6},{8,9},{9,8},{10,11... | collective-permute-start | bytes 1572872 | tf_op jit(solution)/shard_map/ppermute | solution.py:460
  13.8 12.8 %collective-permute-start.9 = (bf16[128,1536]{1,0:T(8,128)(2,1)S(1)}, bf16[128,1536]{1,0:T(8,128)(2,1)S(1)}, u32[]{:S(2)}, u32[]{:S(2)}) collective-permute-start(bf16[128,1536]{1,0:T(8,128)(2,1)S(1)} %collective-permute-done.rest_1_), channel_id=1, source_target_pairs={{0,4},{2,6},{4,0},{6,2},{8,12},{10,14},{12,8},{14,10},{16,20},{18,... | collective-permute-start | bytes 1179656 | tf_op jit(solution)/shard_map/ppermute | solution.py:21
  15.5 16.5 %collective-permute-start.10 = (bf16[128,1536]{1,0:T(8,128)(2,1)S(1)}, bf16[128,1536]{1,0:T(8,128)(2,1)S(1)}, u32[]{:S(2)}, u32[]{:S(2)}) collective-permute-start(bf16[128,1536]{1,0:T(8,128)(2,1)S(1)} %collective-permute-done.rest_1_), channel_id=1, source_target_pairs={{0,16},{2,18},{4,20},{6,22},{16,24},{18,26},{20,28},{22,30},{24,8}... | collective-permute-start | bytes 1179656 | tf_op jit(solution)/shard_map/ppermute | solution.py:414
  24.0 3.7 %collective-permute-start.6 = (bf16[128,1024]{1,0:T(8,128)(2,1)S(1)}, bf16[128,1024]{1,0:T(8,128)(2,1)S(1)}, u32[]{:S(2)}, u32[]{:S(2)}) collective-permute-start(bf16[128,1024]{1,0:T(8,128)(2,1)S(1)} %get-tuple-element.47), channel_id=1, source_target_pairs={{0,2},{2,0},{4,6},{6,4},{8,10},{10,8},{12,14},{14,12},{16,18},{18,... | collective-permute-start | bytes 786440 | tf_op jit(solution)/shard_map/ppermute | solution.py:21
  24.0 11.9 %collective-permute-start.11 = (bf16[128,1536]{1,0:T(8,128)(2,1)S(1)}, bf16[128,1536]{1,0:T(8,128)(2,1)S(1)}, u32[]{:S(2)}, u32[]{:S(2)}) collective-permute-start(bf16[128,1536]{1,0:T(8,128)(2,1)S(1)} %collective-permute-done.8.rest_3_), channel_id=1, source_target_pairs={{0,4},{2,6},{4,0},{6,2},{8,12},{10,14},{12,8},{14,10},{16,20},{18,... | collective-permute-start | bytes 1179656 | tf_op jit(solution)/shard_map/ppermute | solution.py:21
  26.6 12.0 %collective-permute-start.12 = (bf16[80,1536]{1,0:T(8,128)(2,1)S(1)}, bf16[80,1536]{1,0:T(8,128)(2,1)S(1)}, u32[]{:S(2)}, u32[]{:S(2)}) collective-permute-start(bf16[80,1536]{1,0:T(8,128)(2,1)S(1)} %slice.6), channel_id=1, source_target_pairs={{0,16},{2,18},{4,20},{6,22},{16,24},{18,26},{20,28},{22,30},{24,8}... | collective-permute-start | bytes 737288 | tf_op jit(solution)/shard_map/ppermute | solution.py:414
  32.1 6.6 %collective-permute-start.13 = (bf16[48,1536]{1,0:T(8,128)(2,1)S(1)}, bf16[48,1536]{1,0:T(8,128)(2,1)S(1)}, u32[]{:S(2)}, u32[]{:S(2)}) collective-permute-start(bf16[48,1536]{1,0:T(8,128)(2,1)S(1)} %slice.7), channel_id=1, source_target_pairs={{0,4},{2,6},{4,0},{6,2},{8,12},{10,14},{12,8},{14,10},{16,20},{18,... | collective-permute-start | bytes 442376 | tf_op jit(solution)/shard_map/ppermute | solution.py:21
  34.7 1.5 %collective-permute-start.5 = (bf16[128,512]{1,0:T(8,128)(2,1)S(1)}, bf16[128,512]{1,0:T(8,128)(2,1)S(1)}, u32[]{:S(2)}, u32[]{:S(2)}) collective-permute-start(bf16[128,512]{1,0:T(8,128)(2,1)S(1)} %get-tuple-element.46), channel_id=1, source_target_pairs={{0,2},{2,0},{4,6},{6,4},{8,10},{10,8},{12,14},{14,12},{16,18},{18,... | collective-permute-start | bytes 393224 | tf_op jit(solution)/shard_map/ppermute | solution.py:21
  34.8 1.5 %collective-permute-start.4 = (bf16[128,512]{1,0:T(8,128)(2,1)S(1)}, bf16[128,512]{1,0:T(8,128)(2,1)S(1)}, u32[]{:S(2)}, u32[]{:S(2)}) collective-permute-start(bf16[128,512]{1,0:T(8,128)(2,1)S(1)} %get-tuple-element.45), channel_id=1, source_target_pairs={{0,2},{2,0},{4,6},{6,4},{8,10},{10,8},{12,14},{14,12},{16,18},{18,... | collective-permute-start | bytes 393224 | tf_op jit(solution)/shard_map/ppermute | solution.py:21
  37.0 4.1 %collective-permute-start.17 = (bf16[256,512]{1,0:T(8,128)(2,1)S(1)}, bf16[256,512]{1,0:T(8,128)(2,1)S(1)}, u32[]{:S(2)}, u32[]{:S(2)}) collective-permute-start(bf16[256,512]{1,0:T(8,128)(2,1)S(1)} %get-tuple-element.62), channel_id=1, source_target_pairs={{0,2},{2,0},{4,6},{6,4},{8,10},{10,8},{12,14},{14,12},{16,18},{18,... | collective-permute-start | bytes 786440 | tf_op jit(solution)/shard_map/ppermute | solution.py:21
  37.8 3.3 %collective-permute-start.16 = (bf16[256,512]{1,0:T(8,128)(2,1)S(1)}, bf16[256,512]{1,0:T(8,128)(2,1)S(1)}, u32[]{:S(2)}, u32[]{:S(2)}) collective-permute-start(bf16[256,512]{1,0:T(8,128)(2,1)S(1)} %get-tuple-element.61), channel_id=1, source_target_pairs={{0,2},{2,0},{4,6},{6,4},{8,10},{10,8},{12,14},{14,12},{16,18},{18,... | collective-permute-start | bytes 786440 | tf_op jit(solution)/shard_map/ppermute | solution.py:21
  38.7 2.5 %collective-permute-start.18 = (bf16[256,512]{1,0:T(8,128)(2,1)S(1)}, bf16[256,512]{1,0:T(8,128)(2,1)S(1)}, u32[]{:S(2)}, u32[]{:S(2)}) collective-permute-start(bf16[256,512]{1,0:T(8,128)(2,1)S(1)} %get-tuple-element.64), channel_id=1, source_target_pairs={{0,2},{2,0},{4,6},{6,4},{8,10},{10,8},{12,14},{14,12},{16,18},{18,... | collective-permute-start | bytes 786440 | tf_op jit(solution)/shard_map/ppermute | solution.py:21
  38.9 1.8 %collective-permute-start.14 = (bf16[80,1536]{1,0:T(8,128)(2,1)S(1)}, bf16[80,1536]{1,0:T(8,128)(2,1)S(1)}, u32[]{:S(2)}, u32[]{:S(2)}) collective-permute-start(bf16[80,1536]{1,0:T(8,128)(2,1)S(1)} %collective-permute-done.12.rest_0_), channel_id=1, source_target_pairs={{0,2},{2,0},{4,6},{6,4},{8,10},{10,8},{12,14},{14,12},{16,18},{18,... | collective-permute-start | bytes 737288 | tf_op jit(solution)/shard_map/ppermute | solution.py:21
  39.2 1.6 %collective-permute-start.15 = (bf16[48,1536]{1,0:T(8,128)(2,1)S(1)}, bf16[48,1536]{1,0:T(8,128)(2,1)S(1)}, u32[]{:S(2)}, u32[]{:S(2)}) collective-permute-start(bf16[48,1536]{1,0:T(8,128)(2,1)S(1)} %collective-permute-done.13.rest_1_), channel_id=1, source_target_pairs={{0,2},{2,0},{4,6},{6,4},{8,10},{10,8},{12,14},{14,12},{16,18},{18,... | collective-permute-start | bytes 442376 | tf_op jit(solution)/shard_map/ppermute | solution.py:21

commit v2 on v1

--- a/solution.py
+++ b/solution.py
@@ -343,30 +343,23 @@
         their_total_ref[block:, here] = edge[block:].astype(jnp.bfloat16)
 
 
-def last_project_kernel(features_ref, *rest):
-    shard_refs, total_refs, out_ref = rest[:4], rest[4:-1], rest[-1]
-    first = 0
-    for total_ref in total_refs:
-        columns = slice(first, first + total_ref.shape[1])
-        weight = jnp.concatenate([ref[:, columns] for ref in shard_refs], axis=0)
-        out_ref[:, columns] = total_ref[...] + jnp.dot(
-            features_ref[...], weight, preferred_element_type=jnp.float32
-        )
-        first += total_ref.shape[1]
-
-
-def finish_kernel(total_ref, *rest):
-    more_refs, (out_ref, held, sems) = rest[:-3], rest[-3:]
+def finish_kernel(parts, features_ref, *rest):
+    operands, (out_ref, held, sems) = rest[:-3], rest[-3:]
+    shard_refs, sum_refs = operands[: -2 * parts], operands[-2 * parts :]
+    total_refs, more_refs = sum_refs[:parts], sum_refs[parts:]
     block = out_ref.shape[0] // 2
     ctx = lax.axis_index("ctx")
     copies = []
     for which, place in ((0, ctx), (1, 1 - ctx)):
         rows = slice(which * block, (which + 1) * block)
         first = 0
-        for more_ref in more_refs:
-            columns = slice(first, first + more_ref.shape[1])
-            held[rows, columns] = (total_ref[rows, columns] + more_ref[rows]).astype(jnp.bfloat16)
-            first += more_ref.shape[1]
+        for total_ref, more_ref in zip(total_refs, more_refs, strict=True):
+            columns = slice(first, first + total_ref.shape[1])
+            weight = jnp.concatenate([ref[:, columns] for ref in shard_refs], axis=0)
+            total = jnp.dot(features_ref[rows], weight, preferred_element_type=jnp.float32)
+            total = total + (total_ref[rows] + more_ref[rows])
+            held[rows, columns] = total.astype(jnp.bfloat16)
+            first += total_ref.shape[1]
         target = out_ref.at[pl.ds(pl.multiple_of(place * block, block), block)]
         copies.append(pltpu.make_async_copy(held.at[rows], target, sems.at[which]))
         copies[-1].start()
@@ -540,21 +533,14 @@
         if part == parts - 1:
             their_total = after(their_total, *last)
         mores.append(to_core(their_total))
-    total = call(
-        last_project_kernel,
-        "last_project",
-        (local_rows, width),
-        [VMEM()] * (1 + 2 * len(last) + parts),
-        dtypes=[jnp.float32],
-    )(last_features, *last, *last_swapped, *own_totals)
     return call(
-        finish_kernel,
+        functools.partial(finish_kernel, parts),
         "finish",
         (local_rows, width),
-        [VMEM()] * (1 + parts),
+        [VMEM()] * (1 + 2 * len(last) + 2 * parts),
         scratch=[pltpu.VMEM((local_rows, width), bf16), pltpu.SemaphoreType.DMA((2,))],
         out_spec=HBM(),
-    )(total, *mores)
+    )(last_features, *last, *last_swapped, *own_totals, *mores)
 
 
 def body(projections, block_source, clip_ids, out_weight):

time: 42.3 us -> 42.1 us (level)
    pallas_call x2 -> x1, Pallas kernels: 1.33 us -> 1.17 us  [body_edge(): call(functools.partial(finish_kernel, parts), 'finish', (local_rows, widt...]
  transfers between devices with their start and end apart: 19 -> 19, of which waited for: 8 -> 8; matrix products, arithmetic and copies ran while one was open for 0% -> 0% of each run, Pallas kernels for 24% -> 23%
where the time goes in v2:
time: 42.1 us; the launch traced here: 41.9 us
  starting transfers between devices  20 us (48%)
  waiting for transfers between devices  11 us (26%)
  Pallas kernels  10.7 us (25%)
    ppermute x4, starting transfers between devices, around(): lax.ppermute(value, 'dp', [(4 * here + rest, 4 * there + rest) for here,...  9.15 us
    ppermute x4, waiting for transfers between devices, around(): lax.ppermute(value, 'dp', [(4 * here + rest, 4 * there + rest) for here,...  8.74 us
    ppermute x13, starting transfers between devices, partner(): return lax.ppermute(value, axis, pairs)  8.49 us
    ppermute x2, starting transfers between devices, body_edge(): halos = [lax.ppermute(part, 'ctx', [(0, 1), (1, 0)]) for part in packed]  2.33 us
    ppermute x13, waiting for transfers between devices, partner(): return lax.ppermute(value, axis, pairs)  2.3 us
    pallas_call x2, Pallas kernels, edge_rows(): call(functools.partial(edge_kernel, sum(part_heads[:part])), 'edge_rows',...  2.24 us
    pallas_call x1, Pallas kernels, body_edge(): call(stage_kernel, 'stage', [own.shape, (7, 8, 128)], [HBM()] * 3, dtypes...  1.91 us
    pallas_call x1, Pallas kernels, body_edge(): call(inner_kernel, 'inner_rows', [(block_rows, features), (block_rows, fe...  1.73 us
  transfers between devices with their start and end apart: 19, of which 8 were waited for; matrix products, arithmetic and copies ran while one was open for 0% of the time, Pallas kernels for 23%

profile of v2, /device:TPU:0, one launch (start us, length us, event | category | flops | bytes accessed | tf_op | source)
XLA Modules:
  0.0 41.9 jit_solution(8388955622528357078)
XLA Ops:
  0.0 0.5 %collective-permute-start.1 = (bf16[2,128,6144]{2,1,0:T(8,128)(2,1)}, bf16[2,128,6144]{2,1,0:T(8,128)(2,1)S(1)}, u32[]{:S(2)}, u32[]{:S(2)}) collective-permute-start(bf16[2,128,6144]{2,1,0:T(8,128)(2,1)} %bitcast.1), channel_id=1, source_target_pairs={{0,2},{2,0},{4,6},{6,4},{8,10},{10,8},{12,14},{14,12},{16,18},{18,... | collective-permute-start | bytes 9437192 | tf_op jit(solution)/shard_map/ppermute | solution.py:21
  0.5 3.6 %collective-permute-start = (bf16[128,1536]{1,0:T(8,128)(2,1)}, bf16[128,1536]{1,0:T(8,128)(2,1)S(1)}, u32[]{:S(2)}, u32[]{:S(2)}) collective-permute-start(bf16[128,1536]{1,0:T(8,128)(2,1)} %rest_0_.7), channel_id=1, source_target_pairs={{0,16},{2,18},{4,20},{6,22},{16,24},{18,26},{20,28},{22,30},{24,8}... | collective-permute-start | bytes 1179656 | tf_op jit(solution)/shard_map/ppermute | solution.py:407
  4.0 1.5 %collective-permute-start.7 = (bf16[128,1536]{1,0:T(8,128)(2,1)}, bf16[128,1536]{1,0:T(8,128)(2,1)S(1)}, u32[]{:S(2)}, u32[]{:S(2)}) collective-permute-start(bf16[128,1536]{1,0:T(8,128)(2,1)} %rest_0_.7), channel_id=1, source_target_pairs={{0,4},{2,6},{4,0},{6,2},{8,12},{10,14},{12,8},{14,10},{16,20},{18,... | collective-permute-start | bytes 1179656 | tf_op jit(solution)/shard_map/ppermute | solution.py:21
  5.5 1.9 %stage.1 = (bf16[2,128,6144]{2,1,0:T(8,128)(2,1)S(1)}, s32[7,8,128]{2,1,0:T(8,128)S(1)}) custom-call(s32[1,1,2]{2,1,0:T(1,128)} %sources.1, s32[1,4]{1,0:T(1,128)} %clips.1, bf16[2,128,6144]{2,1,0:T(8,128)(2,1)} %bitcast.2), custom_call_target="tpu_custom_call" | custom-call | tf_op jit(solution)/shard_map/stage/pallas_call | solution.py:425
  7.5 0.0 collective-permute-done.1.partner_ref
  7.5 0.0 copy-start
  7.5 0.2 pack_first.1
  7.7 1.6 %collective-permute-start.2 = (bf16[128,2048]{1,0:T(8,128)(2,1)S(1)}, bf16[128,2048]{1,0:T(8,128)(2,1)S(1)}, u32[]{:S(2)}, u32[]{:S(2)}) collective-permute-start(bf16[128,2048]{1,0:T(8,128)(2,1)S(1)} %pack_first.1), channel_id=1, source_target_pairs={{0,1},{1,0},{2,3},{3,2},{4,5},{5,4},{6,7},{7,6},{8,9},{9,8},{10,11... | collective-permute-start | bytes 1572872 | tf_op jit(solution)/shard_map/ppermute | solution.py:453
  9.3 1.4 %collective-permute-start.8 = (bf16[128,1536]{1,0:T(8,128)(2,1)S(1)}, bf16[128,1536]{1,0:T(8,128)(2,1)S(1)}, u32[]{:S(2)}, u32[]{:S(2)}) collective-permute-start(bf16[128,1536]{1,0:T(8,128)(2,1)S(1)} %copy-done), channel_id=1, source_target_pairs={{0,8},{2,10},{4,12},{6,14},{16,0},{18,2},{20,4},{22,6},{24,16},{26... | collective-permute-start | bytes 1179656 | tf_op jit(solution)/shard_map/ppermute | solution.py:407
  10.7 0.7 %pack.1 = (bf16[2,128,6144]{2,1,0:T(8,128)(2,1)S(1)}, bf16[128,2048]{1,0:T(8,128)(2,1)S(1)}) custom-call(s32[7,8,128]{2,1,0:T(8,128)S(1)} %get-tuple-element.40.facts_ref, bf16[2,128,6144]{2,1,0:T(8,128)(2,1)S(1)} %get-tuple-element.36.own_ref, bf16[2,128,6144]{2,1,0:T(8,128)(2,1)S(1)} %collective-permute-done.1.partner_ref), custom_call_target="tpu_custom_call" | custom-call | tf_op jit(solution)/shard_map/pack/pallas_call | solution.py:445
  11.4 0.7 %collective-permute-start.3 = (bf16[128,2048]{1,0:T(8,128)(2,1)S(1)}, bf16[128,2048]{1,0:T(8,128)(2,1)S(1)}, u32[]{:S(2)}, u32[]{:S(2)}) collective-permute-start(bf16[128,2048]{1,0:T(8,128)(2,1)S(1)} %get-tuple-element.38), channel_id=1, source_target_pairs={{0,1},{1,0},{2,3},{3,2},{4,5},{5,4},{6,7},{7,6},{8,9},{9,8},{10,11... | collective-permute-start | bytes 1572872 | tf_op jit(solution)/shard_map/ppermute | solution.py:453
  12.2 1.6 %collective-permute-done.rest_1_ = bf16[128,1536]{1,0:T(8,128)(2,1)S(1)} collective-permute-done((bf16[128,1536]{1,0:T(8,128)(2,1)}, bf16[128,1536]{1,0:T(8,128)(2,1)S(1)}, u32[]{:S(2)}, u32[]{:S(2)}) %collective-permute-start) | collective-permute-done | bytes 393248 | tf_op jit(solution)/shard_map/ppermute | solution.py:407
  13.8 1.5 %collective-permute-start.9 = (bf16[128,1536]{1,0:T(8,128)(2,1)S(1)}, bf16[128,1536]{1,0:T(8,128)(2,1)S(1)}, u32[]{:S(2)}, u32[]{:S(2)}) collective-permute-start(bf16[128,1536]{1,0:T(8,128)(2,1)S(1)} %collective-permute-done.rest_1_), channel_id=1, source_target_pairs={{0,4},{2,6},{4,0},{6,2},{8,12},{10,14},{12,8},{14,10},{16,20},{18,... | collective-permute-start | bytes 1179656 | tf_op jit(solution)/shard_map/ppermute | solution.py:21
  15.3 0.2 collective-permute-done.7.rest_2_
  15.5 3.1 %collective-permute-start.10 = (bf16[128,1536]{1,0:T(8,128)(2,1)S(1)}, bf16[128,1536]{1,0:T(8,128)(2,1)S(1)}, u32[]{:S(2)}, u32[]{:S(2)}) collective-permute-start(bf16[128,1536]{1,0:T(8,128)(2,1)S(1)} %collective-permute-done.rest_1_), channel_id=1, source_target_pairs={{0,16},{2,18},{4,20},{6,22},{16,24},{18,26},{20,28},{22,30},{24,8}... | collective-permute-start | bytes 1179656 | tf_op jit(solution)/shard_map/ppermute | solution.py:407
  18.6 1.7 %inner_rows.1 = (bf16[128,2048]{1,0:T(8,128)(2,1)S(1)}, bf16[128,1024]{1,0:T(8,128)(2,1)S(1)}) custom-call(s32[7,8,128]{2,1,0:T(8,128)S(1)} %get-tuple-element.40.facts_ref, bf16[2,128,6144]{2,1,0:T(8,128)(2,1)S(1)} %get-tuple-element.41.rows_ref), custom_call_target="tpu_custom_call" | custom-call | tf_op jit(solution)/shard_map/inner_rows/pallas_call | solution.py:469
  20.3 3.7 %collective-permute-done.8.rest_3_ = bf16[128,1536]{1,0:T(8,128)(2,1)S(1)} collective-permute-done((bf16[128,1536]{1,0:T(8,128)(2,1)S(1)}, bf16[128,1536]{1,0:T(8,128)(2,1)S(1)}, u32[]{:S(2)}, u32[]{:S(2)}) %collective-permute-start.8) | collective-permute-done | bytes 393248 | tf_op jit(solution)/shard_map/ppermute | solution.py:407
  24.0 0.0 collective-permute-start.6
  24.0 0.0 collective-permute-done.2.halo_ref
  24.0 1.5 %collective-permute-start.11 = (bf16[128,1536]{1,0:T(8,128)(2,1)S(1)}, bf16[128,1536]{1,0:T(8,128)(2,1)S(1)}, u32[]{:S(2)}, u32[]{:S(2)}) collective-permute-start(bf16[128,1536]{1,0:T(8,128)(2,1)S(1)} %collective-permute-done.8.rest_3_), channel_id=1, source_target_pairs={{0,4},{2,6},{4,0},{6,2},{8,12},{10,14},{12,8},{14,10},{16,20},{18,... | collective-permute-start | bytes 1179656 | tf_op jit(solution)/shard_map/ppermute | solution.py:21
  25.5 1.1 %edge_rows.2 = (bf16[128,1024]{1,0:T(8,128)(2,1)S(1)}, bf16[128,512]{1,0:T(8,128)(2,1)S(1)}) custom-call(s32[7,8,128]{2,1,0:T(8,128)S(1)} %get-tuple-element.40.facts_ref, bf16[2,128,6144]{2,1,0:T(8,128)(2,1)S(1)} %get-tuple-element.41.rows_ref, bf16[128,2048]{1,0:T(8,128)(2,1)S(1)} %collective-permute-done.2.halo_ref), custom_call_target="tpu_custom_call" | custom-call | tf_op jit(solution)/shard_map/edge_rows/pallas_call | solution.py:457
  26.6 0.0 collective-permute-done.9.rest_4_
  26.6 1.1 %collective-permute-start.12 = (bf16[80,1536]{1,0:T(8,128)(2,1)S(1)}, bf16[80,1536]{1,0:T(8,128)(2,1)S(1)}, u32[]{:S(2)}, u32[]{:S(2)}) collective-permute-start(bf16[80,1536]{1,0:T(8,128)(2,1)S(1)} %slice.6), channel_id=1, source_target_pairs={{0,16},{2,18},{4,20},{6,22},{16,24},{18,26},{20,28},{22,30},{24,8}... | collective-permute-start | bytes 737288 | tf_op jit(solution)/shard_map/ppermute | solution.py:407
  27.7 0.9 %inner_project.1 = (f32[256,1536]{1,0:T(8,128)S(1)}, bf16[256,256]{1,0:T(8,128)(2,1)S(1)}) custom-call(bf16[128,2048]{1,0:T(8,128)(2,1)S(1)} %get-tuple-element.42.inner_ref, bf16[128,1024]{1,0:T(8,128)(2,1)S(1)} %collective-permute-done.6.their_ref, bf16[128,1536]{1,0:T(8,128)(2,1)S(1)} %copy-done, bf16[128,1536]{1,0:T(8,128)(2,1)S(1)} %collective-permute-done.rest_1_, ...), custom_call_target="tpu_custom_call" | custom-call | tf_op jit(solution)/shard_map/inner_project/pallas_call | solution.py:483
  28.6 3.5 %collective-permute-done.10.rest_0_.rest_5_ = bf16[128,1536]{1,0:T(8,128)(2,1)S(1)} collective-permute-done((bf16[128,1536]{1,0:T(8,128)(2,1)S(1)}, bf16[128,1536]{1,0:T(8,128)(2,1)S(1)}, u32[]{:S(2)}, u32[]{:S(2)}) %collective-permute-start.10) | collective-permute-done | bytes 393248 | tf_op jit(solution)/shard_map/ppermute | solution.py:407
  32.1 1.6 %collective-permute-start.13 = (bf16[48,1536]{1,0:T(8,128)(2,1)S(1)}, bf16[48,1536]{1,0:T(8,128)(2,1)S(1)}, u32[]{:S(2)}, u32[]{:S(2)}) collective-permute-start(bf16[48,1536]{1,0:T(8,128)(2,1)S(1)} %slice.7), channel_id=1, source_target_pairs={{0,4},{2,6},{4,0},{6,2},{8,12},{10,14},{12,8},{14,10},{16,20},{18,... | collective-permute-start | bytes 442376 | tf_op jit(solution)/shard_map/ppermute | solution.py:21
  33.6 0.0 collective-permute-done.3.halo_ref
  33.6 1.1 %edge_rows.3 = (bf16[128,1024]{1,0:T(8,128)(2,1)S(1)}, bf16[128,512]{1,0:T(8,128)(2,1)S(1)}) custom-call(s32[7,8,128]{2,1,0:T(8,128)S(1)} %get-tuple-element.40.facts_ref, bf16[2,128,6144]{2,1,0:T(8,128)(2,1)S(1)} %get-tuple-element.41.rows_ref, bf16[128,2048]{1,0:T(8,128)(2,1)S(1)} %collective-permute-done.3.halo_ref), custom_call_target="tpu_custom_call" | custom-call | tf_op jit(solution)/shard_map/edge_rows/pallas_call | solution.py:457
  34.7 0.1 collective-permute-start.5
  34.8 0.5 %collective-permute-start.4 = (bf16[128,512]{1,0:T(8,128)(2,1)S(1)}, bf16[128,512]{1,0:T(8,128)(2,1)S(1)}, u32[]{:S(2)}, u32[]{:S(2)}) collective-permute-start(bf16[128,512]{1,0:T(8,128)(2,1)S(1)} %get-tuple-element.45), channel_id=1, source_target_pairs={{0,2},{2,0},{4,6},{6,4},{8,10},{10,8},{12,14},{14,12},{16,18},{18,... | collective-permute-start | bytes 393224 | tf_op jit(solution)/shard_map/ppermute | solution.py:21
  35.3 0.6 %collective-permute-done.11.rest_1_.rest_6_ = bf16[128,1536]{1,0:T(8,128)(2,1)S(1)} collective-permute-done((bf16[128,1536]{1,0:T(8,128)(2,1)S(1)}, bf16[128,1536]{1,0:T(8,128)(2,1)S(1)}, u32[]{:S(2)}, u32[]{:S(2)}) %collective-permute-start.11) | collective-permute-done | bytes 393248 | tf_op jit(solution)/shard_map/ppermute | solution.py:21
  35.9 0.4 add_products.1.inner_total_ref
  36.2 0.0 collective-permute-done.5.refs_3_
  36.3 0.1 collective-permute-done.4.refs_2_
  36.3 0.2 arrange.1
  36.6 0.4 %project.4 = (f32[256,512]{1,0:T(8,128)S(1)}, bf16[256,512]{1,0:T(8,128)(2,1)S(1)}) custom-call(bf16[256,896]{1,0:T(8,128)(2,1)S(1)} %get-tuple-element.57.edge_ref, f32[256,1536]{1,0:T(8,128)S(1)} %add_products.1.inner_total_ref, bf16[128,1536]{1,0:T(8,128)(2,1)S(1)} %copy-done, bf16[128,1536]{1,0:T(8,128)(2,1)S(1)} %collective-permute-done.rest_1_, ...), custom_call_target="tpu_custom_call" | custom-call | tf_op jit(solution)/shard_map/project/pallas_call | solution.py:525
  37.0 0.4 collective-permute-start.17
  37.4 0.4 %project.3 = (f32[256,512]{1,0:T(8,128)S(1)}, bf16[256,512]{1,0:T(8,128)(2,1)S(1)}) custom-call(bf16[256,896]{1,0:T(8,128)(2,1)S(1)} %get-tuple-element.57.edge_ref, f32[256,1536]{1,0:T(8,128)S(1)} %add_products.1.inner_total_ref, bf16[128,1536]{1,0:T(8,128)(2,1)S(1)} %copy-done, bf16[128,1536]{1,0:T(8,128)(2,1)S(1)} %collective-permute-done.rest_1_, ...), custom_call_target="tpu_custom_call" | custom-call | tf_op jit(solution)/shard_map/project/pallas_call | solution.py:525
  37.8 0.3 collective-permute-start.16
  38.1 0.4 %project.5 = (f32[256,512]{1,0:T(8,128)S(1)}, bf16[256,512]{1,0:T(8,128)(2,1)S(1)}) custom-call(bf16[256,896]{1,0:T(8,128)(2,1)S(1)} %get-tuple-element.57.edge_ref, f32[256,1536]{1,0:T(8,128)S(1)} %add_products.1.inner_total_ref, bf16[128,1536]{1,0:T(8,128)(2,1)S(1)} %copy-done, bf16[128,1536]{1,0:T(8,128)(2,1)S(1)} %collective-permute-done.rest_1_, ...), custom_call_target="tpu_custom_call" | custom-call | tf_op jit(solution)/shard_map/project/pallas_call | solution.py:525
  38.5 0.1 collective-permute-done.13.rest_1_
  38.6 0.0 collective-permute-done.12.rest_0_
  38.7 0.3 collective-permute-start.18
  38.9 0.2 collective-permute-start.14
  39.2 0.3 collective-permute-start.15
  39.5 1.3 %collective-permute-done.15.rest_3_ = bf16[48,1536]{1,0:T(8,128)(2,1)S(1)} collective-permute-done((bf16[48,1536]{1,0:T(8,128)(2,1)S(1)}, bf16[48,1536]{1,0:T(8,128)(2,1)S(1)}, u32[]{:S(2)}, u32[]{:S(2)}) %collective-permute-start.15) | collective-permute-done | bytes 147488 | tf_op jit(solution)/shard_map/ppermute | solution.py:21
  40.8 0.0 collective-permute-done.18.rest_9_
  40.8 1.2 %finish.1 = bf16[256,1536]{1,0:T(8,128)(2,1)} custom-call(bf16[256,256]{1,0:T(8,128)(2,1)S(1)} %get-tuple-element.55.features_ref, bf16[80,1536]{1,0:T(8,128)(2,1)S(1)} %collective-permute-done.12.rest_0_, bf16[48,1536]{1,0:T(8,128)(2,1)S(1)} %collective-permute-done.13.rest_1_, bf16[80,1536]{1,0:T(8,128)(2,1)S(1)} %collective-permute-done.14.rest_2_, ...), custom_call_target="tpu_custom_call" | custom-call | tf_op jit(solution)/shard_map/finish/pallas_call | solution.py:536
  (7 shorter events, 0.0 us)
Async XLA Ops:
  0.0 7.5 %collective-permute-start.1 = (bf16[2,128,6144]{2,1,0:T(8,128)(2,1)}, bf16[2,128,6144]{2,1,0:T(8,128)(2,1)S(1)}, u32[]{:S(2)}, u32[]{:S(2)}) collective-permute-start(bf16[2,128,6144]{2,1,0:T(8,128)(2,1)} %bitcast.1), channel_id=1, source_target_pairs={{0,2},{2,0},{4,6},{6,4},{8,10},{10,8},{12,14},{14,12},{16,18},{18,... | collective-permute-start | bytes 9437192 | tf_op jit(solution)/shard_map/ppermute | solution.py:21
  0.5 13.3 %collective-permute-start = (bf16[128,1536]{1,0:T(8,128)(2,1)}, bf16[128,1536]{1,0:T(8,128)(2,1)S(1)}, u32[]{:S(2)}, u32[]{:S(2)}) collective-permute-start(bf16[128,1536]{1,0:T(8,128)(2,1)} %rest_0_.7), channel_id=1, source_target_pairs={{0,16},{2,18},{4,20},{6,22},{16,24},{18,26},{20,28},{22,30},{24,8}... | collective-permute-start | bytes 1179656 | tf_op jit(solution)/shard_map/ppermute | solution.py:407
  4.0 11.5 %collective-permute-start.7 = (bf16[128,1536]{1,0:T(8,128)(2,1)}, bf16[128,1536]{1,0:T(8,128)(2,1)S(1)}, u32[]{:S(2)}, u32[]{:S(2)}) collective-permute-start(bf16[128,1536]{1,0:T(8,128)(2,1)} %rest_0_.7), channel_id=1, source_target_pairs={{0,4},{2,6},{4,0},{6,2},{8,12},{10,14},{12,8},{14,10},{16,20},{18,... | collective-permute-start | bytes 1179656 | tf_op jit(solution)/shard_map/ppermute | solution.py:21
  7.5 1.9 %copy-start = (bf16[128,1536]{1,0:T(8,128)(2,1)S(1)}, bf16[128,1536]{1,0:T(8,128)(2,1)}, u32[]{:S(2)}) copy-start(bf16[128,1536]{1,0:T(8,128)(2,1)} %rest_0_.7) | copy-start | bytes 1179652
  7.7 16.2 %collective-permute-start.2 = (bf16[128,2048]{1,0:T(8,128)(2,1)S(1)}, bf16[128,2048]{1,0:T(8,128)(2,1)S(1)}, u32[]{:S(2)}, u32[]{:S(2)}) collective-permute-start(bf16[128,2048]{1,0:T(8,128)(2,1)S(1)} %pack_first.1), channel_id=1, source_target_pairs={{0,1},{1,0},{2,3},{3,2},{4,5},{5,4},{6,7},{7,6},{8,9},{9,8},{10,11... | collective-permute-start | bytes 1572872 | tf_op jit(solution)/shard_map/ppermute | solution.py:453
  9.3 14.6 %collective-permute-start.8 = (bf16[128,1536]{1,0:T(8,128)(2,1)S(1)}, bf16[128,1536]{1,0:T(8,128)(2,1)S(1)}, u32[]{:S(2)}, u32[]{:S(2)}) collective-permute-start(bf16[128,1536]{1,0:T(8,128)(2,1)S(1)} %copy-done), channel_id=1, source_target_pairs={{0,8},{2,10},{4,12},{6,14},{16,0},{18,2},{20,4},{22,6},{24,16},{26... | collective-permute-start | bytes 1179656 | tf_op jit(solution)/shard_map/ppermute | solution.py:407
  11.4 22.2 %collective-permute-start.3 = (bf16[128,2048]{1,0:T(8,128)(2,1)S(1)}, bf16[128,2048]{1,0:T(8,128)(2,1)S(1)}, u32[]{:S(2)}, u32[]{:S(2)}) collective-permute-start(bf16[128,2048]{1,0:T(8,128)(2,1)S(1)} %get-tuple-element.38), channel_id=1, source_target_pairs={{0,1},{1,0},{2,3},{3,2},{4,5},{5,4},{6,7},{7,6},{8,9},{9,8},{10,11... | collective-permute-start | bytes 1572872 | tf_op jit(solution)/shard_map/ppermute | solution.py:453
  13.8 12.8 %collective-permute-start.9 = (bf16[128,1536]{1,0:T(8,128)(2,1)S(1)}, bf16[128,1536]{1,0:T(8,128)(2,1)S(1)}, u32[]{:S(2)}, u32[]{:S(2)}) collective-permute-start(bf16[128,1536]{1,0:T(8,128)(2,1)S(1)} %collective-permute-done.rest_1_), channel_id=1, source_target_pairs={{0,4},{2,6},{4,0},{6,2},{8,12},{10,14},{12,8},{14,10},{16,20},{18,... | collective-permute-start | bytes 1179656 | tf_op jit(solution)/shard_map/ppermute | solution.py:21
  15.5 16.5 %collective-permute-start.10 = (bf16[128,1536]{1,0:T(8,128)(2,1)S(1)}, bf16[128,1536]{1,0:T(8,128)(2,1)S(1)}, u32[]{:S(2)}, u32[]{:S(2)}) collective-permute-start(bf16[128,1536]{1,0:T(8,128)(2,1)S(1)} %collective-permute-done.rest_1_), channel_id=1, source_target_pairs={{0,16},{2,18},{4,20},{6,22},{16,24},{18,26},{20,28},{22,30},{24,8}... | collective-permute-start | bytes 1179656 | tf_op jit(solution)/shard_map/ppermute | solution.py:407
  24.0 3.7 %collective-permute-start.6 = (bf16[128,1024]{1,0:T(8,128)(2,1)S(1)}, bf16[128,1024]{1,0:T(8,128)(2,1)S(1)}, u32[]{:S(2)}, u32[]{:S(2)}) collective-permute-start(bf16[128,1024]{1,0:T(8,128)(2,1)S(1)} %get-tuple-element.47), channel_id=1, source_target_pairs={{0,2},{2,0},{4,6},{6,4},{8,10},{10,8},{12,14},{14,12},{16,18},{18,... | collective-permute-start | bytes 786440 | tf_op jit(solution)/shard_map/ppermute | solution.py:21
  24.0 11.9 %collective-permute-start.11 = (bf16[128,1536]{1,0:T(8,128)(2,1)S(1)}, bf16[128,1536]{1,0:T(8,128)(2,1)S(1)}, u32[]{:S(2)}, u32[]{:S(2)}) collective-permute-start(bf16[128,1536]{1,0:T(8,128)(2,1)S(1)} %collective-permute-done.8.rest_3_), channel_id=1, source_target_pairs={{0,4},{2,6},{4,0},{6,2},{8,12},{10,14},{12,8},{14,10},{16,20},{18,... | collective-permute-start | bytes 1179656 | tf_op jit(solution)/shard_map/ppermute | solution.py:21
  26.6 12.0 %collective-permute-start.12 = (bf16[80,1536]{1,0:T(8,128)(2,1)S(1)}, bf16[80,1536]{1,0:T(8,128)(2,1)S(1)}, u32[]{:S(2)}, u32[]{:S(2)}) collective-permute-start(bf16[80,1536]{1,0:T(8,128)(2,1)S(1)} %slice.6), channel_id=1, source_target_pairs={{0,16},{2,18},{4,20},{6,22},{16,24},{18,26},{20,28},{22,30},{24,8}... | collective-permute-start | bytes 737288 | tf_op jit(solution)/shard_map/ppermute | solution.py:407
  32.1 6.6 %collective-permute-start.13 = (bf16[48,1536]{1,0:T(8,128)(2,1)S(1)}, bf16[48,1536]{1,0:T(8,128)(2,1)S(1)}, u32[]{:S(2)}, u32[]{:S(2)}) collective-permute-start(bf16[48,1536]{1,0:T(8,128)(2,1)S(1)} %slice.7), channel_id=1, source_target_pairs={{0,4},{2,6},{4,0},{6,2},{8,12},{10,14},{12,8},{14,10},{16,20},{18,... | collective-permute-start | bytes 442376 | tf_op jit(solution)/shard_map/ppermute | solution.py:21
  34.7 1.5 %collective-permute-start.5 = (bf16[128,512]{1,0:T(8,128)(2,1)S(1)}, bf16[128,512]{1,0:T(8,128)(2,1)S(1)}, u32[]{:S(2)}, u32[]{:S(2)}) collective-permute-start(bf16[128,512]{1,0:T(8,128)(2,1)S(1)} %get-tuple-element.46), channel_id=1, source_target_pairs={{0,2},{2,0},{4,6},{6,4},{8,10},{10,8},{12,14},{14,12},{16,18},{18,... | collective-permute-start | bytes 393224 | tf_op jit(solution)/shard_map/ppermute | solution.py:21
  34.8 1.5 %collective-permute-start.4 = (bf16[128,512]{1,0:T(8,128)(2,1)S(1)}, bf16[128,512]{1,0:T(8,128)(2,1)S(1)}, u32[]{:S(2)}, u32[]{:S(2)}) collective-permute-start(bf16[128,512]{1,0:T(8,128)(2,1)S(1)} %get-tuple-element.45), channel_id=1, source_target_pairs={{0,2},{2,0},{4,6},{6,4},{8,10},{10,8},{12,14},{14,12},{16,18},{18,... | collective-permute-start | bytes 393224 | tf_op jit(solution)/shard_map/ppermute | solution.py:21
  37.0 3.8 %collective-permute-start.17 = (bf16[256,512]{1,0:T(8,128)(2,1)S(1)}, bf16[256,512]{1,0:T(8,128)(2,1)S(1)}, u32[]{:S(2)}, u32[]{:S(2)}) collective-permute-start(bf16[256,512]{1,0:T(8,128)(2,1)S(1)} %get-tuple-element.62), channel_id=1, source_target_pairs={{0,2},{2,0},{4,6},{6,4},{8,10},{10,8},{12,14},{14,12},{16,18},{18,... | collective-permute-start | bytes 786440 | tf_op jit(solution)/shard_map/ppermute | solution.py:21
  37.8 2.9 %collective-permute-start.16 = (bf16[256,512]{1,0:T(8,128)(2,1)S(1)}, bf16[256,512]{1,0:T(8,128)(2,1)S(1)}, u32[]{:S(2)}, u32[]{:S(2)}) collective-permute-start(bf16[256,512]{1,0:T(8,128)(2,1)S(1)} %get-tuple-element.61), channel_id=1, source_target_pairs={{0,2},{2,0},{4,6},{6,4},{8,10},{10,8},{12,14},{14,12},{16,18},{18,... | collective-permute-start | bytes 786440 | tf_op jit(solution)/shard_map/ppermute | solution.py:21
  38.7 2.1 %collective-permute-start.18 = (bf16[256,512]{1,0:T(8,128)(2,1)S(1)}, bf16[256,512]{1,0:T(8,128)(2,1)S(1)}, u32[]{:S(2)}, u32[]{:S(2)}) collective-permute-start(bf16[256,512]{1,0:T(8,128)(2,1)S(1)} %get-tuple-element.64), channel_id=1, source_target_pairs={{0,2},{2,0},{4,6},{6,4},{8,10},{10,8},{12,14},{14,12},{16,18},{18,... | collective-permute-start | bytes 786440 | tf_op jit(solution)/shard_map/ppermute | solution.py:21
  38.9 1.8 %collective-permute-start.14 = (bf16[80,1536]{1,0:T(8,128)(2,1)S(1)}, bf16[80,1536]{1,0:T(8,128)(2,1)S(1)}, u32[]{:S(2)}, u32[]{:S(2)}) collective-permute-start(bf16[80,1536]{1,0:T(8,128)(2,1)S(1)} %collective-permute-done.12.rest_0_), channel_id=1, source_target_pairs={{0,2},{2,0},{4,6},{6,4},{8,10},{10,8},{12,14},{14,12},{16,18},{18,... | collective-permute-start | bytes 737288 | tf_op jit(solution)/shard_map/ppermute | solution.py:21
  39.2 1.6 %collective-permute-start.15 = (bf16[48,1536]{1,0:T(8,128)(2,1)S(1)}, bf16[48,1536]{1,0:T(8,128)(2,1)S(1)}, u32[]{:S(2)}, u32[]{:S(2)}) collective-permute-start(bf16[48,1536]{1,0:T(8,128)(2,1)S(1)} %collective-permute-done.13.rest_1_), channel_id=1, source_target_pairs={{0,2},{2,0},{4,6},{6,4},{8,10},{10,8},{12,14},{14,12},{16,18},{18,... | collective-permute-start | bytes 442376 | tf_op jit(solution)/shard_map/ppermute | solution.py:21

commit v3 on v1

--- a/solution.py
+++ b/solution.py
@@ -343,33 +343,48 @@
         their_total_ref[block:, here] = edge[block:].astype(jnp.bfloat16)
 
 
-def last_project_kernel(features_ref, *rest):
-    shard_refs, total_refs, out_ref = rest[:4], rest[4:-1], rest[-1]
+def gather_sums_kernel(parts, features_ref, *rest):
+    operands, out_ref = rest[:-1], rest[-1]
+    shard_refs, sum_refs = operands[: -2 * parts + 1], operands[-2 * parts + 1 :]
+    depth = sum(ref.shape[0] for ref in shard_refs)
     first = 0
-    for total_ref in total_refs:
+    for part in range(parts):
+        total_ref = sum_refs[part]
         columns = slice(first, first + total_ref.shape[1])
         weight = jnp.concatenate([ref[:, columns] for ref in shard_refs], axis=0)
-        out_ref[:, columns] = total_ref[...] + jnp.dot(
-            features_ref[...], weight, preferred_element_type=jnp.float32
+        total = total_ref[...] + jnp.dot(
+            features_ref[:, :depth], weight, preferred_element_type=jnp.float32
         )
+        out_ref[:, columns] = total if part == parts - 1 else total + sum_refs[parts + part][...]
         first += total_ref.shape[1]
 
 
-def finish_kernel(total_ref, *rest):
-    more_refs, (out_ref, held, sems) = rest[:-3], rest[-3:]
+def finish_kernel(features_ref, total_ref, more_ref, *rest):
+    shard_refs, (out_ref, held, sems) = rest[:-3], rest[-3:]
+    depth = sum(ref.shape[0] for ref in shard_refs)
+    width, late = out_ref.shape[1], more_ref.shape[1]
     block = out_ref.shape[0] // 2
+    pieces = sems.shape[1]
+    some = block // pieces
     ctx = lax.axis_index("ctx")
     copies = []
     for which, place in ((0, ctx), (1, 1 - ctx)):
-        rows = slice(which * block, (which + 1) * block)
-        first = 0
-        for more_ref in more_refs:
-            columns = slice(first, first + more_ref.shape[1])
-            held[rows, columns] = (total_ref[rows, columns] + more_ref[rows]).astype(jnp.bfloat16)
-            first += more_ref.shape[1]
-        target = out_ref.at[pl.ds(pl.multiple_of(place * block, block), block)]
-        copies.append(pltpu.make_async_copy(held.at[rows], target, sems.at[which]))
-        copies[-1].start()
+        for piece in range(pieces):
+            rows = slice(which * block + piece * some, which * block + (piece + 1) * some)
+            for first in range(0, width, late):
+                columns = slice(first, first + late)
+                weight = jnp.concatenate([ref[:, columns] for ref in shard_refs], axis=0)
+                total = total_ref[rows, columns] + jnp.dot(
+                    features_ref[rows, depth:], weight, preferred_element_type=jnp.float32
+                )
+                if first + late == width:
+                    total = total + more_ref[rows]
+                held[rows, columns] = total.astype(jnp.bfloat16)
+            there = pl.ds(pl.multiple_of(place * block + piece * some, some), some)
+            copies.append(
+                pltpu.make_async_copy(held.at[rows], out_ref.at[there], sems.at[which, piece])
+            )
+            copies[-1].start()
     for copy in copies:
         copy.wait()
 
@@ -541,20 +556,20 @@
             their_total = after(their_total, *last)
         mores.append(to_core(their_total))
     total = call(
-        last_project_kernel,
-        "last_project",
+        functools.partial(gather_sums_kernel, parts),
+        "gather_sums",
         (local_rows, width),
-        [VMEM()] * (1 + 2 * len(last) + parts),
+        [VMEM()] * (len(last) + 2 * parts),
         dtypes=[jnp.float32],
-    )(last_features, *last, *last_swapped, *own_totals)
+    )(last_features, *last, *own_totals, *mores[:-1])
     return call(
         finish_kernel,
         "finish",
         (local_rows, width),
-        [VMEM()] * (1 + parts),
-        scratch=[pltpu.VMEM((local_rows, width), bf16), pltpu.SemaphoreType.DMA((2,))],
+        [VMEM()] * (3 + len(last)),
+        scratch=[pltpu.VMEM((local_rows, width), bf16), pltpu.SemaphoreType.DMA((2, 2))],
         out_spec=HBM(),
-    )(total, *mores)
+    )(last_features, total, mores[-1], *last_swapped)
 
 
 def body(projections, block_source, clip_ids, out_weight):

time: 42.3 us -> 42 us (level)
  no operation moved by 1% of the time
where the time goes in v3:
time: 42 us; the launch traced here: 41.9 us
  starting transfers between devices  20 us (48%)
  Pallas kernels  11 us (26%)
  waiting for transfers between devices  10.7 us (25%)
    ppermute x4, starting transfers between devices, around(): lax.ppermute(value, 'dp', [(4 * here + rest, 4 * there + rest) for here,...  9.14 us
    ppermute x4, waiting for transfers between devices, around(): lax.ppermute(value, 'dp', [(4 * here + rest, 4 * there + rest) for here,...  8.74 us
    ppermute x13, starting transfers between devices, partner(): return lax.ppermute(value, axis, pairs)  8.49 us
    ppermute x2, starting transfers between devices, body_edge(): halos = [lax.ppermute(part, 'ctx', [(0, 1), (1, 0)]) for part in packed]  2.32 us
    pallas_call x2, Pallas kernels, edge_rows(): call(functools.partial(edge_kernel, sum(part_heads[:part])), 'edge_rows',...  2.24 us
    ppermute x13, waiting for transfers between devices, partner(): return lax.ppermute(value, axis, pairs)  1.93 us
    pallas_call x1, Pallas kernels, body_edge(): call(stage_kernel, 'stage', [own.shape, (7, 8, 128)], [HBM()] * 3, dtypes...  1.91 us
    pallas_call x1, Pallas kernels, body_edge(): call(inner_kernel, 'inner_rows', [(block_rows, features), (block_rows, fe...  1.73 us
  transfers between devices with their start and end apart: 19, of which 8 were waited for; matrix products, arithmetic and copies ran while one was open for 0% of the time, Pallas kernels for 24%

profile of v3, /device:TPU:0, one launch (start us, length us, event | category | flops | bytes accessed | tf_op | source)
XLA Modules:
  0.0 41.9 jit_solution(1521474508997465766)
XLA Ops:
  0.0 0.5 %collective-permute-start.1 = (bf16[2,128,6144]{2,1,0:T(8,128)(2,1)}, bf16[2,128,6144]{2,1,0:T(8,128)(2,1)S(1)}, u32[]{:S(2)}, u32[]{:S(2)}) collective-permute-start(bf16[2,128,6144]{2,1,0:T(8,128)(2,1)} %bitcast.1), channel_id=1, source_target_pairs={{0,2},{2,0},{4,6},{6,4},{8,10},{10,8},{12,14},{14,12},{16,18},{18,... | collective-permute-start | bytes 9437192 | tf_op jit(solution)/shard_map/ppermute | solution.py:21
  0.5 3.6 %collective-permute-start = (bf16[128,1536]{1,0:T(8,128)(2,1)}, bf16[128,1536]{1,0:T(8,128)(2,1)S(1)}, u32[]{:S(2)}, u32[]{:S(2)}) collective-permute-start(bf16[128,1536]{1,0:T(8,128)(2,1)} %rest_0_.7), channel_id=1, source_target_pairs={{0,16},{2,18},{4,20},{6,22},{16,24},{18,26},{20,28},{22,30},{24,8}... | collective-permute-start | bytes 1179656 | tf_op jit(solution)/shard_map/ppermute | solution.py:429
  4.0 1.5 %collective-permute-start.7 = (bf16[128,1536]{1,0:T(8,128)(2,1)}, bf16[128,1536]{1,0:T(8,128)(2,1)S(1)}, u32[]{:S(2)}, u32[]{:S(2)}) collective-permute-start(bf16[128,1536]{1,0:T(8,128)(2,1)} %rest_0_.7), channel_id=1, source_target_pairs={{0,4},{2,6},{4,0},{6,2},{8,12},{10,14},{12,8},{14,10},{16,20},{18,... | collective-permute-start | bytes 1179656 | tf_op jit(solution)/shard_map/ppermute | solution.py:21
  5.5 1.9 %stage.1 = (bf16[2,128,6144]{2,1,0:T(8,128)(2,1)S(1)}, s32[7,8,128]{2,1,0:T(8,128)S(1)}) custom-call(s32[1,1,2]{2,1,0:T(1,128)} %sources.1, s32[1,4]{1,0:T(1,128)} %clips.1, bf16[2,128,6144]{2,1,0:T(8,128)(2,1)} %bitcast.2), custom_call_target="tpu_custom_call" | custom-call | tf_op jit(solution)/shard_map/stage/pallas_call | solution.py:447
  7.5 0.0 collective-permute-done.1.partner_ref
  7.5 0.0 copy-start
  7.5 0.2 pack_first.1
  7.7 1.6 %collective-permute-start.2 = (bf16[128,2048]{1,0:T(8,128)(2,1)S(1)}, bf16[128,2048]{1,0:T(8,128)(2,1)S(1)}, u32[]{:S(2)}, u32[]{:S(2)}) collective-permute-start(bf16[128,2048]{1,0:T(8,128)(2,1)S(1)} %pack_first.1), channel_id=1, source_target_pairs={{0,1},{1,0},{2,3},{3,2},{4,5},{5,4},{6,7},{7,6},{8,9},{9,8},{10,11... | collective-permute-start | bytes 1572872 | tf_op jit(solution)/shard_map/ppermute | solution.py:475
  9.3 1.4 %collective-permute-start.8 = (bf16[128,1536]{1,0:T(8,128)(2,1)S(1)}, bf16[128,1536]{1,0:T(8,128)(2,1)S(1)}, u32[]{:S(2)}, u32[]{:S(2)}) collective-permute-start(bf16[128,1536]{1,0:T(8,128)(2,1)S(1)} %copy-done), channel_id=1, source_target_pairs={{0,8},{2,10},{4,12},{6,14},{16,0},{18,2},{20,4},{22,6},{24,16},{26... | collective-permute-start | bytes 1179656 | tf_op jit(solution)/shard_map/ppermute | solution.py:429
  10.7 0.7 %pack.1 = (bf16[2,128,6144]{2,1,0:T(8,128)(2,1)S(1)}, bf16[128,2048]{1,0:T(8,128)(2,1)S(1)}) custom-call(s32[7,8,128]{2,1,0:T(8,128)S(1)} %get-tuple-element.40.facts_ref, bf16[2,128,6144]{2,1,0:T(8,128)(2,1)S(1)} %get-tuple-element.36.own_ref, bf16[2,128,6144]{2,1,0:T(8,128)(2,1)S(1)} %collective-permute-done.1.partner_ref), custom_call_target="tpu_custom_call" | custom-call | tf_op jit(solution)/shard_map/pack/pallas_call | solution.py:467
  11.4 0.7 %collective-permute-start.3 = (bf16[128,2048]{1,0:T(8,128)(2,1)S(1)}, bf16[128,2048]{1,0:T(8,128)(2,1)S(1)}, u32[]{:S(2)}, u32[]{:S(2)}) collective-permute-start(bf16[128,2048]{1,0:T(8,128)(2,1)S(1)} %get-tuple-element.38), channel_id=1, source_target_pairs={{0,1},{1,0},{2,3},{3,2},{4,5},{5,4},{6,7},{7,6},{8,9},{9,8},{10,11... | collective-permute-start | bytes 1572872 | tf_op jit(solution)/shard_map/ppermute | solution.py:475
  12.2 1.6 %collective-permute-done.rest_1_ = bf16[128,1536]{1,0:T(8,128)(2,1)S(1)} collective-permute-done((bf16[128,1536]{1,0:T(8,128)(2,1)}, bf16[128,1536]{1,0:T(8,128)(2,1)S(1)}, u32[]{:S(2)}, u32[]{:S(2)}) %collective-permute-start) | collective-permute-done | bytes 393248 | tf_op jit(solution)/shard_map/ppermute | solution.py:429
  13.8 1.5 %collective-permute-start.9 = (bf16[128,1536]{1,0:T(8,128)(2,1)S(1)}, bf16[128,1536]{1,0:T(8,128)(2,1)S(1)}, u32[]{:S(2)}, u32[]{:S(2)}) collective-permute-start(bf16[128,1536]{1,0:T(8,128)(2,1)S(1)} %collective-permute-done.rest_1_), channel_id=1, source_target_pairs={{0,4},{2,6},{4,0},{6,2},{8,12},{10,14},{12,8},{14,10},{16,20},{18,... | collective-permute-start | bytes 1179656 | tf_op jit(solution)/shard_map/ppermute | solution.py:21
  15.3 0.2 collective-permute-done.7.rest_2_
  15.5 3.1 %collective-permute-start.10 = (bf16[128,1536]{1,0:T(8,128)(2,1)S(1)}, bf16[128,1536]{1,0:T(8,128)(2,1)S(1)}, u32[]{:S(2)}, u32[]{:S(2)}) collective-permute-start(bf16[128,1536]{1,0:T(8,128)(2,1)S(1)} %collective-permute-done.rest_1_), channel_id=1, source_target_pairs={{0,16},{2,18},{4,20},{6,22},{16,24},{18,26},{20,28},{22,30},{24,8}... | collective-permute-start | bytes 1179656 | tf_op jit(solution)/shard_map/ppermute | solution.py:429
  18.6 1.7 %inner_rows.1 = (bf16[128,2048]{1,0:T(8,128)(2,1)S(1)}, bf16[128,1024]{1,0:T(8,128)(2,1)S(1)}) custom-call(s32[7,8,128]{2,1,0:T(8,128)S(1)} %get-tuple-element.40.facts_ref, bf16[2,128,6144]{2,1,0:T(8,128)(2,1)S(1)} %get-tuple-element.41.rows_ref), custom_call_target="tpu_custom_call" | custom-call | tf_op jit(solution)/shard_map/inner_rows/pallas_call | solution.py:491
  20.3 3.7 %collective-permute-done.8.rest_3_ = bf16[128,1536]{1,0:T(8,128)(2,1)S(1)} collective-permute-done((bf16[128,1536]{1,0:T(8,128)(2,1)S(1)}, bf16[128,1536]{1,0:T(8,128)(2,1)S(1)}, u32[]{:S(2)}, u32[]{:S(2)}) %collective-permute-start.8) | collective-permute-done | bytes 393248 | tf_op jit(solution)/shard_map/ppermute | solution.py:429
  24.0 0.0 collective-permute-start.6
  24.0 0.0 collective-permute-done.2.halo_ref
  24.0 1.5 %collective-permute-start.11 = (bf16[128,1536]{1,0:T(8,128)(2,1)S(1)}, bf16[128,1536]{1,0:T(8,128)(2,1)S(1)}, u32[]{:S(2)}, u32[]{:S(2)}) collective-permute-start(bf16[128,1536]{1,0:T(8,128)(2,1)S(1)} %collective-permute-done.8.rest_3_), channel_id=1, source_target_pairs={{0,4},{2,6},{4,0},{6,2},{8,12},{10,14},{12,8},{14,10},{16,20},{18,... | collective-permute-start | bytes 1179656 | tf_op jit(solution)/shard_map/ppermute | solution.py:21
  25.5 1.1 %edge_rows.2 = (bf16[128,1024]{1,0:T(8,128)(2,1)S(1)}, bf16[128,512]{1,0:T(8,128)(2,1)S(1)}) custom-call(s32[7,8,128]{2,1,0:T(8,128)S(1)} %get-tuple-element.40.facts_ref, bf16[2,128,6144]{2,1,0:T(8,128)(2,1)S(1)} %get-tuple-element.41.rows_ref, bf16[128,2048]{1,0:T(8,128)(2,1)S(1)} %collective-permute-done.2.halo_ref), custom_call_target="tpu_custom_call" | custom-call | tf_op jit(solution)/shard_map/edge_rows/pallas_call | solution.py:479
  26.6 0.0 collective-permute-done.9.rest_4_
  26.6 1.1 %collective-permute-start.12 = (bf16[80,1536]{1,0:T(8,128)(2,1)S(1)}, bf16[80,1536]{1,0:T(8,128)(2,1)S(1)}, u32[]{:S(2)}, u32[]{:S(2)}) collective-permute-start(bf16[80,1536]{1,0:T(8,128)(2,1)S(1)} %slice.6), channel_id=1, source_target_pairs={{0,16},{2,18},{4,20},{6,22},{16,24},{18,26},{20,28},{22,30},{24,8}... | collective-permute-start | bytes 737288 | tf_op jit(solution)/shard_map/ppermute | solution.py:429
  27.7 0.0 collective-permute-done.6.their_ref
  27.7 0.9 %inner_project.1 = (f32[256,1536]{1,0:T(8,128)S(1)}, bf16[256,256]{1,0:T(8,128)(2,1)S(1)}) custom-call(bf16[128,2048]{1,0:T(8,128)(2,1)S(1)} %get-tuple-element.42.inner_ref, bf16[128,1024]{1,0:T(8,128)(2,1)S(1)} %collective-permute-done.6.their_ref, bf16[128,1536]{1,0:T(8,128)(2,1)S(1)} %copy-done, bf16[128,1536]{1,0:T(8,128)(2,1)S(1)} %collective-permute-done.rest_1_, ...), custom_call_target="tpu_custom_call" | custom-call | tf_op jit(solution)/shard_map/inner_project/pallas_call | solution.py:505
  28.6 3.5 %collective-permute-done.10.rest_0_.rest_5_ = bf16[128,1536]{1,0:T(8,128)(2,1)S(1)} collective-permute-done((bf16[128,1536]{1,0:T(8,128)(2,1)S(1)}, bf16[128,1536]{1,0:T(8,128)(2,1)S(1)}, u32[]{:S(2)}, u32[]{:S(2)}) %collective-permute-start.10) | collective-permute-done | bytes 393248 | tf_op jit(solution)/shard_map/ppermute | solution.py:429
  32.1 1.6 %collective-permute-start.13 = (bf16[48,1536]{1,0:T(8,128)(2,1)S(1)}, bf16[48,1536]{1,0:T(8,128)(2,1)S(1)}, u32[]{:S(2)}, u32[]{:S(2)}) collective-permute-start(bf16[48,1536]{1,0:T(8,128)(2,1)S(1)} %slice.7), channel_id=1, source_target_pairs={{0,4},{2,6},{4,0},{6,2},{8,12},{10,14},{12,8},{14,10},{16,20},{18,... | collective-permute-start | bytes 442376 | tf_op jit(solution)/shard_map/ppermute | solution.py:21
  33.6 0.0 collective-permute-done.3.halo_ref
  33.6 1.1 %edge_rows.3 = (bf16[128,1024]{1,0:T(8,128)(2,1)S(1)}, bf16[128,512]{1,0:T(8,128)(2,1)S(1)}) custom-call(s32[7,8,128]{2,1,0:T(8,128)S(1)} %get-tuple-element.40.facts_ref, bf16[2,128,6144]{2,1,0:T(8,128)(2,1)S(1)} %get-tuple-element.41.rows_ref, bf16[128,2048]{1,0:T(8,128)(2,1)S(1)} %collective-permute-done.3.halo_ref), custom_call_target="tpu_custom_call" | custom-call | tf_op jit(solution)/shard_map/edge_rows/pallas_call | solution.py:479
  34.7 0.1 collective-permute-start.5
  34.8 0.5 %collective-permute-start.4 = (bf16[128,512]{1,0:T(8,128)(2,1)S(1)}, bf16[128,512]{1,0:T(8,128)(2,1)S(1)}, u32[]{:S(2)}, u32[]{:S(2)}) collective-permute-start(bf16[128,512]{1,0:T(8,128)(2,1)S(1)} %get-tuple-element.45), channel_id=1, source_target_pairs={{0,2},{2,0},{4,6},{6,4},{8,10},{10,8},{12,14},{14,12},{16,18},{18,... | collective-permute-start | bytes 393224 | tf_op jit(solution)/shard_map/ppermute | solution.py:21
  35.3 0.6 %collective-permute-done.11.rest_1_.rest_6_ = bf16[128,1536]{1,0:T(8,128)(2,1)S(1)} collective-permute-done((bf16[128,1536]{1,0:T(8,128)(2,1)S(1)}, bf16[128,1536]{1,0:T(8,128)(2,1)S(1)}, u32[]{:S(2)}, u32[]{:S(2)}) %collective-permute-start.11) | collective-permute-done | bytes 393248 | tf_op jit(solution)/shard_map/ppermute | solution.py:21
  35.9 0.4 add_products.1.inner_total_ref
  36.2 0.0 collective-permute-done.5.refs_3_
  36.3 0.1 collective-permute-done.4.refs_2_
  36.3 0.2 arrange.1
  36.6 0.4 %project.4 = (f32[256,512]{1,0:T(8,128)S(1)}, bf16[256,512]{1,0:T(8,128)(2,1)S(1)}) custom-call(bf16[256,896]{1,0:T(8,128)(2,1)S(1)} %get-tuple-element.57.edge_ref, f32[256,1536]{1,0:T(8,128)S(1)} %add_products.1.inner_total_ref, bf16[128,1536]{1,0:T(8,128)(2,1)S(1)} %copy-done, bf16[128,1536]{1,0:T(8,128)(2,1)S(1)} %collective-permute-done.rest_1_, ...), custom_call_target="tpu_custom_call" | custom-call | tf_op jit(solution)/shard_map/project/pallas_call | solution.py:547
  37.0 0.4 collective-permute-start.15
  37.4 0.4 %project.3 = (f32[256,512]{1,0:T(8,128)S(1)}, bf16[256,512]{1,0:T(8,128)(2,1)S(1)}) custom-call(bf16[256,896]{1,0:T(8,128)(2,1)S(1)} %get-tuple-element.57.edge_ref, f32[256,1536]{1,0:T(8,128)S(1)} %add_products.1.inner_total_ref, bf16[128,1536]{1,0:T(8,128)(2,1)S(1)} %copy-done, bf16[128,1536]{1,0:T(8,128)(2,1)S(1)} %collective-permute-done.rest_1_, ...), custom_call_target="tpu_custom_call" | custom-call | tf_op jit(solution)/shard_map/project/pallas_call | solution.py:547
  37.8 0.3 collective-permute-start.14
  38.1 0.4 %project.5 = (f32[256,512]{1,0:T(8,128)S(1)}, bf16[256,512]{1,0:T(8,128)(2,1)S(1)}) custom-call(bf16[256,896]{1,0:T(8,128)(2,1)S(1)} %get-tuple-element.57.edge_ref, f32[256,1536]{1,0:T(8,128)S(1)} %add_products.1.inner_total_ref, bf16[128,1536]{1,0:T(8,128)(2,1)S(1)} %copy-done, bf16[128,1536]{1,0:T(8,128)(2,1)S(1)} %collective-permute-done.rest_1_, ...), custom_call_target="tpu_custom_call" | custom-call | tf_op jit(solution)/shard_map/project/pallas_call | solution.py:547
  38.5 0.1 collective-permute-done.13.rest_1_
  38.7 0.3 collective-permute-start.16
  38.9 0.2 collective-permute-start.17
  39.2 0.3 collective-permute-start.18
  39.5 0.3 gather_sums.1.total_ref
  39.8 0.9 %collective-permute-done.18.rest_1_ = bf16[48,1536]{1,0:T(8,128)(2,1)S(1)} collective-permute-done((bf16[48,1536]{1,0:T(8,128)(2,1)S(1)}, bf16[48,1536]{1,0:T(8,128)(2,1)S(1)}, u32[]{:S(2)}, u32[]{:S(2)}) %collective-permute-start.18) | collective-permute-done | bytes 147488 | tf_op jit(solution)/shard_map/ppermute | solution.py:21
  40.8 1.1 %finish.1 = bf16[256,1536]{1,0:T(8,128)(2,1)} custom-call(bf16[256,256]{1,0:T(8,128)(2,1)S(1)} %get-tuple-element.55.features_ref, f32[256,1536]{1,0:T(8,128)S(1)} %gather_sums.1.total_ref, bf16[256,512]{1,0:T(8,128)(2,1)S(1)} %collective-permute-done.16.more_ref, bf16[80,1536]{1,0:T(8,128)(2,1)S(1)} %collective-permute-done.17.rest_0_, ...), custom_call_target="tpu_custom_call" | custom-call | tf_op jit(solution)/shard_map/finish/pallas_call | solution.py:565
  (8 shorter events, 0.0 us)
Async XLA Ops:
  0.0 7.5 %collective-permute-start.1 = (bf16[2,128,6144]{2,1,0:T(8,128)(2,1)}, bf16[2,128,6144]{2,1,0:T(8,128)(2,1)S(1)}, u32[]{:S(2)}, u32[]{:S(2)}) collective-permute-start(bf16[2,128,6144]{2,1,0:T(8,128)(2,1)} %bitcast.1), channel_id=1, source_target_pairs={{0,2},{2,0},{4,6},{6,4},{8,10},{10,8},{12,14},{14,12},{16,18},{18,... | collective-permute-start | bytes 9437192 | tf_op jit(solution)/shard_map/ppermute | solution.py:21
  0.5 13.3 %collective-permute-start = (bf16[128,1536]{1,0:T(8,128)(2,1)}, bf16[128,1536]{1,0:T(8,128)(2,1)S(1)}, u32[]{:S(2)}, u32[]{:S(2)}) collective-permute-start(bf16[128,1536]{1,0:T(8,128)(2,1)} %rest_0_.7), channel_id=1, source_target_pairs={{0,16},{2,18},{4,20},{6,22},{16,24},{18,26},{20,28},{22,30},{24,8}... | collective-permute-start | bytes 1179656 | tf_op jit(solution)/shard_map/ppermute | solution.py:429
  4.0 11.5 %collective-permute-start.7 = (bf16[128,1536]{1,0:T(8,128)(2,1)}, bf16[128,1536]{1,0:T(8,128)(2,1)S(1)}, u32[]{:S(2)}, u32[]{:S(2)}) collective-permute-start(bf16[128,1536]{1,0:T(8,128)(2,1)} %rest_0_.7), channel_id=1, source_target_pairs={{0,4},{2,6},{4,0},{6,2},{8,12},{10,14},{12,8},{14,10},{16,20},{18,... | collective-permute-start | bytes 1179656 | tf_op jit(solution)/shard_map/ppermute | solution.py:21
  7.5 1.9 %copy-start = (bf16[128,1536]{1,0:T(8,128)(2,1)S(1)}, bf16[128,1536]{1,0:T(8,128)(2,1)}, u32[]{:S(2)}) copy-start(bf16[128,1536]{1,0:T(8,128)(2,1)} %rest_0_.7) | copy-start | bytes 1179652
  7.7 16.2 %collective-permute-start.2 = (bf16[128,2048]{1,0:T(8,128)(2,1)S(1)}, bf16[128,2048]{1,0:T(8,128)(2,1)S(1)}, u32[]{:S(2)}, u32[]{:S(2)}) collective-permute-start(bf16[128,2048]{1,0:T(8,128)(2,1)S(1)} %pack_first.1), channel_id=1, source_target_pairs={{0,1},{1,0},{2,3},{3,2},{4,5},{5,4},{6,7},{7,6},{8,9},{9,8},{10,11... | collective-permute-start | bytes 1572872 | tf_op jit(solution)/shard_map/ppermute | solution.py:475
  9.3 14.6 %collective-permute-start.8 = (bf16[128,1536]{1,0:T(8,128)(2,1)S(1)}, bf16[128,1536]{1,0:T(8,128)(2,1)S(1)}, u32[]{:S(2)}, u32[]{:S(2)}) collective-permute-start(bf16[128,1536]{1,0:T(8,128)(2,1)S(1)} %copy-done), channel_id=1, source_target_pairs={{0,8},{2,10},{4,12},{6,14},{16,0},{18,2},{20,4},{22,6},{24,16},{26... | collective-permute-start | bytes 1179656 | tf_op jit(solution)/shard_map/ppermute | solution.py:429
  11.4 22.2 %collective-permute-start.3 = (bf16[128,2048]{1,0:T(8,128)(2,1)S(1)}, bf16[128,2048]{1,0:T(8,128)(2,1)S(1)}, u32[]{:S(2)}, u32[]{:S(2)}) collective-permute-start(bf16[128,2048]{1,0:T(8,128)(2,1)S(1)} %get-tuple-element.38), channel_id=1, source_target_pairs={{0,1},{1,0},{2,3},{3,2},{4,5},{5,4},{6,7},{7,6},{8,9},{9,8},{10,11... | collective-permute-start | bytes 1572872 | tf_op jit(solution)/shard_map/ppermute | solution.py:475
  13.8 12.8 %collective-permute-start.9 = (bf16[128,1536]{1,0:T(8,128)(2,1)S(1)}, bf16[128,1536]{1,0:T(8,128)(2,1)S(1)}, u32[]{:S(2)}, u32[]{:S(2)}) collective-permute-start(bf16[128,1536]{1,0:T(8,128)(2,1)S(1)} %collective-permute-done.rest_1_), channel_id=1, source_target_pairs={{0,4},{2,6},{4,0},{6,2},{8,12},{10,14},{12,8},{14,10},{16,20},{18,... | collective-permute-start | bytes 1179656 | tf_op jit(solution)/shard_map/ppermute | solution.py:21
  15.5 16.5 %collective-permute-start.10 = (bf16[128,1536]{1,0:T(8,128)(2,1)S(1)}, bf16[128,1536]{1,0:T(8,128)(2,1)S(1)}, u32[]{:S(2)}, u32[]{:S(2)}) collective-permute-start(bf16[128,1536]{1,0:T(8,128)(2,1)S(1)} %collective-permute-done.rest_1_), channel_id=1, source_target_pairs={{0,16},{2,18},{4,20},{6,22},{16,24},{18,26},{20,28},{22,30},{24,8}... | collective-permute-start | bytes 1179656 | tf_op jit(solution)/shard_map/ppermute | solution.py:429
  24.0 3.7 %collective-permute-start.6 = (bf16[128,1024]{1,0:T(8,128)(2,1)S(1)}, bf16[128,1024]{1,0:T(8,128)(2,1)S(1)}, u32[]{:S(2)}, u32[]{:S(2)}) collective-permute-start(bf16[128,1024]{1,0:T(8,128)(2,1)S(1)} %get-tuple-element.47), channel_id=1, source_target_pairs={{0,2},{2,0},{4,6},{6,4},{8,10},{10,8},{12,14},{14,12},{16,18},{18,... | collective-permute-start | bytes 786440 | tf_op jit(solution)/shard_map/ppermute | solution.py:21
  24.0 11.9 %collective-permute-start.11 = (bf16[128,1536]{1,0:T(8,128)(2,1)S(1)}, bf16[128,1536]{1,0:T(8,128)(2,1)S(1)}, u32[]{:S(2)}, u32[]{:S(2)}) collective-permute-start(bf16[128,1536]{1,0:T(8,128)(2,1)S(1)} %collective-permute-done.8.rest_3_), channel_id=1, source_target_pairs={{0,4},{2,6},{4,0},{6,2},{8,12},{10,14},{12,8},{14,10},{16,20},{18,... | collective-permute-start | bytes 1179656 | tf_op jit(solution)/shard_map/ppermute | solution.py:21
  26.6 12.0 %collective-permute-start.12 = (bf16[80,1536]{1,0:T(8,128)(2,1)S(1)}, bf16[80,1536]{1,0:T(8,128)(2,1)S(1)}, u32[]{:S(2)}, u32[]{:S(2)}) collective-permute-start(bf16[80,1536]{1,0:T(8,128)(2,1)S(1)} %slice.6), channel_id=1, source_target_pairs={{0,16},{2,18},{4,20},{6,22},{16,24},{18,26},{20,28},{22,30},{24,8}... | collective-permute-start | bytes 737288 | tf_op jit(solution)/shard_map/ppermute | solution.py:429
  32.1 6.6 %collective-permute-start.13 = (bf16[48,1536]{1,0:T(8,128)(2,1)S(1)}, bf16[48,1536]{1,0:T(8,128)(2,1)S(1)}, u32[]{:S(2)}, u32[]{:S(2)}) collective-permute-start(bf16[48,1536]{1,0:T(8,128)(2,1)S(1)} %slice.7), channel_id=1, source_target_pairs={{0,4},{2,6},{4,0},{6,2},{8,12},{10,14},{12,8},{14,10},{16,20},{18,... | collective-permute-start | bytes 442376 | tf_op jit(solution)/shard_map/ppermute | solution.py:21
  34.7 1.5 %collective-permute-start.5 = (bf16[128,512]{1,0:T(8,128)(2,1)S(1)}, bf16[128,512]{1,0:T(8,128)(2,1)S(1)}, u32[]{:S(2)}, u32[]{:S(2)}) collective-permute-start(bf16[128,512]{1,0:T(8,128)(2,1)S(1)} %get-tuple-element.46), channel_id=1, source_target_pairs={{0,2},{2,0},{4,6},{6,4},{8,10},{10,8},{12,14},{14,12},{16,18},{18,... | collective-permute-start | bytes 393224 | tf_op jit(solution)/shard_map/ppermute | solution.py:21
  34.8 1.5 %collective-permute-start.4 = (bf16[128,512]{1,0:T(8,128)(2,1)S(1)}, bf16[128,512]{1,0:T(8,128)(2,1)S(1)}, u32[]{:S(2)}, u32[]{:S(2)}) collective-permute-start(bf16[128,512]{1,0:T(8,128)(2,1)S(1)} %get-tuple-element.45), channel_id=1, source_target_pairs={{0,2},{2,0},{4,6},{6,4},{8,10},{10,8},{12,14},{14,12},{16,18},{18,... | collective-permute-start | bytes 393224 | tf_op jit(solution)/shard_map/ppermute | solution.py:21
  37.0 2.5 %collective-permute-start.15 = (bf16[256,512]{1,0:T(8,128)(2,1)S(1)}, bf16[256,512]{1,0:T(8,128)(2,1)S(1)}, u32[]{:S(2)}, u32[]{:S(2)}) collective-permute-start(bf16[256,512]{1,0:T(8,128)(2,1)S(1)} %get-tuple-element.62), channel_id=1, source_target_pairs={{0,2},{2,0},{4,6},{6,4},{8,10},{10,8},{12,14},{14,12},{16,18},{18,... | collective-permute-start | bytes 786440 | tf_op jit(solution)/shard_map/ppermute | solution.py:21
  37.8 1.6 %collective-permute-start.14 = (bf16[256,512]{1,0:T(8,128)(2,1)S(1)}, bf16[256,512]{1,0:T(8,128)(2,1)S(1)}, u32[]{:S(2)}, u32[]{:S(2)}) collective-permute-start(bf16[256,512]{1,0:T(8,128)(2,1)S(1)} %get-tuple-element.61), channel_id=1, source_target_pairs={{0,2},{2,0},{4,6},{6,4},{8,10},{10,8},{12,14},{14,12},{16,18},{18,... | collective-permute-start | bytes 786440 | tf_op jit(solution)/shard_map/ppermute | solution.py:21
  38.7 2.1 %collective-permute-start.16 = (bf16[256,512]{1,0:T(8,128)(2,1)S(1)}, bf16[256,512]{1,0:T(8,128)(2,1)S(1)}, u32[]{:S(2)}, u32[]{:S(2)}) collective-permute-start(bf16[256,512]{1,0:T(8,128)(2,1)S(1)} %get-tuple-element.64), channel_id=1, source_target_pairs={{0,2},{2,0},{4,6},{6,4},{8,10},{10,8},{12,14},{14,12},{16,18},{18,... | collective-permute-start | bytes 786440 | tf_op jit(solution)/shard_map/ppermute | solution.py:21
  38.9 1.8 %collective-permute-start.17 = (bf16[80,1536]{1,0:T(8,128)(2,1)S(1)}, bf16[80,1536]{1,0:T(8,128)(2,1)S(1)}, u32[]{:S(2)}, u32[]{:S(2)}) collective-permute-start(bf16[80,1536]{1,0:T(8,128)(2,1)S(1)} %collective-permute-done.12.rest_0_), channel_id=1, source_target_pairs={{0,2},{2,0},{4,6},{6,4},{8,10},{10,8},{12,14},{14,12},{16,18},{18,... | collective-permute-start | bytes 737288 | tf_op jit(solution)/shard_map/ppermute | solution.py:21
  39.2 1.6 %collective-permute-start.18 = (bf16[48,1536]{1,0:T(8,128)(2,1)S(1)}, bf16[48,1536]{1,0:T(8,128)(2,1)S(1)}, u32[]{:S(2)}, u32[]{:S(2)}) collective-permute-start(bf16[48,1536]{1,0:T(8,128)(2,1)S(1)} %collective-permute-done.13.rest_1_), channel_id=1, source_target_pairs={{0,2},{2,0},{4,6},{6,4},{8,10},{10,8},{12,14},{14,12},{16,18},{18,... | collective-permute-start | bytes 442376 | tf_op jit(solution)/shard_map/ppermute | solution.py:21

commit v4 on v3

--- a/solution.py
+++ b/solution.py
@@ -93,18 +93,11 @@
     parts = sems.shape[1]
     slots = own_ref.shape[0]
     rows = own_ref.shape[1] // parts
-    copies = []
-    for block in range(slots):
-        for part in range(parts):
-            here = (block, pl.ds(part * rows, rows))
-            copies.append(
-                pltpu.make_async_copy(own_ref.at[here], out_ref.at[here], sems.at[block, part])
-            )
     few = [
         pltpu.make_async_copy(sources, source_ref, few_sems.at[0]),
         pltpu.make_async_copy(clips, clip_ref, few_sems.at[1]),
     ]
-    for copy in few + copies:
+    for copy in few:
         copy.start()
     for copy in few:
         copy.wait()
@@ -114,6 +107,28 @@
         source = source_ref[0, 0, block]
         facts[away] = (source // (2 * slots) != dp).astype(jnp.int32)
         facts[at] = lax.rem(source, slots)
+
+    def copies(slot):
+        found = []
+        for part in range(parts):
+            here = (slot, pl.ds(part * rows, rows))
+            found.append(
+                pltpu.make_async_copy(own_ref.at[here], out_ref.at[here], sems.at[slot, part])
+            )
+        return found
+
+    def used(slot):
+        edge = jnp.logical_and(facts[EDGE_AWAY] == 0, facts[EDGE_SLOT] == slot)
+        inner = jnp.logical_and(facts[INNER_AWAY] == 0, facts[INNER_SLOT] == slot)
+        return jnp.logical_or(edge, inner)
+
+    for slot in range(slots):
+
+        @pl.when(used(slot))
+        def _():
+            for copy in copies(slot):
+                copy.start()
+
     edge_clip = clip_ref[0, 1 + ctx]
     crosses = edge_clip == clip_ref[0, 2 - ctx]
     facts[CROSSES] = crosses.astype(jnp.int32)
@@ -121,8 +136,12 @@
     facts[INNER_JOINS] = (clip_ref[0, 2 * ctx] == clip_ref[0, 2 * ctx + 1]).astype(jnp.int32)
     for which, fact in facts.items():
         facts_ref[which] = jnp.full(facts_ref.shape[1:], fact, jnp.int32)
-    for copy in copies:
-        copy.wait()
+    for slot in range(slots):
+
+        @pl.when(used(slot))
+        def _():
+            for copy in copies(slot):
+                copy.wait()
 
 
 def fact(facts_ref, which):

time: 42 us -> 42 us (level)
  Pallas kernels: 11 us -> 11.7 us
  starting transfers between devices: 20 us -> 19.3 us
    pallas_call x1, Pallas kernels: 1.91 us -> 2.61 us  [body_edge(): call(stage_kernel, 'stage', [own.shape, (7, 8, 128)], [HBM()] * 3, dtypes...]
    ppermute x2, starting transfers between devices: 2.32 us -> 1.86 us  [body_edge(): halos = [lax.ppermute(part, 'ctx', [(0, 1), (1, 0)]) for part in packed]]
  transfers between devices with their start and end apart: 19 -> 19, of which waited for: 8 -> 8; matrix products, arithmetic and copies ran while one was open for 0% -> 0% of each run, Pallas kernels for 24% -> 25%
where the time goes in v4:
time: 42 us; the launch traced here: 41.9 us
  starting transfers between devices  19.3 us (46%)
  Pallas kernels  11.7 us (28%)
  waiting for transfers between devices  10.7 us (25%)
    ppermute x4, starting transfers between devices, around(): lax.ppermute(value, 'dp', [(4 * here + rest, 4 * there + rest) for here,...  8.92 us
    ppermute x4, waiting for transfers between devices, around(): lax.ppermute(value, 'dp', [(4 * here + rest, 4 * there + rest) for here,...  8.74 us
    ppermute x13, starting transfers between devices, partner(): return lax.ppermute(value, axis, pairs)  8.49 us
    pallas_call x1, Pallas kernels, body_edge(): call(stage_kernel, 'stage', [own.shape, (7, 8, 128)], [HBM()] * 3, dtypes...  2.61 us
    pallas_call x2, Pallas kernels, edge_rows(): call(functools.partial(edge_kernel, sum(part_heads[:part])), 'edge_rows',...  2.24 us
    ppermute x13, waiting for transfers between devices, partner(): return lax.ppermute(value, axis, pairs)  1.93 us
    ppermute x2, starting transfers between devices, body_edge(): halos = [lax.ppermute(part, 'ctx', [(0, 1), (1, 0)]) for part in packed]  1.86 us
    pallas_call x1, Pallas kernels, body_edge(): call(inner_kernel, 'inner_rows', [(block_rows, features), (block_rows, fe...  1.73 us
  transfers between devices with their start and end apart: 19, of which 8 were waited for; matrix products, arithmetic and copies ran while one was open for 0% of the time, Pallas kernels for 25%

profile of v4, /device:TPU:0, one launch (start us, length us, event | category | flops | bytes accessed | tf_op | source)
XLA Modules:
  0.0 41.9 jit_solution(14099233940146579222)
XLA Ops:
  0.0 0.5 %collective-permute-start.1 = (bf16[2,128,6144]{2,1,0:T(8,128)(2,1)}, bf16[2,128,6144]{2,1,0:T(8,128)(2,1)S(1)}, u32[]{:S(2)}, u32[]{:S(2)}) collective-permute-start(bf16[2,128,6144]{2,1,0:T(8,128)(2,1)} %bitcast.1), channel_id=1, source_target_pairs={{0,2},{2,0},{4,6},{6,4},{8,10},{10,8},{12,14},{14,12},{16,18},{18,... | collective-permute-start | bytes 9437192 | tf_op jit(solution)/shard_map/ppermute | solution.py:21
  0.5 3.6 %collective-permute-start = (bf16[128,1536]{1,0:T(8,128)(2,1)}, bf16[128,1536]{1,0:T(8,128)(2,1)S(1)}, u32[]{:S(2)}, u32[]{:S(2)}) collective-permute-start(bf16[128,1536]{1,0:T(8,128)(2,1)} %rest_0_.7), channel_id=1, source_target_pairs={{0,16},{2,18},{4,20},{6,22},{16,24},{18,26},{20,28},{22,30},{24,8}... | collective-permute-start | bytes 1179656 | tf_op jit(solution)/shard_map/ppermute | solution.py:448
  4.0 1.5 %collective-permute-start.7 = (bf16[128,1536]{1,0:T(8,128)(2,1)}, bf16[128,1536]{1,0:T(8,128)(2,1)S(1)}, u32[]{:S(2)}, u32[]{:S(2)}) collective-permute-start(bf16[128,1536]{1,0:T(8,128)(2,1)} %rest_0_.7), channel_id=1, source_target_pairs={{0,4},{2,6},{4,0},{6,2},{8,12},{10,14},{12,8},{14,10},{16,20},{18,... | collective-permute-start | bytes 1179656 | tf_op jit(solution)/shard_map/ppermute | solution.py:21
  5.5 2.6 %stage.1 = (bf16[2,128,6144]{2,1,0:T(8,128)(2,1)S(1)}, s32[7,8,128]{2,1,0:T(8,128)S(1)}) custom-call(s32[1,1,2]{2,1,0:T(1,128)} %sources.1, s32[1,4]{1,0:T(1,128)} %clips.1, bf16[2,128,6144]{2,1,0:T(8,128)(2,1)} %bitcast.2), custom_call_target="tpu_custom_call" | custom-call | tf_op jit(solution)/shard_map/stage/pallas_call | solution.py:466
  8.1 0.0 collective-permute-done.1.partner_ref
  8.2 0.0 copy-start
  8.2 0.2 pack_first.1
  8.4 1.1 %collective-permute-start.2 = (bf16[128,2048]{1,0:T(8,128)(2,1)S(1)}, bf16[128,2048]{1,0:T(8,128)(2,1)S(1)}, u32[]{:S(2)}, u32[]{:S(2)}) collective-permute-start(bf16[128,2048]{1,0:T(8,128)(2,1)S(1)} %pack_first.1), channel_id=1, source_target_pairs={{0,1},{1,0},{2,3},{3,2},{4,5},{5,4},{6,7},{7,6},{8,9},{9,8},{10,11... | collective-permute-start | bytes 1572872 | tf_op jit(solution)/shard_map/ppermute | solution.py:494
  9.5 1.2 %collective-permute-start.8 = (bf16[128,1536]{1,0:T(8,128)(2,1)S(1)}, bf16[128,1536]{1,0:T(8,128)(2,1)S(1)}, u32[]{:S(2)}, u32[]{:S(2)}) collective-permute-start(bf16[128,1536]{1,0:T(8,128)(2,1)S(1)} %copy-done), channel_id=1, source_target_pairs={{0,8},{2,10},{4,12},{6,14},{16,0},{18,2},{20,4},{22,6},{24,16},{26... | collective-permute-start | bytes 1179656 | tf_op jit(solution)/shard_map/ppermute | solution.py:448
  10.7 0.7 %pack.1 = (bf16[2,128,6144]{2,1,0:T(8,128)(2,1)S(1)}, bf16[128,2048]{1,0:T(8,128)(2,1)S(1)}) custom-call(s32[7,8,128]{2,1,0:T(8,128)S(1)} %get-tuple-element.40.facts_ref, bf16[2,128,6144]{2,1,0:T(8,128)(2,1)S(1)} %get-tuple-element.36.own_ref, bf16[2,128,6144]{2,1,0:T(8,128)(2,1)S(1)} %collective-permute-done.1.partner_ref), custom_call_target="tpu_custom_call" | custom-call | tf_op jit(solution)/shard_map/pack/pallas_call | solution.py:486
  11.4 0.7 %collective-permute-start.3 = (bf16[128,2048]{1,0:T(8,128)(2,1)S(1)}, bf16[128,2048]{1,0:T(8,128)(2,1)S(1)}, u32[]{:S(2)}, u32[]{:S(2)}) collective-permute-start(bf16[128,2048]{1,0:T(8,128)(2,1)S(1)} %get-tuple-element.38), channel_id=1, source_target_pairs={{0,1},{1,0},{2,3},{3,2},{4,5},{5,4},{6,7},{7,6},{8,9},{9,8},{10,11... | collective-permute-start | bytes 1572872 | tf_op jit(solution)/shard_map/ppermute | solution.py:494
  12.2 1.6 %collective-permute-done.rest_1_ = bf16[128,1536]{1,0:T(8,128)(2,1)S(1)} collective-permute-done((bf16[128,1536]{1,0:T(8,128)(2,1)}, bf16[128,1536]{1,0:T(8,128)(2,1)S(1)}, u32[]{:S(2)}, u32[]{:S(2)}) %collective-permute-start) | collective-permute-done | bytes 393248 | tf_op jit(solution)/shard_map/ppermute | solution.py:448
  13.8 1.5 %collective-permute-start.9 = (bf16[128,1536]{1,0:T(8,128)(2,1)S(1)}, bf16[128,1536]{1,0:T(8,128)(2,1)S(1)}, u32[]{:S(2)}, u32[]{:S(2)}) collective-permute-start(bf16[128,1536]{1,0:T(8,128)(2,1)S(1)} %collective-permute-done.rest_1_), channel_id=1, source_target_pairs={{0,4},{2,6},{4,0},{6,2},{8,12},{10,14},{12,8},{14,10},{16,20},{18,... | collective-permute-start | bytes 1179656 | tf_op jit(solution)/shard_map/ppermute | solution.py:21
  15.3 0.2 collective-permute-done.7.rest_2_
  15.5 3.1 %collective-permute-start.10 = (bf16[128,1536]{1,0:T(8,128)(2,1)S(1)}, bf16[128,1536]{1,0:T(8,128)(2,1)S(1)}, u32[]{:S(2)}, u32[]{:S(2)}) collective-permute-start(bf16[128,1536]{1,0:T(8,128)(2,1)S(1)} %collective-permute-done.rest_1_), channel_id=1, source_target_pairs={{0,16},{2,18},{4,20},{6,22},{16,24},{18,26},{20,28},{22,30},{24,8}... | collective-permute-start | bytes 1179656 | tf_op jit(solution)/shard_map/ppermute | solution.py:448
  18.6 1.7 %inner_rows.1 = (bf16[128,2048]{1,0:T(8,128)(2,1)S(1)}, bf16[128,1024]{1,0:T(8,128)(2,1)S(1)}) custom-call(s32[7,8,128]{2,1,0:T(8,128)S(1)} %get-tuple-element.40.facts_ref, bf16[2,128,6144]{2,1,0:T(8,128)(2,1)S(1)} %get-tuple-element.41.rows_ref), custom_call_target="tpu_custom_call" | custom-call | tf_op jit(solution)/shard_map/inner_rows/pallas_call | solution.py:510
  20.3 3.7 %collective-permute-done.8.rest_3_ = bf16[128,1536]{1,0:T(8,128)(2,1)S(1)} collective-permute-done((bf16[128,1536]{1,0:T(8,128)(2,1)S(1)}, bf16[128,1536]{1,0:T(8,128)(2,1)S(1)}, u32[]{:S(2)}, u32[]{:S(2)}) %collective-permute-start.8) | collective-permute-done | bytes 393248 | tf_op jit(solution)/shard_map/ppermute | solution.py:448
  24.0 0.0 collective-permute-start.6
  24.0 1.5 %collective-permute-start.11 = (bf16[128,1536]{1,0:T(8,128)(2,1)S(1)}, bf16[128,1536]{1,0:T(8,128)(2,1)S(1)}, u32[]{:S(2)}, u32[]{:S(2)}) collective-permute-start(bf16[128,1536]{1,0:T(8,128)(2,1)S(1)} %collective-permute-done.8.rest_3_), channel_id=1, source_target_pairs={{0,4},{2,6},{4,0},{6,2},{8,12},{10,14},{12,8},{14,10},{16,20},{18,... | collective-permute-start | bytes 1179656 | tf_op jit(solution)/shard_map/ppermute | solution.py:21
  25.5 1.1 %edge_rows.2 = (bf16[128,1024]{1,0:T(8,128)(2,1)S(1)}, bf16[128,512]{1,0:T(8,128)(2,1)S(1)}) custom-call(s32[7,8,128]{2,1,0:T(8,128)S(1)} %get-tuple-element.40.facts_ref, bf16[2,128,6144]{2,1,0:T(8,128)(2,1)S(1)} %get-tuple-element.41.rows_ref, bf16[128,2048]{1,0:T(8,128)(2,1)S(1)} %collective-permute-done.2.halo_ref), custom_call_target="tpu_custom_call" | custom-call | tf_op jit(solution)/shard_map/edge_rows/pallas_call | solution.py:498
  26.6 0.0 collective-permute-done.9.rest_4_
  26.6 1.1 %collective-permute-start.12 = (bf16[80,1536]{1,0:T(8,128)(2,1)S(1)}, bf16[80,1536]{1,0:T(8,128)(2,1)S(1)}, u32[]{:S(2)}, u32[]{:S(2)}) collective-permute-start(bf16[80,1536]{1,0:T(8,128)(2,1)S(1)} %slice.6), channel_id=1, source_target_pairs={{0,16},{2,18},{4,20},{6,22},{16,24},{18,26},{20,28},{22,30},{24,8}... | collective-permute-start | bytes 737288 | tf_op jit(solution)/shard_map/ppermute | solution.py:448
  27.7 0.0 collective-permute-done.6.their_ref
  27.7 0.9 %inner_project.1 = (f32[256,1536]{1,0:T(8,128)S(1)}, bf16[256,256]{1,0:T(8,128)(2,1)S(1)}) custom-call(bf16[128,2048]{1,0:T(8,128)(2,1)S(1)} %get-tuple-element.42.inner_ref, bf16[128,1024]{1,0:T(8,128)(2,1)S(1)} %collective-permute-done.6.their_ref, bf16[128,1536]{1,0:T(8,128)(2,1)S(1)} %copy-done, bf16[128,1536]{1,0:T(8,128)(2,1)S(1)} %collective-permute-done.rest_1_, ...), custom_call_target="tpu_custom_call" | custom-call | tf_op jit(solution)/shard_map/inner_project/pallas_call | solution.py:524
  28.6 3.5 %collective-permute-done.10.rest_0_.rest_5_ = bf16[128,1536]{1,0:T(8,128)(2,1)S(1)} collective-permute-done((bf16[128,1536]{1,0:T(8,128)(2,1)S(1)}, bf16[128,1536]{1,0:T(8,128)(2,1)S(1)}, u32[]{:S(2)}, u32[]{:S(2)}) %collective-permute-start.10) | collective-permute-done | bytes 393248 | tf_op jit(solution)/shard_map/ppermute | solution.py:448
  32.1 1.6 %collective-permute-start.13 = (bf16[48,1536]{1,0:T(8,128)(2,1)S(1)}, bf16[48,1536]{1,0:T(8,128)(2,1)S(1)}, u32[]{:S(2)}, u32[]{:S(2)}) collective-permute-start(bf16[48,1536]{1,0:T(8,128)(2,1)S(1)} %slice.7), channel_id=1, source_target_pairs={{0,4},{2,6},{4,0},{6,2},{8,12},{10,14},{12,8},{14,10},{16,20},{18,... | collective-permute-start | bytes 442376 | tf_op jit(solution)/shard_map/ppermute | solution.py:21
  33.6 1.1 %edge_rows.3 = (bf16[128,1024]{1,0:T(8,128)(2,1)S(1)}, bf16[128,512]{1,0:T(8,128)(2,1)S(1)}) custom-call(s32[7,8,128]{2,1,0:T(8,128)S(1)} %get-tuple-element.40.facts_ref, bf16[2,128,6144]{2,1,0:T(8,128)(2,1)S(1)} %get-tuple-element.41.rows_ref, bf16[128,2048]{1,0:T(8,128)(2,1)S(1)} %collective-permute-done.3.halo_ref), custom_call_target="tpu_custom_call" | custom-call | tf_op jit(solution)/shard_map/edge_rows/pallas_call | solution.py:498
  34.7 0.1 collective-permute-start.5
  34.8 0.5 %collective-permute-start.4 = (bf16[128,512]{1,0:T(8,128)(2,1)S(1)}, bf16[128,512]{1,0:T(8,128)(2,1)S(1)}, u32[]{:S(2)}, u32[]{:S(2)}) collective-permute-start(bf16[128,512]{1,0:T(8,128)(2,1)S(1)} %get-tuple-element.45), channel_id=1, source_target_pairs={{0,2},{2,0},{4,6},{6,4},{8,10},{10,8},{12,14},{14,12},{16,18},{18,... | collective-permute-start | bytes 393224 | tf_op jit(solution)/shard_map/ppermute | solution.py:21
  35.3 0.6 %collective-permute-done.11.rest_1_.rest_6_ = bf16[128,1536]{1,0:T(8,128)(2,1)S(1)} collective-permute-done((bf16[128,1536]{1,0:T(8,128)(2,1)S(1)}, bf16[128,1536]{1,0:T(8,128)(2,1)S(1)}, u32[]{:S(2)}, u32[]{:S(2)}) %collective-permute-start.11) | collective-permute-done | bytes 393248 | tf_op jit(solution)/shard_map/ppermute | solution.py:21
  35.9 0.4 add_products.1.inner_total_ref
  36.3 0.1 collective-permute-done.4.refs_2_
  36.3 0.2 arrange.1
  36.6 0.4 %project.4 = (f32[256,512]{1,0:T(8,128)S(1)}, bf16[256,512]{1,0:T(8,128)(2,1)S(1)}) custom-call(bf16[256,896]{1,0:T(8,128)(2,1)S(1)} %get-tuple-element.57.edge_ref, f32[256,1536]{1,0:T(8,128)S(1)} %add_products.1.inner_total_ref, bf16[128,1536]{1,0:T(8,128)(2,1)S(1)} %copy-done, bf16[128,1536]{1,0:T(8,128)(2,1)S(1)} %collective-permute-done.rest_1_, ...), custom_call_target="tpu_custom_call" | custom-call | tf_op jit(solution)/shard_map/project/pallas_call | solution.py:566
  37.0 0.4 collective-permute-start.15
  37.4 0.4 %project.3 = (f32[256,512]{1,0:T(8,128)S(1)}, bf16[256,512]{1,0:T(8,128)(2,1)S(1)}) custom-call(bf16[256,896]{1,0:T(8,128)(2,1)S(1)} %get-tuple-element.57.edge_ref, f32[256,1536]{1,0:T(8,128)S(1)} %add_products.1.inner_total_ref, bf16[128,1536]{1,0:T(8,128)(2,1)S(1)} %copy-done, bf16[128,1536]{1,0:T(8,128)(2,1)S(1)} %collective-permute-done.rest_1_, ...), custom_call_target="tpu_custom_call" | custom-call | tf_op jit(solution)/shard_map/project/pallas_call | solution.py:566
  37.8 0.3 collective-permute-start.14
  38.1 0.4 %project.5 = (f32[256,512]{1,0:T(8,128)S(1)}, bf16[256,512]{1,0:T(8,128)(2,1)S(1)}) custom-call(bf16[256,896]{1,0:T(8,128)(2,1)S(1)} %get-tuple-element.57.edge_ref, f32[256,1536]{1,0:T(8,128)S(1)} %add_products.1.inner_total_ref, bf16[128,1536]{1,0:T(8,128)(2,1)S(1)} %copy-done, bf16[128,1536]{1,0:T(8,128)(2,1)S(1)} %collective-permute-done.rest_1_, ...), custom_call_target="tpu_custom_call" | custom-call | tf_op jit(solution)/shard_map/project/pallas_call | solution.py:566
  38.5 0.1 collective-permute-done.13.rest_1_
  38.7 0.3 collective-permute-start.16
  38.9 0.2 collective-permute-start.17
  39.2 0.3 collective-permute-start.18
  39.5 0.0 collective-permute-done.14.rest_5_
  39.5 0.3 gather_sums.1.total_ref
  39.8 0.9 %collective-permute-done.18.rest_1_ = bf16[48,1536]{1,0:T(8,128)(2,1)S(1)} collective-permute-done((bf16[48,1536]{1,0:T(8,128)(2,1)S(1)}, bf16[48,1536]{1,0:T(8,128)(2,1)S(1)}, u32[]{:S(2)}, u32[]{:S(2)}) %collective-permute-start.18) | collective-permute-done | bytes 147488 | tf_op jit(solution)/shard_map/ppermute | solution.py:21
  40.8 0.0 collective-permute-done.17.rest_0_
  40.8 0.0 collective-permute-done.16.more_ref
  40.8 1.1 %finish.1 = bf16[256,1536]{1,0:T(8,128)(2,1)} custom-call(bf16[256,256]{1,0:T(8,128)(2,1)S(1)} %get-tuple-element.55.features_ref, f32[256,1536]{1,0:T(8,128)S(1)} %gather_sums.1.total_ref, bf16[256,512]{1,0:T(8,128)(2,1)S(1)} %collective-permute-done.16.more_ref, bf16[80,1536]{1,0:T(8,128)(2,1)S(1)} %collective-permute-done.17.rest_0_, ...), custom_call_target="tpu_custom_call" | custom-call | tf_op jit(solution)/shard_map/finish/pallas_call | solution.py:584
  (8 shorter events, 0.0 us)
Async XLA Ops:
  0.0 8.2 %collective-permute-start.1 = (bf16[2,128,6144]{2,1,0:T(8,128)(2,1)}, bf16[2,128,6144]{2,1,0:T(8,128)(2,1)S(1)}, u32[]{:S(2)}, u32[]{:S(2)}) collective-permute-start(bf16[2,128,6144]{2,1,0:T(8,128)(2,1)} %bitcast.1), channel_id=1, source_target_pairs={{0,2},{2,0},{4,6},{6,4},{8,10},{10,8},{12,14},{14,12},{16,18},{18,... | collective-permute-start | bytes 9437192 | tf_op jit(solution)/shard_map/ppermute | solution.py:21
  0.5 13.3 %collective-permute-start = (bf16[128,1536]{1,0:T(8,128)(2,1)}, bf16[128,1536]{1,0:T(8,128)(2,1)S(1)}, u32[]{:S(2)}, u32[]{:S(2)}) collective-permute-start(bf16[128,1536]{1,0:T(8,128)(2,1)} %rest_0_.7), channel_id=1, source_target_pairs={{0,16},{2,18},{4,20},{6,22},{16,24},{18,26},{20,28},{22,30},{24,8}... | collective-permute-start | bytes 1179656 | tf_op jit(solution)/shard_map/ppermute | solution.py:448
  4.0 11.5 %collective-permute-start.7 = (bf16[128,1536]{1,0:T(8,128)(2,1)}, bf16[128,1536]{1,0:T(8,128)(2,1)S(1)}, u32[]{:S(2)}, u32[]{:S(2)}) collective-permute-start(bf16[128,1536]{1,0:T(8,128)(2,1)} %rest_0_.7), channel_id=1, source_target_pairs={{0,4},{2,6},{4,0},{6,2},{8,12},{10,14},{12,8},{14,10},{16,20},{18,... | collective-permute-start | bytes 1179656 | tf_op jit(solution)/shard_map/ppermute | solution.py:21
  8.2 1.4 %copy-start = (bf16[128,1536]{1,0:T(8,128)(2,1)S(1)}, bf16[128,1536]{1,0:T(8,128)(2,1)}, u32[]{:S(2)}) copy-start(bf16[128,1536]{1,0:T(8,128)(2,1)} %rest_0_.7) | copy-start | bytes 1179652
  8.4 15.5 %collective-permute-start.2 = (bf16[128,2048]{1,0:T(8,128)(2,1)S(1)}, bf16[128,2048]{1,0:T(8,128)(2,1)S(1)}, u32[]{:S(2)}, u32[]{:S(2)}) collective-permute-start(bf16[128,2048]{1,0:T(8,128)(2,1)S(1)} %pack_first.1), channel_id=1, source_target_pairs={{0,1},{1,0},{2,3},{3,2},{4,5},{5,4},{6,7},{7,6},{8,9},{9,8},{10,11... | collective-permute-start | bytes 1572872 | tf_op jit(solution)/shard_map/ppermute | solution.py:494
  9.5 14.4 %collective-permute-start.8 = (bf16[128,1536]{1,0:T(8,128)(2,1)S(1)}, bf16[128,1536]{1,0:T(8,128)(2,1)S(1)}, u32[]{:S(2)}, u32[]{:S(2)}) collective-permute-start(bf16[128,1536]{1,0:T(8,128)(2,1)S(1)} %copy-done), channel_id=1, source_target_pairs={{0,8},{2,10},{4,12},{6,14},{16,0},{18,2},{20,4},{22,6},{24,16},{26... | collective-permute-start | bytes 1179656 | tf_op jit(solution)/shard_map/ppermute | solution.py:448
  11.4 22.2 %collective-permute-start.3 = (bf16[128,2048]{1,0:T(8,128)(2,1)S(1)}, bf16[128,2048]{1,0:T(8,128)(2,1)S(1)}, u32[]{:S(2)}, u32[]{:S(2)}) collective-permute-start(bf16[128,2048]{1,0:T(8,128)(2,1)S(1)} %get-tuple-element.38), channel_id=1, source_target_pairs={{0,1},{1,0},{2,3},{3,2},{4,5},{5,4},{6,7},{7,6},{8,9},{9,8},{10,11... | collective-permute-start | bytes 1572872 | tf_op jit(solution)/shard_map/ppermute | solution.py:494
  13.8 12.8 %collective-permute-start.9 = (bf16[128,1536]{1,0:T(8,128)(2,1)S(1)}, bf16[128,1536]{1,0:T(8,128)(2,1)S(1)}, u32[]{:S(2)}, u32[]{:S(2)}) collective-permute-start(bf16[128,1536]{1,0:T(8,128)(2,1)S(1)} %collective-permute-done.rest_1_), channel_id=1, source_target_pairs={{0,4},{2,6},{4,0},{6,2},{8,12},{10,14},{12,8},{14,10},{16,20},{18,... | collective-permute-start | bytes 1179656 | tf_op jit(solution)/shard_map/ppermute | solution.py:21
  15.5 16.5 %collective-permute-start.10 = (bf16[128,1536]{1,0:T(8,128)(2,1)S(1)}, bf16[128,1536]{1,0:T(8,128)(2,1)S(1)}, u32[]{:S(2)}, u32[]{:S(2)}) collective-permute-start(bf16[128,1536]{1,0:T(8,128)(2,1)S(1)} %collective-permute-done.rest_1_), channel_id=1, source_target_pairs={{0,16},{2,18},{4,20},{6,22},{16,24},{18,26},{20,28},{22,30},{24,8}... | collective-permute-start | bytes 1179656 | tf_op jit(solution)/shard_map/ppermute | solution.py:448
  24.0 3.7 %collective-permute-start.6 = (bf16[128,1024]{1,0:T(8,128)(2,1)S(1)}, bf16[128,1024]{1,0:T(8,128)(2,1)S(1)}, u32[]{:S(2)}, u32[]{:S(2)}) collective-permute-start(bf16[128,1024]{1,0:T(8,128)(2,1)S(1)} %get-tuple-element.47), channel_id=1, source_target_pairs={{0,2},{2,0},{4,6},{6,4},{8,10},{10,8},{12,14},{14,12},{16,18},{18,... | collective-permute-start | bytes 786440 | tf_op jit(solution)/shard_map/ppermute | solution.py:21
  24.0 11.9 %collective-permute-start.11 = (bf16[128,1536]{1,0:T(8,128)(2,1)S(1)}, bf16[128,1536]{1,0:T(8,128)(2,1)S(1)}, u32[]{:S(2)}, u32[]{:S(2)}) collective-permute-start(bf16[128,1536]{1,0:T(8,128)(2,1)S(1)} %collective-permute-done.8.rest_3_), channel_id=1, source_target_pairs={{0,4},{2,6},{4,0},{6,2},{8,12},{10,14},{12,8},{14,10},{16,20},{18,... | collective-permute-start | bytes 1179656 | tf_op jit(solution)/shard_map/ppermute | solution.py:21
  26.6 12.0 %collective-permute-start.12 = (bf16[80,1536]{1,0:T(8,128)(2,1)S(1)}, bf16[80,1536]{1,0:T(8,128)(2,1)S(1)}, u32[]{:S(2)}, u32[]{:S(2)}) collective-permute-start(bf16[80,1536]{1,0:T(8,128)(2,1)S(1)} %slice.6), channel_id=1, source_target_pairs={{0,16},{2,18},{4,20},{6,22},{16,24},{18,26},{20,28},{22,30},{24,8}... | collective-permute-start | bytes 737288 | tf_op jit(solution)/shard_map/ppermute | solution.py:448
  32.1 6.6 %collective-permute-start.13 = (bf16[48,1536]{1,0:T(8,128)(2,1)S(1)}, bf16[48,1536]{1,0:T(8,128)(2,1)S(1)}, u32[]{:S(2)}, u32[]{:S(2)}) collective-permute-start(bf16[48,1536]{1,0:T(8,128)(2,1)S(1)} %slice.7), channel_id=1, source_target_pairs={{0,4},{2,6},{4,0},{6,2},{8,12},{10,14},{12,8},{14,10},{16,20},{18,... | collective-permute-start | bytes 442376 | tf_op jit(solution)/shard_map/ppermute | solution.py:21
  34.7 1.5 %collective-permute-start.5 = (bf16[128,512]{1,0:T(8,128)(2,1)S(1)}, bf16[128,512]{1,0:T(8,128)(2,1)S(1)}, u32[]{:S(2)}, u32[]{:S(2)}) collective-permute-start(bf16[128,512]{1,0:T(8,128)(2,1)S(1)} %get-tuple-element.46), channel_id=1, source_target_pairs={{0,2},{2,0},{4,6},{6,4},{8,10},{10,8},{12,14},{14,12},{16,18},{18,... | collective-permute-start | bytes 393224 | tf_op jit(solution)/shard_map/ppermute | solution.py:21
  34.8 1.5 %collective-permute-start.4 = (bf16[128,512]{1,0:T(8,128)(2,1)S(1)}, bf16[128,512]{1,0:T(8,128)(2,1)S(1)}, u32[]{:S(2)}, u32[]{:S(2)}) collective-permute-start(bf16[128,512]{1,0:T(8,128)(2,1)S(1)} %get-tuple-element.45), channel_id=1, source_target_pairs={{0,2},{2,0},{4,6},{6,4},{8,10},{10,8},{12,14},{14,12},{16,18},{18,... | collective-permute-start | bytes 393224 | tf_op jit(solution)/shard_map/ppermute | solution.py:21
  37.0 2.5 %collective-permute-start.15 = (bf16[256,512]{1,0:T(8,128)(2,1)S(1)}, bf16[256,512]{1,0:T(8,128)(2,1)S(1)}, u32[]{:S(2)}, u32[]{:S(2)}) collective-permute-start(bf16[256,512]{1,0:T(8,128)(2,1)S(1)} %get-tuple-element.62), channel_id=1, source_target_pairs={{0,2},{2,0},{4,6},{6,4},{8,10},{10,8},{12,14},{14,12},{16,18},{18,... | collective-permute-start | bytes 786440 | tf_op jit(solution)/shard_map/ppermute | solution.py:21
  37.8 1.6 %collective-permute-start.14 = (bf16[256,512]{1,0:T(8,128)(2,1)S(1)}, bf16[256,512]{1,0:T(8,128)(2,1)S(1)}, u32[]{:S(2)}, u32[]{:S(2)}) collective-permute-start(bf16[256,512]{1,0:T(8,128)(2,1)S(1)} %get-tuple-element.61), channel_id=1, source_target_pairs={{0,2},{2,0},{4,6},{6,4},{8,10},{10,8},{12,14},{14,12},{16,18},{18,... | collective-permute-start | bytes 786440 | tf_op jit(solution)/shard_map/ppermute | solution.py:21
  38.7 2.1 %collective-permute-start.16 = (bf16[256,512]{1,0:T(8,128)(2,1)S(1)}, bf16[256,512]{1,0:T(8,128)(2,1)S(1)}, u32[]{:S(2)}, u32[]{:S(2)}) collective-permute-start(bf16[256,512]{1,0:T(8,128)(2,1)S(1)} %get-tuple-element.64), channel_id=1, source_target_pairs={{0,2},{2,0},{4,6},{6,4},{8,10},{10,8},{12,14},{14,12},{16,18},{18,... | collective-permute-start | bytes 786440 | tf_op jit(solution)/shard_map/ppermute | solution.py:21
  38.9 1.8 %collective-permute-start.17 = (bf16[80,1536]{1,0:T(8,128)(2,1)S(1)}, bf16[80,1536]{1,0:T(8,128)(2,1)S(1)}, u32[]{:S(2)}, u32[]{:S(2)}) collective-permute-start(bf16[80,1536]{1,0:T(8,128)(2,1)S(1)} %collective-permute-done.12.rest_0_), channel_id=1, source_target_pairs={{0,2},{2,0},{4,6},{6,4},{8,10},{10,8},{12,14},{14,12},{16,18},{18,... | collective-permute-start | bytes 737288 | tf_op jit(solution)/shard_map/ppermute | solution.py:21
  39.2 1.6 %collective-permute-start.18 = (bf16[48,1536]{1,0:T(8,128)(2,1)S(1)}, bf16[48,1536]{1,0:T(8,128)(2,1)S(1)}, u32[]{:S(2)}, u32[]{:S(2)}) collective-permute-start(bf16[48,1536]{1,0:T(8,128)(2,1)S(1)} %collective-permute-done.13.rest_1_), channel_id=1, source_target_pairs={{0,2},{2,0},{4,6},{6,4},{8,10},{10,8},{12,14},{14,12},{16,18},{18,... | collective-permute-start | bytes 442376 | tf_op jit(solution)/shard_map/ppermute | solution.py:21

commit v5 on v4

--- a/solution.py
+++ b/solution.py
@@ -193,8 +193,8 @@
     contract_last = (((1,), (1,)), ((), ()))
     ones = jnp.ones((2 * out_ref.shape[0], HEAD), jnp.bfloat16)
     odd_core = lax.rem(lax.axis_index("dp"), 2) == 1
-    for start in range(0, heads, 4):
-        group = min(4, heads - start)
+    for start in range(0, heads, 8):
+        group = min(8, heads - start)
         scores = []
         for head in range(start, start + group):
             queries = load_queries(head)

time: 42 us -> 42 us (level)
  Pallas kernels: 11.7 us -> 10.6 us
  waiting for transfers between devices: 10.7 us -> 11.5 us
    ppermute x4, waiting for transfers between devices: 8.74 us -> 9.22 us  [around(): lax.ppermute(value, 'dp', [(4 * here + rest, 4 * there + rest) for here,...]
    ppermute x2, starting transfers between devices: 1.86 us -> 2.33 us  [body_edge(): halos = [lax.ppermute(part, 'ctx', [(0, 1), (1, 0)]) for part in packed]]
    pallas_call x1, Pallas kernels: 2.61 us -> 2.14 us  [body_edge(): call(stage_kernel, 'stage', [own.shape, (7, 8, 128)], [HBM()] * 3, dtypes...]
  transfers between devices with their start and end apart: 19 -> 19, of which waited for: 8 -> 7; matrix products, arithmetic and copies ran while one was open for 0% -> 0% of each run, Pallas kernels for 25% -> 23%
where the time goes in v5:
time: 42 us; the launch traced here: 41.9 us
  starting transfers between devices  19.6 us (47%)
  waiting for transfers between devices  11.5 us (27%)
  Pallas kernels  10.6 us (25%)
    ppermute x4, waiting for transfers between devices, around(): lax.ppermute(value, 'dp', [(4 * here + rest, 4 * there + rest) for here,...  9.22 us
    ppermute x4, starting transfers between devices, around(): lax.ppermute(value, 'dp', [(4 * here + rest, 4 * there + rest) for here,...  8.92 us
    ppermute x13, starting transfers between devices, partner(): return lax.ppermute(value, axis, pairs)  8.31 us
    ppermute x2, starting transfers between devices, body_edge(): halos = [lax.ppermute(part, 'ctx', [(0, 1), (1, 0)]) for part in packed]  2.33 us
    ppermute x13, waiting for transfers between devices, partner(): return lax.ppermute(value, axis, pairs)  2.29 us
    pallas_call x1, Pallas kernels, body_edge(): call(stage_kernel, 'stage', [own.shape, (7, 8, 128)], [HBM()] * 3, dtypes...  2.14 us
    pallas_call x2, Pallas kernels, edge_rows(): call(functools.partial(edge_kernel, sum(part_heads[:part])), 'edge_rows',...  1.87 us
    pallas_call x1, Pallas kernels, body_edge(): call(inner_kernel, 'inner_rows', [(block_rows, features), (block_rows, fe...  1.44 us
  transfers between devices with their start and end apart: 19, of which 7 were waited for; matrix products, arithmetic and copies ran while one was open for 0% of the time, Pallas kernels for 23%

profile of v5, /device:TPU:0, one launch (start us, length us, event | category | flops | bytes accessed | tf_op | source)
XLA Modules:
  0.0 41.9 jit_solution(16584048179151841629)
XLA Ops:
  0.0 0.5 %collective-permute-start.1 = (bf16[2,128,6144]{2,1,0:T(8,128)(2,1)}, bf16[2,128,6144]{2,1,0:T(8,128)(2,1)S(1)}, u32[]{:S(2)}, u32[]{:S(2)}) collective-permute-start(bf16[2,128,6144]{2,1,0:T(8,128)(2,1)} %bitcast.1), channel_id=1, source_target_pairs={{0,2},{2,0},{4,6},{6,4},{8,10},{10,8},{12,14},{14,12},{16,18},{18,... | collective-permute-start | bytes 9437192 | tf_op jit(solution)/shard_map/ppermute | solution.py:21
  0.5 3.6 %collective-permute-start = (bf16[128,1536]{1,0:T(8,128)(2,1)}, bf16[128,1536]{1,0:T(8,128)(2,1)S(1)}, u32[]{:S(2)}, u32[]{:S(2)}) collective-permute-start(bf16[128,1536]{1,0:T(8,128)(2,1)} %rest_0_.7), channel_id=1, source_target_pairs={{0,16},{2,18},{4,20},{6,22},{16,24},{18,26},{20,28},{22,30},{24,8}... | collective-permute-start | bytes 1179656 | tf_op jit(solution)/shard_map/ppermute | solution.py:448
  4.0 1.5 %collective-permute-start.7 = (bf16[128,1536]{1,0:T(8,128)(2,1)}, bf16[128,1536]{1,0:T(8,128)(2,1)S(1)}, u32[]{:S(2)}, u32[]{:S(2)}) collective-permute-start(bf16[128,1536]{1,0:T(8,128)(2,1)} %rest_0_.7), channel_id=1, source_target_pairs={{0,4},{2,6},{4,0},{6,2},{8,12},{10,14},{12,8},{14,10},{16,20},{18,... | collective-permute-start | bytes 1179656 | tf_op jit(solution)/shard_map/ppermute | solution.py:21
  5.5 2.1 %stage.1 = (bf16[2,128,6144]{2,1,0:T(8,128)(2,1)S(1)}, s32[7,8,128]{2,1,0:T(8,128)S(1)}) custom-call(s32[1,1,2]{2,1,0:T(1,128)} %sources.1, s32[1,4]{1,0:T(1,128)} %clips.1, bf16[2,128,6144]{2,1,0:T(8,128)(2,1)} %bitcast.2), custom_call_target="tpu_custom_call" | custom-call | tf_op jit(solution)/shard_map/stage/pallas_call | solution.py:466
  7.7 0.0 collective-permute-done.1.partner_ref
  7.7 0.0 copy-start
  7.7 0.2 pack_first.1
  7.9 1.6 %collective-permute-start.2 = (bf16[128,2048]{1,0:T(8,128)(2,1)S(1)}, bf16[128,2048]{1,0:T(8,128)(2,1)S(1)}, u32[]{:S(2)}, u32[]{:S(2)}) collective-permute-start(bf16[128,2048]{1,0:T(8,128)(2,1)S(1)} %pack_first.1), channel_id=1, source_target_pairs={{0,1},{1,0},{2,3},{3,2},{4,5},{5,4},{6,7},{7,6},{8,9},{9,8},{10,11... | collective-permute-start | bytes 1572872 | tf_op jit(solution)/shard_map/ppermute | solution.py:494
  9.5 1.2 %collective-permute-start.8 = (bf16[128,1536]{1,0:T(8,128)(2,1)S(1)}, bf16[128,1536]{1,0:T(8,128)(2,1)S(1)}, u32[]{:S(2)}, u32[]{:S(2)}) collective-permute-start(bf16[128,1536]{1,0:T(8,128)(2,1)S(1)} %copy-done), channel_id=1, source_target_pairs={{0,8},{2,10},{4,12},{6,14},{16,0},{18,2},{20,4},{22,6},{24,16},{26... | collective-permute-start | bytes 1179656 | tf_op jit(solution)/shard_map/ppermute | solution.py:448
  10.7 0.7 %pack.1 = (bf16[2,128,6144]{2,1,0:T(8,128)(2,1)S(1)}, bf16[128,2048]{1,0:T(8,128)(2,1)S(1)}) custom-call(s32[7,8,128]{2,1,0:T(8,128)S(1)} %get-tuple-element.40.facts_ref, bf16[2,128,6144]{2,1,0:T(8,128)(2,1)S(1)} %get-tuple-element.36.own_ref, bf16[2,128,6144]{2,1,0:T(8,128)(2,1)S(1)} %collective-permute-done.1.partner_ref), custom_call_target="tpu_custom_call" | custom-call | tf_op jit(solution)/shard_map/pack/pallas_call | solution.py:486
  11.4 0.7 %collective-permute-start.3 = (bf16[128,2048]{1,0:T(8,128)(2,1)S(1)}, bf16[128,2048]{1,0:T(8,128)(2,1)S(1)}, u32[]{:S(2)}, u32[]{:S(2)}) collective-permute-start(bf16[128,2048]{1,0:T(8,128)(2,1)S(1)} %get-tuple-element.38), channel_id=1, source_target_pairs={{0,1},{1,0},{2,3},{3,2},{4,5},{5,4},{6,7},{7,6},{8,9},{9,8},{10,11... | collective-permute-start | bytes 1572872 | tf_op jit(solution)/shard_map/ppermute | solution.py:494
  12.2 1.6 %collective-permute-done.rest_1_ = bf16[128,1536]{1,0:T(8,128)(2,1)S(1)} collective-permute-done((bf16[128,1536]{1,0:T(8,128)(2,1)}, bf16[128,1536]{1,0:T(8,128)(2,1)S(1)}, u32[]{:S(2)}, u32[]{:S(2)}) %collective-permute-start) | collective-permute-done | bytes 393248 | tf_op jit(solution)/shard_map/ppermute | solution.py:448
  13.8 1.5 %collective-permute-start.9 = (bf16[128,1536]{1,0:T(8,128)(2,1)S(1)}, bf16[128,1536]{1,0:T(8,128)(2,1)S(1)}, u32[]{:S(2)}, u32[]{:S(2)}) collective-permute-start(bf16[128,1536]{1,0:T(8,128)(2,1)S(1)} %collective-permute-done.rest_1_), channel_id=1, source_target_pairs={{0,4},{2,6},{4,0},{6,2},{8,12},{10,14},{12,8},{14,10},{16,20},{18,... | collective-permute-start | bytes 1179656 | tf_op jit(solution)/shard_map/ppermute | solution.py:21
  15.3 0.2 collective-permute-done.7.rest_2_
  15.5 3.1 %collective-permute-start.10 = (bf16[128,1536]{1,0:T(8,128)(2,1)S(1)}, bf16[128,1536]{1,0:T(8,128)(2,1)S(1)}, u32[]{:S(2)}, u32[]{:S(2)}) collective-permute-start(bf16[128,1536]{1,0:T(8,128)(2,1)S(1)} %collective-permute-done.rest_1_), channel_id=1, source_target_pairs={{0,16},{2,18},{4,20},{6,22},{16,24},{18,26},{20,28},{22,30},{24,8}... | collective-permute-start | bytes 1179656 | tf_op jit(solution)/shard_map/ppermute | solution.py:448
  18.6 1.4 %inner_rows.1 = (bf16[128,2048]{1,0:T(8,128)(2,1)S(1)}, bf16[128,1024]{1,0:T(8,128)(2,1)S(1)}) custom-call(s32[7,8,128]{2,1,0:T(8,128)S(1)} %get-tuple-element.40.facts_ref, bf16[2,128,6144]{2,1,0:T(8,128)(2,1)S(1)} %get-tuple-element.41.rows_ref), custom_call_target="tpu_custom_call" | custom-call | tf_op jit(solution)/shard_map/inner_rows/pallas_call | solution.py:510
  20.0 4.0 %collective-permute-done.8.rest_3_ = bf16[128,1536]{1,0:T(8,128)(2,1)S(1)} collective-permute-done((bf16[128,1536]{1,0:T(8,128)(2,1)S(1)}, bf16[128,1536]{1,0:T(8,128)(2,1)S(1)}, u32[]{:S(2)}, u32[]{:S(2)}) %collective-permute-start.8) | collective-permute-done | bytes 393248 | tf_op jit(solution)/shard_map/ppermute | solution.py:448
  24.0 0.0 collective-permute-start.6
  24.0 0.0 collective-permute-done.2.halo_ref
  24.0 1.5 %collective-permute-start.11 = (bf16[128,1536]{1,0:T(8,128)(2,1)S(1)}, bf16[128,1536]{1,0:T(8,128)(2,1)S(1)}, u32[]{:S(2)}, u32[]{:S(2)}) collective-permute-start(bf16[128,1536]{1,0:T(8,128)(2,1)S(1)} %collective-permute-done.8.rest_3_), channel_id=1, source_target_pairs={{0,4},{2,6},{4,0},{6,2},{8,12},{10,14},{12,8},{14,10},{16,20},{18,... | collective-permute-start | bytes 1179656 | tf_op jit(solution)/shard_map/ppermute | solution.py:21
  25.5 0.9 %edge_rows.2 = (bf16[128,1024]{1,0:T(8,128)(2,1)S(1)}, bf16[128,512]{1,0:T(8,128)(2,1)S(1)}) custom-call(s32[7,8,128]{2,1,0:T(8,128)S(1)} %get-tuple-element.40.facts_ref, bf16[2,128,6144]{2,1,0:T(8,128)(2,1)S(1)} %get-tuple-element.41.rows_ref, bf16[128,2048]{1,0:T(8,128)(2,1)S(1)} %collective-permute-done.2.halo_ref), custom_call_target="tpu_custom_call" | custom-call | tf_op jit(solution)/shard_map/edge_rows/pallas_call | solution.py:498
  26.4 1.1 %collective-permute-start.12 = (bf16[80,1536]{1,0:T(8,128)(2,1)S(1)}, bf16[80,1536]{1,0:T(8,128)(2,1)S(1)}, u32[]{:S(2)}, u32[]{:S(2)}) collective-permute-start(bf16[80,1536]{1,0:T(8,128)(2,1)S(1)} %slice.6), channel_id=1, source_target_pairs={{0,16},{2,18},{4,20},{6,22},{16,24},{18,26},{20,28},{22,30},{24,8}... | collective-permute-start | bytes 737288 | tf_op jit(solution)/shard_map/ppermute | solution.py:448
  27.5 0.0 collective-permute-done.6.their_ref
  27.5 0.9 %inner_project.1 = (f32[256,1536]{1,0:T(8,128)S(1)}, bf16[256,256]{1,0:T(8,128)(2,1)S(1)}) custom-call(bf16[128,2048]{1,0:T(8,128)(2,1)S(1)} %get-tuple-element.42.inner_ref, bf16[128,1024]{1,0:T(8,128)(2,1)S(1)} %collective-permute-done.6.their_ref, bf16[128,1536]{1,0:T(8,128)(2,1)S(1)} %copy-done, bf16[128,1536]{1,0:T(8,128)(2,1)S(1)} %collective-permute-done.rest_1_, ...), custom_call_target="tpu_custom_call" | custom-call | tf_op jit(solution)/shard_map/inner_project/pallas_call | solution.py:524
  28.4 3.6 %collective-permute-done.10.rest_0_.rest_5_ = bf16[128,1536]{1,0:T(8,128)(2,1)S(1)} collective-permute-done((bf16[128,1536]{1,0:T(8,128)(2,1)S(1)}, bf16[128,1536]{1,0:T(8,128)(2,1)S(1)}, u32[]{:S(2)}, u32[]{:S(2)}) %collective-permute-start.10) | collective-permute-done | bytes 393248 | tf_op jit(solution)/shard_map/ppermute | solution.py:448
  32.1 1.6 %collective-permute-start.13 = (bf16[48,1536]{1,0:T(8,128)(2,1)S(1)}, bf16[48,1536]{1,0:T(8,128)(2,1)S(1)}, u32[]{:S(2)}, u32[]{:S(2)}) collective-permute-start(bf16[48,1536]{1,0:T(8,128)(2,1)S(1)} %slice.7), channel_id=1, source_target_pairs={{0,4},{2,6},{4,0},{6,2},{8,12},{10,14},{12,8},{14,10},{16,20},{18,... | collective-permute-start | bytes 442376 | tf_op jit(solution)/shard_map/ppermute | solution.py:21
  33.6 0.0 collective-permute-done.3.halo_ref
  33.6 0.9 %edge_rows.3 = (bf16[128,1024]{1,0:T(8,128)(2,1)S(1)}, bf16[128,512]{1,0:T(8,128)(2,1)S(1)}) custom-call(s32[7,8,128]{2,1,0:T(8,128)S(1)} %get-tuple-element.40.facts_ref, bf16[2,128,6144]{2,1,0:T(8,128)(2,1)S(1)} %get-tuple-element.41.rows_ref, bf16[128,2048]{1,0:T(8,128)(2,1)S(1)} %collective-permute-done.3.halo_ref), custom_call_target="tpu_custom_call" | custom-call | tf_op jit(solution)/shard_map/edge_rows/pallas_call | solution.py:498
  34.6 0.1 collective-permute-start.5
  34.6 0.5 %collective-permute-start.4 = (bf16[128,512]{1,0:T(8,128)(2,1)S(1)}, bf16[128,512]{1,0:T(8,128)(2,1)S(1)}, u32[]{:S(2)}, u32[]{:S(2)}) collective-permute-start(bf16[128,512]{1,0:T(8,128)(2,1)S(1)} %get-tuple-element.45), channel_id=1, source_target_pairs={{0,2},{2,0},{4,6},{6,4},{8,10},{10,8},{12,14},{14,12},{16,18},{18,... | collective-permute-start | bytes 393224 | tf_op jit(solution)/shard_map/ppermute | solution.py:21
  35.1 0.7 %collective-permute-done.11.rest_1_.rest_6_ = bf16[128,1536]{1,0:T(8,128)(2,1)S(1)} collective-permute-done((bf16[128,1536]{1,0:T(8,128)(2,1)S(1)}, bf16[128,1536]{1,0:T(8,128)(2,1)S(1)}, u32[]{:S(2)}, u32[]{:S(2)}) %collective-permute-start.11) | collective-permute-done | bytes 393248 | tf_op jit(solution)/shard_map/ppermute | solution.py:21
  35.9 0.4 add_products.1.inner_total_ref
  36.2 0.0 collective-permute-done.5.refs_3_
  36.3 0.0 collective-permute-done.4.refs_2_
  36.3 0.2 arrange.1
  36.5 0.4 %project.4 = (f32[256,512]{1,0:T(8,128)S(1)}, bf16[256,512]{1,0:T(8,128)(2,1)S(1)}) custom-call(bf16[256,896]{1,0:T(8,128)(2,1)S(1)} %get-tuple-element.57.edge_ref, f32[256,1536]{1,0:T(8,128)S(1)} %add_products.1.inner_total_ref, bf16[128,1536]{1,0:T(8,128)(2,1)S(1)} %copy-done, bf16[128,1536]{1,0:T(8,128)(2,1)S(1)} %collective-permute-done.rest_1_, ...), custom_call_target="tpu_custom_call" | custom-call | tf_op jit(solution)/shard_map/project/pallas_call | solution.py:566
  36.9 0.3 collective-permute-start.15
  37.2 0.4 %project.3 = (f32[256,512]{1,0:T(8,128)S(1)}, bf16[256,512]{1,0:T(8,128)(2,1)S(1)}) custom-call(bf16[256,896]{1,0:T(8,128)(2,1)S(1)} %get-tuple-element.57.edge_ref, f32[256,1536]{1,0:T(8,128)S(1)} %add_products.1.inner_total_ref, bf16[128,1536]{1,0:T(8,128)(2,1)S(1)} %copy-done, bf16[128,1536]{1,0:T(8,128)(2,1)S(1)} %collective-permute-done.rest_1_, ...), custom_call_target="tpu_custom_call" | custom-call | tf_op jit(solution)/shard_map/project/pallas_call | solution.py:566
  37.7 0.4 collective-permute-start.14
  38.0 0.4 %project.5 = (f32[256,512]{1,0:T(8,128)S(1)}, bf16[256,512]{1,0:T(8,128)(2,1)S(1)}) custom-call(bf16[256,896]{1,0:T(8,128)(2,1)S(1)} %get-tuple-element.57.edge_ref, f32[256,1536]{1,0:T(8,128)S(1)} %add_products.1.inner_total_ref, bf16[128,1536]{1,0:T(8,128)(2,1)S(1)} %copy-done, bf16[128,1536]{1,0:T(8,128)(2,1)S(1)} %collective-permute-done.rest_1_, ...), custom_call_target="tpu_custom_call" | custom-call | tf_op jit(solution)/shard_map/project/pallas_call | solution.py:566
  38.5 0.2 collective-permute-done.13.rest_1_
  38.6 0.0 collective-permute-done.12.rest_0_
  38.7 0.1 collective-permute-start.16
  38.8 0.4 collective-permute-start.17
  39.2 0.1 collective-permute-start.18
  39.3 0.3 gather_sums.1.total_ref
  39.6 1.1 %collective-permute-done.18.rest_1_ = bf16[48,1536]{1,0:T(8,128)(2,1)S(1)} collective-permute-done((bf16[48,1536]{1,0:T(8,128)(2,1)S(1)}, bf16[48,1536]{1,0:T(8,128)(2,1)S(1)}, u32[]{:S(2)}, u32[]{:S(2)}) %collective-permute-start.18) | collective-permute-done | bytes 147488 | tf_op jit(solution)/shard_map/ppermute | solution.py:21
  40.8 1.1 %finish.1 = bf16[256,1536]{1,0:T(8,128)(2,1)} custom-call(bf16[256,256]{1,0:T(8,128)(2,1)S(1)} %get-tuple-element.55.features_ref, f32[256,1536]{1,0:T(8,128)S(1)} %gather_sums.1.total_ref, bf16[256,512]{1,0:T(8,128)(2,1)S(1)} %collective-permute-done.16.more_ref, bf16[80,1536]{1,0:T(8,128)(2,1)S(1)} %collective-permute-done.17.rest_0_, ...), custom_call_target="tpu_custom_call" | custom-call | tf_op jit(solution)/shard_map/finish/pallas_call | solution.py:584
  (8 shorter events, 0.0 us)
Async XLA Ops:
  0.0 7.7 %collective-permute-start.1 = (bf16[2,128,6144]{2,1,0:T(8,128)(2,1)}, bf16[2,128,6144]{2,1,0:T(8,128)(2,1)S(1)}, u32[]{:S(2)}, u32[]{:S(2)}) collective-permute-start(bf16[2,128,6144]{2,1,0:T(8,128)(2,1)} %bitcast.1), channel_id=1, source_target_pairs={{0,2},{2,0},{4,6},{6,4},{8,10},{10,8},{12,14},{14,12},{16,18},{18,... | collective-permute-start | bytes 9437192 | tf_op jit(solution)/shard_map/ppermute | solution.py:21
  0.5 13.3 %collective-permute-start = (bf16[128,1536]{1,0:T(8,128)(2,1)}, bf16[128,1536]{1,0:T(8,128)(2,1)S(1)}, u32[]{:S(2)}, u32[]{:S(2)}) collective-permute-start(bf16[128,1536]{1,0:T(8,128)(2,1)} %rest_0_.7), channel_id=1, source_target_pairs={{0,16},{2,18},{4,20},{6,22},{16,24},{18,26},{20,28},{22,30},{24,8}... | collective-permute-start | bytes 1179656 | tf_op jit(solution)/shard_map/ppermute | solution.py:448
  4.0 11.5 %collective-permute-start.7 = (bf16[128,1536]{1,0:T(8,128)(2,1)}, bf16[128,1536]{1,0:T(8,128)(2,1)S(1)}, u32[]{:S(2)}, u32[]{:S(2)}) collective-permute-start(bf16[128,1536]{1,0:T(8,128)(2,1)} %rest_0_.7), channel_id=1, source_target_pairs={{0,4},{2,6},{4,0},{6,2},{8,12},{10,14},{12,8},{14,10},{16,20},{18,... | collective-permute-start | bytes 1179656 | tf_op jit(solution)/shard_map/ppermute | solution.py:21
  7.7 1.9 %copy-start = (bf16[128,1536]{1,0:T(8,128)(2,1)S(1)}, bf16[128,1536]{1,0:T(8,128)(2,1)}, u32[]{:S(2)}) copy-start(bf16[128,1536]{1,0:T(8,128)(2,1)} %rest_0_.7) | copy-start | bytes 1179652
  7.9 16.0 %collective-permute-start.2 = (bf16[128,2048]{1,0:T(8,128)(2,1)S(1)}, bf16[128,2048]{1,0:T(8,128)(2,1)S(1)}, u32[]{:S(2)}, u32[]{:S(2)}) collective-permute-start(bf16[128,2048]{1,0:T(8,128)(2,1)S(1)} %pack_first.1), channel_id=1, source_target_pairs={{0,1},{1,0},{2,3},{3,2},{4,5},{5,4},{6,7},{7,6},{8,9},{9,8},{10,11... | collective-permute-start | bytes 1572872 | tf_op jit(solution)/shard_map/ppermute | solution.py:494
  9.5 14.4 %collective-permute-start.8 = (bf16[128,1536]{1,0:T(8,128)(2,1)S(1)}, bf16[128,1536]{1,0:T(8,128)(2,1)S(1)}, u32[]{:S(2)}, u32[]{:S(2)}) collective-permute-start(bf16[128,1536]{1,0:T(8,128)(2,1)S(1)} %copy-done), channel_id=1, source_target_pairs={{0,8},{2,10},{4,12},{6,14},{16,0},{18,2},{20,4},{22,6},{24,16},{26... | collective-permute-start | bytes 1179656 | tf_op jit(solution)/shard_map/ppermute | solution.py:448
  11.4 22.2 %collective-permute-start.3 = (bf16[128,2048]{1,0:T(8,128)(2,1)S(1)}, bf16[128,2048]{1,0:T(8,128)(2,1)S(1)}, u32[]{:S(2)}, u32[]{:S(2)}) collective-permute-start(bf16[128,2048]{1,0:T(8,128)(2,1)S(1)} %get-tuple-element.38), channel_id=1, source_target_pairs={{0,1},{1,0},{2,3},{3,2},{4,5},{5,4},{6,7},{7,6},{8,9},{9,8},{10,11... | collective-permute-start | bytes 1572872 | tf_op jit(solution)/shard_map/ppermute | solution.py:494
  13.8 12.6 %collective-permute-start.9 = (bf16[128,1536]{1,0:T(8,128)(2,1)S(1)}, bf16[128,1536]{1,0:T(8,128)(2,1)S(1)}, u32[]{:S(2)}, u32[]{:S(2)}) collective-permute-start(bf16[128,1536]{1,0:T(8,128)(2,1)S(1)} %collective-permute-done.rest_1_), channel_id=1, source_target_pairs={{0,4},{2,6},{4,0},{6,2},{8,12},{10,14},{12,8},{14,10},{16,20},{18,... | collective-permute-start | bytes 1179656 | tf_op jit(solution)/shard_map/ppermute | solution.py:21
  15.5 16.5 %collective-permute-start.10 = (bf16[128,1536]{1,0:T(8,128)(2,1)S(1)}, bf16[128,1536]{1,0:T(8,128)(2,1)S(1)}, u32[]{:S(2)}, u32[]{:S(2)}) collective-permute-start(bf16[128,1536]{1,0:T(8,128)(2,1)S(1)} %collective-permute-done.rest_1_), channel_id=1, source_target_pairs={{0,16},{2,18},{4,20},{6,22},{16,24},{18,26},{20,28},{22,30},{24,8}... | collective-permute-start | bytes 1179656 | tf_op jit(solution)/shard_map/ppermute | solution.py:448
  24.0 3.6 %collective-permute-start.6 = (bf16[128,1024]{1,0:T(8,128)(2,1)S(1)}, bf16[128,1024]{1,0:T(8,128)(2,1)S(1)}, u32[]{:S(2)}, u32[]{:S(2)}) collective-permute-start(bf16[128,1024]{1,0:T(8,128)(2,1)S(1)} %get-tuple-element.47), channel_id=1, source_target_pairs={{0,2},{2,0},{4,6},{6,4},{8,10},{10,8},{12,14},{14,12},{16,18},{18,... | collective-permute-start | bytes 786440 | tf_op jit(solution)/shard_map/ppermute | solution.py:21
  24.0 11.9 %collective-permute-start.11 = (bf16[128,1536]{1,0:T(8,128)(2,1)S(1)}, bf16[128,1536]{1,0:T(8,128)(2,1)S(1)}, u32[]{:S(2)}, u32[]{:S(2)}) collective-permute-start(bf16[128,1536]{1,0:T(8,128)(2,1)S(1)} %collective-permute-done.8.rest_3_), channel_id=1, source_target_pairs={{0,4},{2,6},{4,0},{6,2},{8,12},{10,14},{12,8},{14,10},{16,20},{18,... | collective-permute-start | bytes 1179656 | tf_op jit(solution)/shard_map/ppermute | solution.py:21
  26.4 12.2 %collective-permute-start.12 = (bf16[80,1536]{1,0:T(8,128)(2,1)S(1)}, bf16[80,1536]{1,0:T(8,128)(2,1)S(1)}, u32[]{:S(2)}, u32[]{:S(2)}) collective-permute-start(bf16[80,1536]{1,0:T(8,128)(2,1)S(1)} %slice.6), channel_id=1, source_target_pairs={{0,16},{2,18},{4,20},{6,22},{16,24},{18,26},{20,28},{22,30},{24,8}... | collective-permute-start | bytes 737288 | tf_op jit(solution)/shard_map/ppermute | solution.py:448
  32.1 6.6 %collective-permute-start.13 = (bf16[48,1536]{1,0:T(8,128)(2,1)S(1)}, bf16[48,1536]{1,0:T(8,128)(2,1)S(1)}, u32[]{:S(2)}, u32[]{:S(2)}) collective-permute-start(bf16[48,1536]{1,0:T(8,128)(2,1)S(1)} %slice.7), channel_id=1, source_target_pairs={{0,4},{2,6},{4,0},{6,2},{8,12},{10,14},{12,8},{14,10},{16,20},{18,... | collective-permute-start | bytes 442376 | tf_op jit(solution)/shard_map/ppermute | solution.py:21
  34.6 1.7 %collective-permute-start.5 = (bf16[128,512]{1,0:T(8,128)(2,1)S(1)}, bf16[128,512]{1,0:T(8,128)(2,1)S(1)}, u32[]{:S(2)}, u32[]{:S(2)}) collective-permute-start(bf16[128,512]{1,0:T(8,128)(2,1)S(1)} %get-tuple-element.46), channel_id=1, source_target_pairs={{0,2},{2,0},{4,6},{6,4},{8,10},{10,8},{12,14},{14,12},{16,18},{18,... | collective-permute-start | bytes 393224 | tf_op jit(solution)/shard_map/ppermute | solution.py:21
  34.6 1.6 %collective-permute-start.4 = (bf16[128,512]{1,0:T(8,128)(2,1)S(1)}, bf16[128,512]{1,0:T(8,128)(2,1)S(1)}, u32[]{:S(2)}, u32[]{:S(2)}) collective-permute-start(bf16[128,512]{1,0:T(8,128)(2,1)S(1)} %get-tuple-element.45), channel_id=1, source_target_pairs={{0,2},{2,0},{4,6},{6,4},{8,10},{10,8},{12,14},{14,12},{16,18},{18,... | collective-permute-start | bytes 393224 | tf_op jit(solution)/shard_map/ppermute | solution.py:21
  36.9 2.3 %collective-permute-start.15 = (bf16[256,512]{1,0:T(8,128)(2,1)S(1)}, bf16[256,512]{1,0:T(8,128)(2,1)S(1)}, u32[]{:S(2)}, u32[]{:S(2)}) collective-permute-start(bf16[256,512]{1,0:T(8,128)(2,1)S(1)} %get-tuple-element.62), channel_id=1, source_target_pairs={{0,2},{2,0},{4,6},{6,4},{8,10},{10,8},{12,14},{14,12},{16,18},{18,... | collective-permute-start | bytes 786440 | tf_op jit(solution)/shard_map/ppermute | solution.py:21
  37.7 1.6 %collective-permute-start.14 = (bf16[256,512]{1,0:T(8,128)(2,1)S(1)}, bf16[256,512]{1,0:T(8,128)(2,1)S(1)}, u32[]{:S(2)}, u32[]{:S(2)}) collective-permute-start(bf16[256,512]{1,0:T(8,128)(2,1)S(1)} %get-tuple-element.61), channel_id=1, source_target_pairs={{0,2},{2,0},{4,6},{6,4},{8,10},{10,8},{12,14},{14,12},{16,18},{18,... | collective-permute-start | bytes 786440 | tf_op jit(solution)/shard_map/ppermute | solution.py:21
  38.7 2.1 %collective-permute-start.16 = (bf16[256,512]{1,0:T(8,128)(2,1)S(1)}, bf16[256,512]{1,0:T(8,128)(2,1)S(1)}, u32[]{:S(2)}, u32[]{:S(2)}) collective-permute-start(bf16[256,512]{1,0:T(8,128)(2,1)S(1)} %get-tuple-element.64), channel_id=1, source_target_pairs={{0,2},{2,0},{4,6},{6,4},{8,10},{10,8},{12,14},{14,12},{16,18},{18,... | collective-permute-start | bytes 786440 | tf_op jit(solution)/shard_map/ppermute | solution.py:21
  38.8 2.0 %collective-permute-start.17 = (bf16[80,1536]{1,0:T(8,128)(2,1)S(1)}, bf16[80,1536]{1,0:T(8,128)(2,1)S(1)}, u32[]{:S(2)}, u32[]{:S(2)}) collective-permute-start(bf16[80,1536]{1,0:T(8,128)(2,1)S(1)} %collective-permute-done.12.rest_0_), channel_id=1, source_target_pairs={{0,2},{2,0},{4,6},{6,4},{8,10},{10,8},{12,14},{14,12},{16,18},{18,... | collective-permute-start | bytes 737288 | tf_op jit(solution)/shard_map/ppermute | solution.py:21
  39.2 1.6 %collective-permute-start.18 = (bf16[48,1536]{1,0:T(8,128)(2,1)S(1)}, bf16[48,1536]{1,0:T(8,128)(2,1)S(1)}, u32[]{:S(2)}, u32[]{:S(2)}) collective-permute-start(bf16[48,1536]{1,0:T(8,128)(2,1)S(1)} %collective-permute-done.13.rest_1_), channel_id=1, source_target_pairs={{0,2},{2,0},{4,6},{6,4},{8,10},{10,8},{12,14},{14,12},{16,18},{18,... | collective-permute-start | bytes 442376 | tf_op jit(solution)/shard_map/ppermute | solution.py:21

commit v6 on v5

--- a/solution.py
+++ b/solution.py
@@ -193,8 +193,8 @@
     contract_last = (((1,), (1,)), ((), ()))
     ones = jnp.ones((2 * out_ref.shape[0], HEAD), jnp.bfloat16)
     odd_core = lax.rem(lax.axis_index("dp"), 2) == 1
-    for start in range(0, heads, 8):
-        group = min(8, heads - start)
+    for start in range(0, heads, 2):
+        group = min(2, heads - start)
         scores = []
         for head in range(start, start + group):
             queries = load_queries(head)

time: 42 us -> 42.4 us (level)
  waiting for transfers between devices: 11.5 us -> 9.4 us
  starting transfers between devices: 19.6 us -> 21.2 us
  Pallas kernels: 10.6 us -> 11.5 us
    ppermute x4, waiting for transfers between devices: 9.22 us -> 7.6 us  [around(): lax.ppermute(value, 'dp', [(4 * here + rest, 4 * there + rest) for here,...]
    pallas_call x1, Pallas kernels: 2.14 us -> 0.81 us  [body_edge(): call(stage_kernel, 'stage', [own.shape, (7, 8, 128)], [HBM()] * 3, dtypes...]
    pallas_call x2, Pallas kernels: 1.87 us -> 3.03 us  [edge_rows(): call(functools.partial(edge_kernel, sum(part_heads[:part])), 'edge_rows',...]
    pallas_call x1, Pallas kernels: 1.44 us -> 2.5 us  [body_edge(): call(inner_kernel, 'inner_rows', [(block_rows, features), (block_rows, fe...]
    ppermute x2, starting transfers between devices: 2.33 us -> 3.27 us  [body_edge(): halos = [lax.ppermute(part, 'ctx', [(0, 1), (1, 0)]) for part in packed]]
    ppermute x13, waiting for transfers between devices: 2.29 us -> 1.79 us  [partner(): return lax.ppermute(value, axis, pairs)]
  transfers between devices with their start and end apart: 19 -> 19, of which waited for: 7 -> 8; matrix products, arithmetic and copies ran while one was open for 0% -> 0% of each run, Pallas kernels for 23% -> 25%
where the time goes in v6:
time: 42.4 us; the launch traced here: 42.2 us
  starting transfers between devices  21.2 us (50%)
  Pallas kernels  11.5 us (27%)
  waiting for transfers between devices  9.4 us (22%)
    ppermute x4, starting transfers between devices, around(): lax.ppermute(value, 'dp', [(4 * here + rest, 4 * there + rest) for here,...  9.3 us
    ppermute x13, starting transfers between devices, partner(): return lax.ppermute(value, axis, pairs)  8.59 us
    ppermute x4, waiting for transfers between devices, around(): lax.ppermute(value, 'dp', [(4 * here + rest, 4 * there + rest) for here,...  7.6 us
    ppermute x2, starting transfers between devices, body_edge(): halos = [lax.ppermute(part, 'ctx', [(0, 1), (1, 0)]) for part in packed]  3.27 us
    pallas_call x2, Pallas kernels, edge_rows(): call(functools.partial(edge_kernel, sum(part_heads[:part])), 'edge_rows',...  3.03 us
    pallas_call x1, Pallas kernels, body_edge(): call(inner_kernel, 'inner_rows', [(block_rows, features), (block_rows, fe...  2.5 us
    ppermute x13, waiting for transfers between devices, partner(): return lax.ppermute(value, axis, pairs)  1.79 us
    pallas_call x3, Pallas kernels, body_edge(): call(functools.partial(project_kernel, part * columns), 'project', [(loca...  1.31 us
  transfers between devices with their start and end apart: 19, of which 8 were waited for; matrix products, arithmetic and copies ran while one was open for 0% of the time, Pallas kernels for 25%

profile of v6, /device:TPU:0, one launch (start us, length us, event | category | flops | bytes accessed | tf_op | source)
XLA Modules:
  0.0 42.2 jit_solution(1096926927616146511)
XLA Ops:
  0.0 0.5 %collective-permute-start.1 = (bf16[2,128,6144]{2,1,0:T(8,128)(2,1)}, bf16[2,128,6144]{2,1,0:T(8,128)(2,1)S(1)}, u32[]{:S(2)}, u32[]{:S(2)}) collective-permute-start(bf16[2,128,6144]{2,1,0:T(8,128)(2,1)} %bitcast.1), channel_id=1, source_target_pairs={{0,2},{2,0},{4,6},{6,4},{8,10},{10,8},{12,14},{14,12},{16,18},{18,... | collective-permute-start | bytes 9437192 | tf_op jit(solution)/shard_map/ppermute | solution.py:21
  0.5 3.6 %collective-permute-start = (bf16[128,1536]{1,0:T(8,128)(2,1)}, bf16[128,1536]{1,0:T(8,128)(2,1)S(1)}, u32[]{:S(2)}, u32[]{:S(2)}) collective-permute-start(bf16[128,1536]{1,0:T(8,128)(2,1)} %rest_0_.7), channel_id=1, source_target_pairs={{0,16},{2,18},{4,20},{6,22},{16,24},{18,26},{20,28},{22,30},{24,8}... | collective-permute-start | bytes 1179656 | tf_op jit(solution)/shard_map/ppermute | solution.py:448
  4.0 1.5 %collective-permute-start.7 = (bf16[128,1536]{1,0:T(8,128)(2,1)}, bf16[128,1536]{1,0:T(8,128)(2,1)S(1)}, u32[]{:S(2)}, u32[]{:S(2)}) collective-permute-start(bf16[128,1536]{1,0:T(8,128)(2,1)} %rest_0_.7), channel_id=1, source_target_pairs={{0,4},{2,6},{4,0},{6,2},{8,12},{10,14},{12,8},{14,10},{16,20},{18,... | collective-permute-start | bytes 1179656 | tf_op jit(solution)/shard_map/ppermute | solution.py:21
  5.5 0.8 %stage.1 = (bf16[2,128,6144]{2,1,0:T(8,128)(2,1)S(1)}, s32[7,8,128]{2,1,0:T(8,128)S(1)}) custom-call(s32[1,1,2]{2,1,0:T(1,128)} %sources.1, s32[1,4]{1,0:T(1,128)} %clips.1, bf16[2,128,6144]{2,1,0:T(8,128)(2,1)} %bitcast.2), custom_call_target="tpu_custom_call" | custom-call | tf_op jit(solution)/shard_map/stage/pallas_call | solution.py:466
  6.3 0.0 collective-permute-done.1.partner_ref
  6.4 0.0 copy-start
  6.4 0.2 pack_first.1
  6.6 2.5 %collective-permute-start.2 = (bf16[128,2048]{1,0:T(8,128)(2,1)S(1)}, bf16[128,2048]{1,0:T(8,128)(2,1)S(1)}, u32[]{:S(2)}, u32[]{:S(2)}) collective-permute-start(bf16[128,2048]{1,0:T(8,128)(2,1)S(1)} %pack_first.1), channel_id=1, source_target_pairs={{0,1},{1,0},{2,3},{3,2},{4,5},{5,4},{6,7},{7,6},{8,9},{9,8},{10,11... | collective-permute-start | bytes 1572872 | tf_op jit(solution)/shard_map/ppermute | solution.py:494
  9.2 1.6 %collective-permute-start.8 = (bf16[128,1536]{1,0:T(8,128)(2,1)S(1)}, bf16[128,1536]{1,0:T(8,128)(2,1)S(1)}, u32[]{:S(2)}, u32[]{:S(2)}) collective-permute-start(bf16[128,1536]{1,0:T(8,128)(2,1)S(1)} %copy-done), channel_id=1, source_target_pairs={{0,8},{2,10},{4,12},{6,14},{16,0},{18,2},{20,4},{22,6},{24,16},{26... | collective-permute-start | bytes 1179656 | tf_op jit(solution)/shard_map/ppermute | solution.py:448
  10.7 0.7 %pack.1 = (bf16[2,128,6144]{2,1,0:T(8,128)(2,1)S(1)}, bf16[128,2048]{1,0:T(8,128)(2,1)S(1)}) custom-call(s32[7,8,128]{2,1,0:T(8,128)S(1)} %get-tuple-element.40.facts_ref, bf16[2,128,6144]{2,1,0:T(8,128)(2,1)S(1)} %get-tuple-element.36.own_ref, bf16[2,128,6144]{2,1,0:T(8,128)(2,1)S(1)} %collective-permute-done.1.partner_ref), custom_call_target="tpu_custom_call" | custom-call | tf_op jit(solution)/shard_map/pack/pallas_call | solution.py:486
  11.4 0.7 %collective-permute-start.3 = (bf16[128,2048]{1,0:T(8,128)(2,1)S(1)}, bf16[128,2048]{1,0:T(8,128)(2,1)S(1)}, u32[]{:S(2)}, u32[]{:S(2)}) collective-permute-start(bf16[128,2048]{1,0:T(8,128)(2,1)S(1)} %get-tuple-element.38), channel_id=1, source_target_pairs={{0,1},{1,0},{2,3},{3,2},{4,5},{5,4},{6,7},{7,6},{8,9},{9,8},{10,11... | collective-permute-start | bytes 1572872 | tf_op jit(solution)/shard_map/ppermute | solution.py:494
  12.2 1.6 %collective-permute-done.rest_1_ = bf16[128,1536]{1,0:T(8,128)(2,1)S(1)} collective-permute-done((bf16[128,1536]{1,0:T(8,128)(2,1)}, bf16[128,1536]{1,0:T(8,128)(2,1)S(1)}, u32[]{:S(2)}, u32[]{:S(2)}) %collective-permute-start) | collective-permute-done | bytes 393248 | tf_op jit(solution)/shard_map/ppermute | solution.py:448
  13.8 1.5 %collective-permute-start.9 = (bf16[128,1536]{1,0:T(8,128)(2,1)S(1)}, bf16[128,1536]{1,0:T(8,128)(2,1)S(1)}, u32[]{:S(2)}, u32[]{:S(2)}) collective-permute-start(bf16[128,1536]{1,0:T(8,128)(2,1)S(1)} %collective-permute-done.rest_1_), channel_id=1, source_target_pairs={{0,4},{2,6},{4,0},{6,2},{8,12},{10,14},{12,8},{14,10},{16,20},{18,... | collective-permute-start | bytes 1179656 | tf_op jit(solution)/shard_map/ppermute | solution.py:21
  15.3 0.2 collective-permute-done.7.rest_2_
  15.5 3.1 %collective-permute-start.10 = (bf16[128,1536]{1,0:T(8,128)(2,1)S(1)}, bf16[128,1536]{1,0:T(8,128)(2,1)S(1)}, u32[]{:S(2)}, u32[]{:S(2)}) collective-permute-start(bf16[128,1536]{1,0:T(8,128)(2,1)S(1)} %collective-permute-done.rest_1_), channel_id=1, source_target_pairs={{0,16},{2,18},{4,20},{6,22},{16,24},{18,26},{20,28},{22,30},{24,8}... | collective-permute-start | bytes 1179656 | tf_op jit(solution)/shard_map/ppermute | solution.py:448
  18.6 2.5 %inner_rows.1 = (bf16[128,2048]{1,0:T(8,128)(2,1)S(1)}, bf16[128,1024]{1,0:T(8,128)(2,1)S(1)}) custom-call(s32[7,8,128]{2,1,0:T(8,128)S(1)} %get-tuple-element.40.facts_ref, bf16[2,128,6144]{2,1,0:T(8,128)(2,1)S(1)} %get-tuple-element.41.rows_ref), custom_call_target="tpu_custom_call" | custom-call | tf_op jit(solution)/shard_map/inner_rows/pallas_call | solution.py:510
  21.1 2.9 %collective-permute-done.8.rest_3_ = bf16[128,1536]{1,0:T(8,128)(2,1)S(1)} collective-permute-done((bf16[128,1536]{1,0:T(8,128)(2,1)S(1)}, bf16[128,1536]{1,0:T(8,128)(2,1)S(1)}, u32[]{:S(2)}, u32[]{:S(2)}) %collective-permute-start.8) | collective-permute-done | bytes 393248 | tf_op jit(solution)/shard_map/ppermute | solution.py:448
  24.0 0.0 collective-permute-start.6
  24.0 1.5 %collective-permute-start.11 = (bf16[128,1536]{1,0:T(8,128)(2,1)S(1)}, bf16[128,1536]{1,0:T(8,128)(2,1)S(1)}, u32[]{:S(2)}, u32[]{:S(2)}) collective-permute-start(bf16[128,1536]{1,0:T(8,128)(2,1)S(1)} %collective-permute-done.8.rest_3_), channel_id=1, source_target_pairs={{0,4},{2,6},{4,0},{6,2},{8,12},{10,14},{12,8},{14,10},{16,20},{18,... | collective-permute-start | bytes 1179656 | tf_op jit(solution)/shard_map/ppermute | solution.py:21
  25.5 1.5 %edge_rows.2 = (bf16[128,1024]{1,0:T(8,128)(2,1)S(1)}, bf16[128,512]{1,0:T(8,128)(2,1)S(1)}) custom-call(s32[7,8,128]{2,1,0:T(8,128)S(1)} %get-tuple-element.40.facts_ref, bf16[2,128,6144]{2,1,0:T(8,128)(2,1)S(1)} %get-tuple-element.41.rows_ref, bf16[128,2048]{1,0:T(8,128)(2,1)S(1)} %collective-permute-done.2.halo_ref), custom_call_target="tpu_custom_call" | custom-call | tf_op jit(solution)/shard_map/edge_rows/pallas_call | solution.py:498
  27.0 1.1 %collective-permute-start.12 = (bf16[80,1536]{1,0:T(8,128)(2,1)S(1)}, bf16[80,1536]{1,0:T(8,128)(2,1)S(1)}, u32[]{:S(2)}, u32[]{:S(2)}) collective-permute-start(bf16[80,1536]{1,0:T(8,128)(2,1)S(1)} %slice.6), channel_id=1, source_target_pairs={{0,16},{2,18},{4,20},{6,22},{16,24},{18,26},{20,28},{22,30},{24,8}... | collective-permute-start | bytes 737288 | tf_op jit(solution)/shard_map/ppermute | solution.py:448
  28.1 0.9 %inner_project.1 = (f32[256,1536]{1,0:T(8,128)S(1)}, bf16[256,256]{1,0:T(8,128)(2,1)S(1)}) custom-call(bf16[128,2048]{1,0:T(8,128)(2,1)S(1)} %get-tuple-element.42.inner_ref, bf16[128,1024]{1,0:T(8,128)(2,1)S(1)} %collective-permute-done.6.their_ref, bf16[128,1536]{1,0:T(8,128)(2,1)S(1)} %copy-done, bf16[128,1536]{1,0:T(8,128)(2,1)S(1)} %collective-permute-done.rest_1_, ...), custom_call_target="tpu_custom_call" | custom-call | tf_op jit(solution)/shard_map/inner_project/pallas_call | solution.py:524
  29.0 3.1 %collective-permute-done.10.rest_0_.rest_5_ = bf16[128,1536]{1,0:T(8,128)(2,1)S(1)} collective-permute-done((bf16[128,1536]{1,0:T(8,128)(2,1)S(1)}, bf16[128,1536]{1,0:T(8,128)(2,1)S(1)}, u32[]{:S(2)}, u32[]{:S(2)}) %collective-permute-start.10) | collective-permute-done | bytes 393248 | tf_op jit(solution)/shard_map/ppermute | solution.py:448
  32.1 1.6 %collective-permute-start.13 = (bf16[48,1536]{1,0:T(8,128)(2,1)S(1)}, bf16[48,1536]{1,0:T(8,128)(2,1)S(1)}, u32[]{:S(2)}, u32[]{:S(2)}) collective-permute-start(bf16[48,1536]{1,0:T(8,128)(2,1)S(1)} %slice.7), channel_id=1, source_target_pairs={{0,4},{2,6},{4,0},{6,2},{8,12},{10,14},{12,8},{14,10},{16,20},{18,... | collective-permute-start | bytes 442376 | tf_op jit(solution)/shard_map/ppermute | solution.py:21
  33.6 1.5 %edge_rows.3 = (bf16[128,1024]{1,0:T(8,128)(2,1)S(1)}, bf16[128,512]{1,0:T(8,128)(2,1)S(1)}) custom-call(s32[7,8,128]{2,1,0:T(8,128)S(1)} %get-tuple-element.40.facts_ref, bf16[2,128,6144]{2,1,0:T(8,128)(2,1)S(1)} %get-tuple-element.41.rows_ref, bf16[128,2048]{1,0:T(8,128)(2,1)S(1)} %collective-permute-done.3.halo_ref), custom_call_target="tpu_custom_call" | custom-call | tf_op jit(solution)/shard_map/edge_rows/pallas_call | solution.py:498
  35.1 0.1 collective-permute-start.5
  35.2 0.5 %collective-permute-start.4 = (bf16[128,512]{1,0:T(8,128)(2,1)S(1)}, bf16[128,512]{1,0:T(8,128)(2,1)S(1)}, u32[]{:S(2)}, u32[]{:S(2)}) collective-permute-start(bf16[128,512]{1,0:T(8,128)(2,1)S(1)} %get-tuple-element.45), channel_id=1, source_target_pairs={{0,2},{2,0},{4,6},{6,4},{8,10},{10,8},{12,14},{14,12},{16,18},{18,... | collective-permute-start | bytes 393224 | tf_op jit(solution)/shard_map/ppermute | solution.py:21
  35.7 0.2 collective-permute-done.11.rest_1_.rest_6_
  35.9 0.4 add_products.1.inner_total_ref
  36.2 0.3 collective-permute-done.5.refs_3_
  36.6 0.2 collective-permute-done.4.refs_2_
  36.7 0.2 arrange.1
  36.9 0.4 %project.4 = (f32[256,512]{1,0:T(8,128)S(1)}, bf16[256,512]{1,0:T(8,128)(2,1)S(1)}) custom-call(bf16[256,896]{1,0:T(8,128)(2,1)S(1)} %get-tuple-element.57.edge_ref, f32[256,1536]{1,0:T(8,128)S(1)} %add_products.1.inner_total_ref, bf16[128,1536]{1,0:T(8,128)(2,1)S(1)} %copy-done, bf16[128,1536]{1,0:T(8,128)(2,1)S(1)} %collective-permute-done.rest_1_, ...), custom_call_target="tpu_custom_call" | custom-call | tf_op jit(solution)/shard_map/project/pallas_call | solution.py:566
  37.4 0.4 collective-permute-start.15
  37.8 0.4 %project.3 = (f32[256,512]{1,0:T(8,128)S(1)}, bf16[256,512]{1,0:T(8,128)(2,1)S(1)}) custom-call(bf16[256,896]{1,0:T(8,128)(2,1)S(1)} %get-tuple-element.57.edge_ref, f32[256,1536]{1,0:T(8,128)S(1)} %add_products.1.inner_total_ref, bf16[128,1536]{1,0:T(8,128)(2,1)S(1)} %copy-done, bf16[128,1536]{1,0:T(8,128)(2,1)S(1)} %collective-permute-done.rest_1_, ...), custom_call_target="tpu_custom_call" | custom-call | tf_op jit(solution)/shard_map/project/pallas_call | solution.py:566
  38.2 0.3 collective-permute-start.14
  38.5 0.4 %project.5 = (f32[256,512]{1,0:T(8,128)S(1)}, bf16[256,512]{1,0:T(8,128)(2,1)S(1)}) custom-call(bf16[256,896]{1,0:T(8,128)(2,1)S(1)} %get-tuple-element.57.edge_ref, f32[256,1536]{1,0:T(8,128)S(1)} %add_products.1.inner_total_ref, bf16[128,1536]{1,0:T(8,128)(2,1)S(1)} %copy-done, bf16[128,1536]{1,0:T(8,128)(2,1)S(1)} %collective-permute-done.rest_1_, ...), custom_call_target="tpu_custom_call" | custom-call | tf_op jit(solution)/shard_map/project/pallas_call | solution.py:566
  38.9 0.0 collective-permute-done.13.rest_1_
  38.9 0.4 collective-permute-start.16
  39.3 0.2 collective-permute-start.17
  39.5 0.3 collective-permute-start.18
  39.8 0.0 collective-permute-done.15.rest_6_
  39.8 0.0 collective-permute-done.14.rest_5_
  39.9 0.3 gather_sums.1.total_ref
  40.2 0.9 %collective-permute-done.18.rest_1_ = bf16[48,1536]{1,0:T(8,128)(2,1)S(1)} collective-permute-done((bf16[48,1536]{1,0:T(8,128)(2,1)S(1)}, bf16[48,1536]{1,0:T(8,128)(2,1)S(1)}, u32[]{:S(2)}, u32[]{:S(2)}) %collective-permute-start.18) | collective-permute-done | bytes 147488 | tf_op jit(solution)/shard_map/ppermute | solution.py:21
  41.1 0.0 collective-permute-done.17.rest_0_
  41.1 0.0 collective-permute-done.16.more_ref
  41.1 1.1 %finish.1 = bf16[256,1536]{1,0:T(8,128)(2,1)} custom-call(bf16[256,256]{1,0:T(8,128)(2,1)S(1)} %get-tuple-element.55.features_ref, f32[256,1536]{1,0:T(8,128)S(1)} %gather_sums.1.total_ref, bf16[256,512]{1,0:T(8,128)(2,1)S(1)} %collective-permute-done.16.more_ref, bf16[80,1536]{1,0:T(8,128)(2,1)S(1)} %collective-permute-done.17.rest_0_, ...), custom_call_target="tpu_custom_call" | custom-call | tf_op jit(solution)/shard_map/finish/pallas_call | solution.py:584
  (8 shorter events, 0.0 us)
Async XLA Ops:
  0.0 6.4 %collective-permute-start.1 = (bf16[2,128,6144]{2,1,0:T(8,128)(2,1)}, bf16[2,128,6144]{2,1,0:T(8,128)(2,1)S(1)}, u32[]{:S(2)}, u32[]{:S(2)}) collective-permute-start(bf16[2,128,6144]{2,1,0:T(8,128)(2,1)} %bitcast.1), channel_id=1, source_target_pairs={{0,2},{2,0},{4,6},{6,4},{8,10},{10,8},{12,14},{14,12},{16,18},{18,... | collective-permute-start | bytes 9437192 | tf_op jit(solution)/shard_map/ppermute | solution.py:21
  0.5 13.3 %collective-permute-start = (bf16[128,1536]{1,0:T(8,128)(2,1)}, bf16[128,1536]{1,0:T(8,128)(2,1)S(1)}, u32[]{:S(2)}, u32[]{:S(2)}) collective-permute-start(bf16[128,1536]{1,0:T(8,128)(2,1)} %rest_0_.7), channel_id=1, source_target_pairs={{0,16},{2,18},{4,20},{6,22},{16,24},{18,26},{20,28},{22,30},{24,8}... | collective-permute-start | bytes 1179656 | tf_op jit(solution)/shard_map/ppermute | solution.py:448
  4.0 11.5 %collective-permute-start.7 = (bf16[128,1536]{1,0:T(8,128)(2,1)}, bf16[128,1536]{1,0:T(8,128)(2,1)S(1)}, u32[]{:S(2)}, u32[]{:S(2)}) collective-permute-start(bf16[128,1536]{1,0:T(8,128)(2,1)} %rest_0_.7), channel_id=1, source_target_pairs={{0,4},{2,6},{4,0},{6,2},{8,12},{10,14},{12,8},{14,10},{16,20},{18,... | collective-permute-start | bytes 1179656 | tf_op jit(solution)/shard_map/ppermute | solution.py:21
  6.4 2.8 %copy-start = (bf16[128,1536]{1,0:T(8,128)(2,1)S(1)}, bf16[128,1536]{1,0:T(8,128)(2,1)}, u32[]{:S(2)}) copy-start(bf16[128,1536]{1,0:T(8,128)(2,1)} %rest_0_.7) | copy-start | bytes 1179652
  6.6 17.3 %collective-permute-start.2 = (bf16[128,2048]{1,0:T(8,128)(2,1)S(1)}, bf16[128,2048]{1,0:T(8,128)(2,1)S(1)}, u32[]{:S(2)}, u32[]{:S(2)}) collective-permute-start(bf16[128,2048]{1,0:T(8,128)(2,1)S(1)} %pack_first.1), channel_id=1, source_target_pairs={{0,1},{1,0},{2,3},{3,2},{4,5},{5,4},{6,7},{7,6},{8,9},{9,8},{10,11... | collective-permute-start | bytes 1572872 | tf_op jit(solution)/shard_map/ppermute | solution.py:494
  9.2 14.8 %collective-permute-start.8 = (bf16[128,1536]{1,0:T(8,128)(2,1)S(1)}, bf16[128,1536]{1,0:T(8,128)(2,1)S(1)}, u32[]{:S(2)}, u32[]{:S(2)}) collective-permute-start(bf16[128,1536]{1,0:T(8,128)(2,1)S(1)} %copy-done), channel_id=1, source_target_pairs={{0,8},{2,10},{4,12},{6,14},{16,0},{18,2},{20,4},{22,6},{24,16},{26... | collective-permute-start | bytes 1179656 | tf_op jit(solution)/shard_map/ppermute | solution.py:448
  11.4 22.2 %collective-permute-start.3 = (bf16[128,2048]{1,0:T(8,128)(2,1)S(1)}, bf16[128,2048]{1,0:T(8,128)(2,1)S(1)}, u32[]{:S(2)}, u32[]{:S(2)}) collective-permute-start(bf16[128,2048]{1,0:T(8,128)(2,1)S(1)} %get-tuple-element.38), channel_id=1, source_target_pairs={{0,1},{1,0},{2,3},{3,2},{4,5},{5,4},{6,7},{7,6},{8,9},{9,8},{10,11... | collective-permute-start | bytes 1572872 | tf_op jit(solution)/shard_map/ppermute | solution.py:494
  13.8 13.2 %collective-permute-start.9 = (bf16[128,1536]{1,0:T(8,128)(2,1)S(1)}, bf16[128,1536]{1,0:T(8,128)(2,1)S(1)}, u32[]{:S(2)}, u32[]{:S(2)}) collective-permute-start(bf16[128,1536]{1,0:T(8,128)(2,1)S(1)} %collective-permute-done.rest_1_), channel_id=1, source_target_pairs={{0,4},{2,6},{4,0},{6,2},{8,12},{10,14},{12,8},{14,10},{16,20},{18,... | collective-permute-start | bytes 1179656 | tf_op jit(solution)/shard_map/ppermute | solution.py:21
  15.5 16.5 %collective-permute-start.10 = (bf16[128,1536]{1,0:T(8,128)(2,1)S(1)}, bf16[128,1536]{1,0:T(8,128)(2,1)S(1)}, u32[]{:S(2)}, u32[]{:S(2)}) collective-permute-start(bf16[128,1536]{1,0:T(8,128)(2,1)S(1)} %collective-permute-done.rest_1_), channel_id=1, source_target_pairs={{0,16},{2,18},{4,20},{6,22},{16,24},{18,26},{20,28},{22,30},{24,8}... | collective-permute-start | bytes 1179656 | tf_op jit(solution)/shard_map/ppermute | solution.py:448
  24.0 4.1 %collective-permute-start.6 = (bf16[128,1024]{1,0:T(8,128)(2,1)S(1)}, bf16[128,1024]{1,0:T(8,128)(2,1)S(1)}, u32[]{:S(2)}, u32[]{:S(2)}) collective-permute-start(bf16[128,1024]{1,0:T(8,128)(2,1)S(1)} %get-tuple-element.47), channel_id=1, source_target_pairs={{0,2},{2,0},{4,6},{6,4},{8,10},{10,8},{12,14},{14,12},{16,18},{18,... | collective-permute-start | bytes 786440 | tf_op jit(solution)/shard_map/ppermute | solution.py:21
  24.0 11.9 %collective-permute-start.11 = (bf16[128,1536]{1,0:T(8,128)(2,1)S(1)}, bf16[128,1536]{1,0:T(8,128)(2,1)S(1)}, u32[]{:S(2)}, u32[]{:S(2)}) collective-permute-start(bf16[128,1536]{1,0:T(8,128)(2,1)S(1)} %collective-permute-done.8.rest_3_), channel_id=1, source_target_pairs={{0,4},{2,6},{4,0},{6,2},{8,12},{10,14},{12,8},{14,10},{16,20},{18,... | collective-permute-start | bytes 1179656 | tf_op jit(solution)/shard_map/ppermute | solution.py:21
  27.0 11.9 %collective-permute-start.12 = (bf16[80,1536]{1,0:T(8,128)(2,1)S(1)}, bf16[80,1536]{1,0:T(8,128)(2,1)S(1)}, u32[]{:S(2)}, u32[]{:S(2)}) collective-permute-start(bf16[80,1536]{1,0:T(8,128)(2,1)S(1)} %slice.6), channel_id=1, source_target_pairs={{0,16},{2,18},{4,20},{6,22},{16,24},{18,26},{20,28},{22,30},{24,8}... | collective-permute-start | bytes 737288 | tf_op jit(solution)/shard_map/ppermute | solution.py:448
  32.1 6.9 %collective-permute-start.13 = (bf16[48,1536]{1,0:T(8,128)(2,1)S(1)}, bf16[48,1536]{1,0:T(8,128)(2,1)S(1)}, u32[]{:S(2)}, u32[]{:S(2)}) collective-permute-start(bf16[48,1536]{1,0:T(8,128)(2,1)S(1)} %slice.7), channel_id=1, source_target_pairs={{0,4},{2,6},{4,0},{6,2},{8,12},{10,14},{12,8},{14,10},{16,20},{18,... | collective-permute-start | bytes 442376 | tf_op jit(solution)/shard_map/ppermute | solution.py:21
  35.1 1.4 %collective-permute-start.5 = (bf16[128,512]{1,0:T(8,128)(2,1)S(1)}, bf16[128,512]{1,0:T(8,128)(2,1)S(1)}, u32[]{:S(2)}, u32[]{:S(2)}) collective-permute-start(bf16[128,512]{1,0:T(8,128)(2,1)S(1)} %get-tuple-element.46), channel_id=1, source_target_pairs={{0,2},{2,0},{4,6},{6,4},{8,10},{10,8},{12,14},{14,12},{16,18},{18,... | collective-permute-start | bytes 393224 | tf_op jit(solution)/shard_map/ppermute | solution.py:21
  35.2 1.5 %collective-permute-start.4 = (bf16[128,512]{1,0:T(8,128)(2,1)S(1)}, bf16[128,512]{1,0:T(8,128)(2,1)S(1)}, u32[]{:S(2)}, u32[]{:S(2)}) collective-permute-start(bf16[128,512]{1,0:T(8,128)(2,1)S(1)} %get-tuple-element.45), channel_id=1, source_target_pairs={{0,2},{2,0},{4,6},{6,4},{8,10},{10,8},{12,14},{14,12},{16,18},{18,... | collective-permute-start | bytes 393224 | tf_op jit(solution)/shard_map/ppermute | solution.py:21
  37.4 2.5 %collective-permute-start.15 = (bf16[256,512]{1,0:T(8,128)(2,1)S(1)}, bf16[256,512]{1,0:T(8,128)(2,1)S(1)}, u32[]{:S(2)}, u32[]{:S(2)}) collective-permute-start(bf16[256,512]{1,0:T(8,128)(2,1)S(1)} %get-tuple-element.62), channel_id=1, source_target_pairs={{0,2},{2,0},{4,6},{6,4},{8,10},{10,8},{12,14},{14,12},{16,18},{18,... | collective-permute-start | bytes 786440 | tf_op jit(solution)/shard_map/ppermute | solution.py:21
  38.2 1.6 %collective-permute-start.14 = (bf16[256,512]{1,0:T(8,128)(2,1)S(1)}, bf16[256,512]{1,0:T(8,128)(2,1)S(1)}, u32[]{:S(2)}, u32[]{:S(2)}) collective-permute-start(bf16[256,512]{1,0:T(8,128)(2,1)S(1)} %get-tuple-element.61), channel_id=1, source_target_pairs={{0,2},{2,0},{4,6},{6,4},{8,10},{10,8},{12,14},{14,12},{16,18},{18,... | collective-permute-start | bytes 786440 | tf_op jit(solution)/shard_map/ppermute | solution.py:21
  38.9 2.2 %collective-permute-start.16 = (bf16[256,512]{1,0:T(8,128)(2,1)S(1)}, bf16[256,512]{1,0:T(8,128)(2,1)S(1)}, u32[]{:S(2)}, u32[]{:S(2)}) collective-permute-start(bf16[256,512]{1,0:T(8,128)(2,1)S(1)} %get-tuple-element.64), channel_id=1, source_target_pairs={{0,2},{2,0},{4,6},{6,4},{8,10},{10,8},{12,14},{14,12},{16,18},{18,... | collective-permute-start | bytes 786440 | tf_op jit(solution)/shard_map/ppermute | solution.py:21
  39.3 1.8 %collective-permute-start.17 = (bf16[80,1536]{1,0:T(8,128)(2,1)S(1)}, bf16[80,1536]{1,0:T(8,128)(2,1)S(1)}, u32[]{:S(2)}, u32[]{:S(2)}) collective-permute-start(bf16[80,1536]{1,0:T(8,128)(2,1)S(1)} %collective-permute-done.12.rest_0_), channel_id=1, source_target_pairs={{0,2},{2,0},{4,6},{6,4},{8,10},{10,8},{12,14},{14,12},{16,18},{18,... | collective-permute-start | bytes 737288 | tf_op jit(solution)/shard_map/ppermute | solution.py:21
  39.5 1.6 %collective-permute-start.18 = (bf16[48,1536]{1,0:T(8,128)(2,1)S(1)}, bf16[48,1536]{1,0:T(8,128)(2,1)S(1)}, u32[]{:S(2)}, u32[]{:S(2)}) collective-permute-start(bf16[48,1536]{1,0:T(8,128)(2,1)S(1)} %collective-permute-done.13.rest_1_), channel_id=1, source_target_pairs={{0,2},{2,0},{4,6},{6,4},{8,10},{10,8},{12,14},{14,12},{16,18},{18,... | collective-permute-start | bytes 442376 | tf_op jit(solution)/shard_map/ppermute | solution.py:21
